TPU v7x, 128 devices: a whole 4x4x4 slice. The times are simulated.
128 devices in a mesh: slab: 16 (over y, x_lo, core), brick: 8 (over x_hi, z).
Axes of the slice: x: 4 (x_hi: 2, x_lo: 2; x = x_hi * 2 + x_lo), y: 4, z: 4, core: 2. Of those that a mesh axis runs over, the one named last changes fastest.
Arguments:
- fluid_velocity: float32 [3, 128, 256, 512], P(None, ('slab', 'brick')), may hold values from -6 to 6
- porosity: float32 [128, 256, 512], P(('slab', 'brick')), may hold values from 0.4 to 0.95
- particle_velocity: float32 [3, 2097152], P(None, ('slab', 'brick')), may hold values from -6 to 6
- drag_coef: float32 [2097152], P(('slab', 'brick')), may hold values from 0.2 to 2
- send_rows: int32 [4194304], P(('slab', 'brick')), may hold values from 0 to 16383, as said below
- counts: int32 [16384], P(('slab', 'brick')), may hold values from 0 to 256, as said below
- recv_cell: int32 [4194304], P(('slab', 'brick')), may hold values from 0 to 131071
Outputs:
- new_velocity: float32 [3, 128, 256, 512], P(None, ('slab', 'brick'))
- slot_force: float32 [3, 4194304], P(None, ('slab', 'brick'))
Inputs may be any that keep to these rules, and one draw needn't show every extreme that they name: One entry equals 256 in every draw; loads differ strongly between destinations; each source's counts sum to at most 16384. `send_rows`: over all destinations of one source, the live slots name distinct particles: each particle is sent to at most one brick owner.
All inputs are finite; a program needn't handle non-finite values.
Results may differ from a plain program's by a relative error of at most 0.00002.
Values sent between devices are 32-bit elements; how exact they have to be, the bound alone decides.
A program may use at most 192 MiB of HBM per device.

v0:
```python
import jax
import jax.numpy as jnp
from jax import lax
from jax.sharding import PartitionSpec as P

time_step = 0.05


def with_halo(block, sides, width):
    for axis, dim in sides:
        count = lax.axis_size(axis)
        forward = [(i, i + 1) for i in range(count - 1)]
        backward = [(target, source) for source, target in forward]
        low = lax.ppermute(
            lax.slice_in_dim(block, block.shape[dim] - width, None, axis=dim), axis, forward
        )
        high = lax.ppermute(lax.slice_in_dim(block, 0, width, axis=dim), axis, backward)
        block = jnp.concatenate([low, block, high], axis=dim)
    return block


def neighbours(padded):
    return [
        padded[:, 2:, 1:-1, 1:-1],
        padded[:, :-2, 1:-1, 1:-1],
        padded[:, 1:-1, 2:, 1:-1],
        padded[:, 1:-1, :-2, 1:-1],
        padded[:, 1:-1, 1:-1, 2:],
        padded[:, 1:-1, 1:-1, :-2],
    ]


def viscous_sum(padded):
    centre = padded[:, 1:-1, 1:-1, 1:-1]
    total = jnp.zeros_like(centre[:3])
    for beside in neighbours(padded):
        weight = 0.5 * (centre[3] + beside[3])
        total = total + weight * (beside[:3] - centre[:3])
    return total


def per_device(
    fluid_velocity, porosity, particle_velocity, drag_coef, send_rows, counts, recv_cell
):
    n_slab = lax.axis_size("slab")
    n_brick = lax.axis_size("brick")
    devices = n_slab * n_brick
    slot_cap = send_rows.shape[0] // devices
    stacked = jnp.concatenate([fluid_velocity, porosity[None]], 0)
    bricks = lax.all_to_all(stacked, "brick", split_axis=2, concat_axis=1, tiled=True)
    part_table = jnp.concatenate([particle_velocity, drag_coef[None]], 0)
    packed = jnp.take(part_table, send_rows, axis=1)
    slot_index = jnp.arange(slot_cap, dtype=jnp.int32)
    slot_live = (slot_index[None, :] < counts[:, None]).reshape(-1)
    packed = jnp.where(slot_live[None, :], packed, 0.0)
    arrived = lax.all_to_all(packed, ("slab", "brick"), split_axis=1, concat_axis=1, tiled=True)
    brick_flat = bricks.reshape(4, -1)
    gathered = jnp.take(brick_flat, recv_cell, axis=1)
    fluid_frac = gathered[3]
    beta = arrived[3] * (1.0 - fluid_frac) / (fluid_frac * fluid_frac)
    force = beta * (gathered[:3] - arrived[:3])
    deposit = jnp.zeros((3, brick_flat.shape[1]), jnp.float32).at[:, recv_cell].add(force)
    deposit = deposit.reshape(3, bricks.shape[1], bricks.shape[2], bricks.shape[3])
    returned = lax.all_to_all(deposit, "brick", split_axis=1, concat_axis=2, tiled=True)
    padded = with_halo(stacked, ((("slab", "brick"), 1),), 1)
    padded = jnp.pad(padded, ((0, 0), (0, 0), (1, 1), (1, 1)))
    viscous = viscous_sum(padded)
    new_velocity = fluid_velocity + time_step * (viscous - returned) / porosity
    return (new_velocity, force)


def solution(mesh):
    placed = (
        P(None, ("slab", "brick"), None, None),
        P(("slab", "brick"), None, None),
        P(None, ("slab", "brick")),
        P(("slab", "brick")),
        P(("slab", "brick")),
        P(("slab", "brick")),
        P(("slab", "brick")),
    )
    return jax.shard_map(
        per_device,
        mesh=mesh,
        in_specs=placed,
        out_specs=(P(None, ("slab", "brick"), None, None), P(None, ("slab", "brick"))),
        check_vma=False,
    )
```

profile of v0, /device:TPU:8, one launch (start us, length us, event | category | flops | bytes accessed | tf_op | source)
XLA Modules:
  0.0 1211.9 jit_solution(9888074661517773885)
XLA Ops:
  0.6 0.9 fusion.37
  1.6 0.9 compare_and_fusion.1
  2.5 1.1 pad_maximum_fusion.1
  3.6 5.1 copy.54
  8.7 112.4 %gather_fusion = f32[32768,4]{1,0:T(8,128)} fusion(f32[4,16384]{0,1:T(8,128)} %copy.54, s32[32768]{0:T(1024)S(1)} %fusion.37), kind=kCustom, calls=%fused_computation | custom fusion | bytes 1179648 | tf_op jit(solution)/shard_map/jit(_take)/gather | solution.py:52
  121.1 9.5 copy.55
  130.7 1.1 select_select_fusion
  131.8 10.4 all-to-all-start
  142.3 1.5 pad_maximum_fusion
  143.8 7.1 collective-permute-start
  150.9 1.9 collective-permute-start.1
  152.8 4.3 copy.56
  157.2 7.6 all-to-all-start.1
  164.8 11.1 sort
  176.1 50.0 %all-to-all-done.1 = f32[4,1,256,512]{3,0,1,2:T(4,128)} async-done(((f32[4,1,256,512]{3,0,1,2:T(4,128)}), f32[4,1,256,512]{3,0,1,2:T(4,128)}, u32[]{:S(2)}, u32[]{:S(2)}) %all-to-all-start.1) | async-done | bytes 2097184 | tf_op jit(solution)/shard_map/all_to_all | solution.py:50
  226.1 30.7 %copy.57 = f32[4,1,256,512]{0,3,2,1:T(8,128)} copy(f32[4,1,256,512]{3,0,1,2:T(4,128)} %all-to-all-done.1) | data formatting | bytes 4194304 | tf_op jit(solution)/shard_map/all_to_all | solution.py:50
  256.9 474.7 %gather_fusion.1 = f32[32768,4]{1,0:T(8,128)} fusion(f32[4,131072]{0,1:T(8,128)} %bitcast.11, s32[32768]{0:T(1024)S(1)} %get-tuple-element.24), kind=kCustom, calls=%fused_computation.1 | custom fusion | bytes 1179648 | tf_op jit(solution)/shard_map/jit(_take)/gather | solution.py:58
  731.6 9.7 copy.58
  741.3 0.2 select_bitcast_fusion
  741.4 0.2 multiply_divide_fusion
  741.7 0.2 fusion.24
  741.9 8.5 copy.59
  750.5 384.6 %scatter_custom_fusion = f32[3,131072]{0,1:T(8,128)} fusion(s32[32768]{0:T(1024)} %get-tuple-element.12, f32[]{:T(128)} %constant.20.clone.1, f32[32768,3]{1,0:T(8,128)} %copy.59, s32[32768]{0:T(1024)S(1)} %broadcast_clamp_fusion), kind=kCustom, calls=%fused_computation.4 | custom fusion | flops 98304 | bytes 1573376 | tf_op jit(solution)/shard_map/scatter-add | solution.py:62
  1135.1 39.2 %copy.60 = f32[3,8,32,512]{3,2,0,1:T(8,128)} copy(f32[3,8,32,512]{0,3,2,1:T(8,128)} %bitcast.16) | data formatting | bytes 3145728 | tf_op jit(solution)/shard_map/reshape | solution.py:63
  1174.3 8.9 all-to-all-start.2
  1183.3 6.6 select_maximum_fusion
  1189.9 3.1 copy-done
  1193.0 3.1 fusion.36
  1196.2 7.0 all-to-all-done.2
  1203.2 1.7 copy.61
  1205.0 0.2 copy-done.7
  1205.2 6.3 fusion.14
  (28 shorter events, 0.5 us)
Async XLA Ops:
  121.1 9.6 copy-start.9
  130.5 11.7 copy-start.1
  130.6 11.7 copy-start.2
  131.8 25.4 %all-to-all-start = ((f32[4,128,256]{2,0,1:T(4,128)}), f32[4,128,256]{2,0,1:T(4,128)S(1)}, u32[]{:S(2)}, u32[]{:S(2)}) async-start(f32[4,128,256]{2,0,1:T(4,128)} %select_select_fusion), calls=%async_computation | async-start | bytes 1048576 | tf_op jit(solution)/shard_map/all_to_all | solution.py:56
  143.8 1039.5 %collective-permute-start = (f32[4,1,256,512]{3,2,1,0:T(8,128)}, f32[4,1,256,512]{3,2,1,0:T(8,128)}, u32[]{:S(2)}, u32[]{:S(2)}) collective-permute-start(f32[4,1,256,512]{3,2,1,0:T(8,128)} %pad_maximum_fusion), channel_id=1, source_target_pairs={{1,0},{2,1},{3,2},{4,3},{5,4},{6,5},{7,6},{8,7},{9,8},{10,9},{11,1... | collective-permute-start | bytes 6291464 | tf_op jit(solution)/shard_map/ppermute | solution.py:17
  150.9 1032.3 %collective-permute-start.1 = (f32[4,1,256,512]{3,2,1,0:T(8,128)}, f32[4,1,256,512]{3,2,1,0:T(8,128)}, u32[]{:S(2)}, u32[]{:S(2)}) collective-permute-start(f32[4,1,256,512]{3,2,1,0:T(8,128)} %pad_maximum_fusion), channel_id=1, source_target_pairs={{0,1},{1,2},{2,3},{3,4},{4,5},{5,6},{6,7},{7,8},{8,9},{9,10},{10,1... | collective-permute-start | bytes 6291464 | tf_op jit(solution)/shard_map/ppermute | solution.py:14
  157.1 7.6 copy-start.8
  157.2 69.0 %all-to-all-start.1 = ((f32[4,1,256,512]{3,0,1,2:T(4,128)}), f32[4,1,256,512]{3,0,1,2:T(4,128)}, u32[]{:S(2)}, u32[]{:S(2)}) async-start(f32[4,1,256,512]{3,0,1,2:T(4,128)} %copy.56), calls=%async_computation.1 | async-start | bytes 4194304 | tf_op jit(solution)/shard_map/all_to_all | solution.py:50
  741.9 8.6 copy-start.3
  1174.3 28.9 %all-to-all-start.2 = ((f32[3,8,32,512]{3,2,0,1:T(8,128)}), f32[3,8,32,512]{3,2,0,1:T(8,128)}, u32[]{:S(2)}, u32[]{:S(2)}) async-start(f32[3,8,32,512]{3,2,0,1:T(8,128)} %copy.60), calls=%async_computation.2 | async-start | bytes 3145728 | tf_op jit(solution)/shard_map/all_to_all | solution.py:64
  1189.9 3.1 copy-start
  1203.2 1.7 copy-start.4
  1203.2 1.7 copy-start.5
  1203.2 1.8 copy-start.6
  1203.2 2.0 copy-start.7
where the time goes:
time: 1230 us; the launch traced here: 1210 us
  local copies, waits for them, and re-layouts  699 us (57%)
  other arithmetic  418 us (34%)
  waiting for transfers between devices  57.1 us (5%)
  starting transfers between devices  36 us (3%)
    gather x2, local copies, waits for them, and re-layouts, per_device(): gathered = jnp.take(brick_flat, recv_cell, axis=1)  484 us
    scatter-add x3, other arithmetic, per_device(): jnp.zeros((3, brick_flat.shape[1]), jnp.float32).at[:, recv_cell].add(force)  396 us
    gather x2, local copies, waits for them, and re-layouts, per_device(): packed = jnp.take(part_table, send_rows, axis=1)  122 us
    all_to_all x1, waiting for transfers between devices, per_device(): lax.all_to_all(stacked, 'brick', split_axis=2, concat_axis=1, tiled=True)  50 us
    reshape x1, local copies, waits for them, and re-layouts, per_device(): deposit.reshape(3, bricks.shape[1], bricks.shape[2], bricks.shape[3])  39.2 us
    all_to_all x1, local copies, waits for them, and re-layouts, per_device(): lax.all_to_all(stacked, 'brick', split_axis=2, concat_axis=1, tiled=True)  30.7 us
  transfers between devices with their start and end apart: 5, of which 2 were waited for; matrix products, arithmetic and copies ran while one was open for 80% of the time, Pallas kernels for 0%

commit v1 on v0

v1 whole, which is shorter than its diff:
```python
import functools

import jax
import jax.numpy as jnp
from jax import lax
from jax.experimental import pallas as pl
from jax.experimental.pallas import tpu as pltpu
from jax.sharding import PartitionSpec as P

time_step = 0.05
F32, BF16, I32 = jnp.float32, jnp.bfloat16, jnp.int32
LAST = 2**31 - 1


def split3(x):
    high = x.astype(BF16)
    rest = x - high.astype(F32)
    mid = rest.astype(BF16)
    low = (rest - mid.astype(F32)).astype(BF16)
    return high, mid, low


def pick_kernel(counts_ref, pv_ref, coef_ref, rows_ref, out_ref, table, *, cap):
    me = lax.axis_index("slab") * lax.axis_size("brick") + lax.axis_index("brick")
    for c in range(4):
        whole = coef_ref[...] if c == 3 else pv_ref[c]
        halves = jnp.concatenate([whole[:64], whole[64:]], axis=1)
        for p, piece in enumerate(split3(halves)):
            table[p * 256 + c * 64 : p * 256 + (c + 1) * 64, :] = piece
    r_iota = lax.broadcasted_iota(I32, (256, cap), 0)
    l_iota = lax.broadcasted_iota(I32, (64, cap), 0)
    k_iota = lax.broadcasted_iota(I32, (1, cap), 1)

    def one(t, carry):
        row = jnp.concatenate([rows_ref[pl.ds(2 * t, 1), :], rows_ref[pl.ds(2 * t + 1, 1), :]], axis=1)
        r = (row & 127) + ((row >> 13) << 7)
        l = (row >> 7) & 63
        onehot = jnp.where(r_iota == r, 1.0, 0.0).astype(BF16)
        got = jnp.dot(table[...], onehot, preferred_element_type=F32)
        got = got[:256] + (got[256:512] + got[512:])
        mask = l_iota == l
        live = k_iota < counts_ref[t]
        slot = (me * cap + k_iota).astype(F32)
        for c in range(4):
            value = jnp.sum(jnp.where(mask, got[c * 64 : (c + 1) * 64], 0.0), axis=0, keepdims=True)
            if c == 0:
                value = jnp.where(live, value, slot)
            if c == 3:
                value = jnp.where(live, value, 0.0)
            out_ref[t, 2 * c : 2 * c + 1, :] = value[:, :128]
            out_ref[t, 2 * c + 1 : 2 * c + 2, :] = value[:, 128:]
        return carry

    lax.fori_loop(0, out_ref.shape[0], one, 0, unroll=2)


def key_kernel(arrived_ref, cell_ref, key_ref, data_ref, starts_ref):
    tiles = cell_ref.shape[0] // 8
    place = lax.broadcasted_iota(I32, (8, 128), 0) * 128 + lax.broadcasted_iota(I32, (8, 128), 1)

    def one(j, sums):
        parts = [arrived_ref[4 * j + i] for i in range(4)]
        rows = pl.ds(pl.multiple_of(8 * j, 8), 8)
        for c in range(4):
            value = jnp.concatenate([part[2 * c : 2 * c + 2] for part in parts], axis=0)
            data_ref[c, rows, :] = value
        live = value != 0.0
        cell = cell_ref[rows, :]
        block = cell >> 12
        slot = j * 1024 + place
        key = ((block - 16) << 27) + (slot << 12) + (cell & 4095)
        key_ref[rows, :] = jnp.where(live, key, LAST)
        block = jnp.where(live, block, 32)
        return tuple(s + jnp.where(block < b + 1, 1, 0) for b, s in enumerate(sums))

    sums = lax.fori_loop(0, tiles, one, tuple(jnp.zeros((8, 128), I32) for _ in range(32)))
    tail = (cell_ref[tiles * 8 - 8 :, :] == 131071) & (data_ref[3, tiles * 8 - 8 :, :] != 0.0) & (place == 1023)
    starts_ref[0] = 0
    for b in range(32):
        starts_ref[b + 1] = jnp.sum(sums[b])
    starts_ref[32] = jnp.where(jnp.sum(jnp.where(tail, 1, 0)) > 0, tiles * 1024, starts_ref[32])


def brick_kernel(
    starts_ref, key_ref, coef_ref, p0_ref, p1_ref, p2_ref, fluid_ref, zlo_ref, zhi_ref, xlo_ref, xhi_ref,
    force_ref, slot_ref, net_ref, padded, table, deposit, *, width,
):
    rows = key_ref.shape[0]
    n = width // 128
    force_ref[...] = jnp.zeros_like(force_ref)
    slot_ref[...] = jnp.where(coef_ref[...] != 0.0, (key_ref[...] >> 12) & 32767, p0_ref[...].astype(I32))
    for z in range(8):
        padded[z + 1, :, 8:40, :] = fluid_ref[z]
        for c in range(4):
            padded[z + 1, c, 7:8, :] = xlo_ref[z, c : c + 1, :]
            padded[z + 1, c, 40:41, :] = xhi_ref[z, c : c + 1, :]
    padded[0, :, 8:40, :] = zlo_ref[...]
    padded[9, :, 8:40, :] = zhi_ref[...]

    r_iota = lax.broadcasted_iota(I32, (256, width), 0)
    l_iota = lax.broadcasted_iota(I32, (16, width), 0)
    p_iota = lax.broadcasted_iota(I32, (1, width), 1)
    y_iota = lax.broadcasted_iota(I32, (8, 512), 1)

    def block(b, carry):
        z, q = b // 4, b % 4
        x8 = pl.multiple_of(q * 8, 8)
        for c in range(4):
            centre = fluid_ref[z, c, pl.ds(x8, 8), :]
            for h in range(2):
                for p, piece in enumerate(split3(centre[:, h * 256 : (h + 1) * 256])):
                    at = p * 64 + c * 16 + h * 8
                    table[at : at + 8, :] = piece.astype(F32)
        pieces = table[...].astype(BF16)
        deposit[...] = jnp.zeros_like(deposit)
        first, end = starts_ref[b], starts_ref[b + 1]
        row0 = first // 128

        def window(w, inner):
            row = row0 + w * n
            at = jnp.minimum(row, rows - n)

            def line(ref):
                return jnp.concatenate([ref[pl.ds(at + i, 1), :] for i in range(n)], axis=1)

            key = line(key_ref)
            valid = ((key >> 27) + 16 == b) & (p_iota >= (row - at) * 128)
            r = jnp.where(valid, key & 255, -1)
            l = ((key >> 9) & 7) + ((key >> 8) & 1) * 8
            onehot = jnp.where(r_iota == r, 1.0, 0.0).astype(BF16)
            got = jnp.dot(pieces, onehot, preferred_element_type=F32)
            got = got[:64] + (got[64:128] + got[128:])
            mask = l_iota == l
            u = [
                jnp.sum(jnp.where(mask, got[c * 16 : (c + 1) * 16], 0.0), axis=0, keepdims=True) for c in range(4)
            ]
            frac = jnp.where(valid, u[3], 1.0)
            beta = line(coef_ref) * (1.0 - frac) / (frac * frac)
            split = []
            for c, ref in enumerate((p0_ref, p1_ref, p2_ref)):
                force = jnp.where(valid, beta * (u[c] - line(ref)), 0.0)
                for i in range(n):
                    force_ref[c, pl.ds(at + i, 1), :] += force[:, i * 128 : (i + 1) * 128]
                split.append(split3(force))
            spread = jnp.concatenate(
                [jnp.where(mask, split[c][p].astype(F32), 0.0) for p in range(3) for c in range(3)], axis=0
            ).astype(BF16)
            deposit[...] += lax.dot_general(
                spread, onehot, (((1,), (1,)), ((), ())), preferred_element_type=F32
            )
            return inner

        windows = jnp.where(end > first, (end - row0 * 128 + width - 1) // width, 0)
        lax.fori_loop(0, windows, window, 0)

        tall = [padded[z + 1, c, pl.ds(x8, 24), :] for c in range(4)]
        below = [padded[z, c, pl.ds(x8 + 8, 8), :] for c in range(4)]
        above = [padded[z + 2, c, pl.ds(x8 + 8, 8), :] for c in range(4)]
        centre = [t[8:16] for t in tall]
        sides = [above, below, [t[9:17] for t in tall], [t[7:15] for t in tall]]
        sides.append([jnp.where(y_iota == 511, 0.0, pltpu.roll(t, 511, 1)) for t in centre])
        sides.append([jnp.where(y_iota == 0, 0.0, pltpu.roll(t, 1, 1)) for t in centre])
        total = [jnp.zeros((8, 512), F32) for _ in range(3)]
        for side in sides:
            weight = 0.5 * (centre[3] + side[3])
            for c in range(3):
                total[c] = total[c] + weight * (side[c] - centre[c])
        summed = deposit[0:48, :] + (deposit[48:96, :] + deposit[96:144, :])
        for c in range(3):
            left, right = summed[c * 16 : c * 16 + 8], summed[c * 16 + 8 : c * 16 + 16]
            net_ref[z, c, pl.ds(x8, 8), :] = total[c] - jnp.concatenate([left, right], axis=1)
        return carry

    lax.fori_loop(0, 32, block, 0)


def shift(block, axis, step):
    count = lax.axis_size(axis)
    pairs = [(i, i + step) for i in range(count) if 0 <= i + step < count]
    return lax.ppermute(block, axis, pairs)


def per_device(
    fluid_velocity, porosity, particle_velocity, drag_coef, send_rows, counts, recv_cell
):
    n_slab = lax.axis_size("slab")
    n_brick = lax.axis_size("brick")
    devices = n_slab * n_brick
    cap = send_rows.shape[0] // devices
    vmem = pl.BlockSpec(memory_space=pltpu.VMEM)
    smem = pl.BlockSpec(memory_space=pltpu.SMEM)
    params = pltpu.CompilerParams(vmem_limit_bytes=40 << 20)

    stacked = jnp.concatenate([fluid_velocity[:, 0], porosity], 0).reshape(4, 8, 32, 512)
    bricks = lax.all_to_all(jnp.swapaxes(stacked, 0, 1), "brick", split_axis=0, concat_axis=0, tiled=True)

    packed = pl.pallas_call(
        functools.partial(pick_kernel, cap=cap),
        out_shape=jax.ShapeDtypeStruct((devices, 8, 128), F32),
        in_specs=[smem, vmem, vmem, vmem],
        out_specs=vmem,
        scratch_shapes=[pltpu.VMEM((768, 256), BF16)],
        compiler_params=params,
        name="pick_particles",
    )(counts, particle_velocity.reshape(3, 128, 128), drag_coef.reshape(128, 128), send_rows.reshape(256, 128))
    arrived = lax.all_to_all(packed, ("slab", "brick"), split_axis=0, concat_axis=0, tiled=True)

    zlo = shift(bricks[7], "slab", 1)
    zhi = shift(bricks[0], "slab", -1)
    xlo = shift(bricks[:, :, 31, :], "brick", 1)
    xhi = shift(bricks[:, :, 0, :], "brick", -1)

    key, data, starts = pl.pallas_call(
        key_kernel,
        out_shape=(
            jax.ShapeDtypeStruct((256, 128), I32),
            jax.ShapeDtypeStruct((4, 256, 128), F32),
            jax.ShapeDtypeStruct((33,), I32),
        ),
        in_specs=[vmem, vmem],
        out_specs=(vmem, vmem, smem),
        compiler_params=params,
        name="block_keys",
    )(arrived, recv_cell.reshape(256, 128))
    flat = data.reshape(4, -1)
    ordered = lax.sort(
        (key.reshape(-1), flat[3], flat[0], flat[1], flat[2]), num_keys=1, is_stable=False
    )
    force, slot, net = pl.pallas_call(
        functools.partial(brick_kernel, width=256),
        out_shape=(
            jax.ShapeDtypeStruct((3, 256, 128), F32),
            jax.ShapeDtypeStruct((256, 128), I32),
            jax.ShapeDtypeStruct((8, 3, 32, 512), F32),
        ),
        in_specs=[smem] + [vmem] * 10,
        out_specs=(vmem, vmem, vmem),
        scratch_shapes=[
            pltpu.VMEM((10, 4, 48, 512), F32),
            pltpu.VMEM((192, 256), F32),
            pltpu.VMEM((144, 256), F32),
        ],
        compiler_params=params,
        name="brick_forces",
    )(starts, *[part.reshape(256, 128) for part in ordered], bricks, zlo, zhi, xlo, xhi)

    returned = lax.all_to_all(net, "brick", split_axis=0, concat_axis=0, tiled=True)
    flat = force.reshape(3, -1)
    back = lax.sort((slot.reshape(-1), flat[0], flat[1], flat[2]), num_keys=1, is_stable=False)
    slot_force = jnp.stack(back[1:])
    returned = jnp.swapaxes(returned, 0, 1).reshape(fluid_velocity.shape)
    new_velocity = fluid_velocity + time_step * returned / porosity
    return (new_velocity, slot_force)


def solution(mesh):
    placed = (
        P(None, ("slab", "brick"), None, None),
        P(("slab", "brick"), None, None),
        P(None, ("slab", "brick")),
        P(("slab", "brick")),
        P(("slab", "brick")),
        P(("slab", "brick")),
        P(("slab", "brick")),
    )
    return jax.shard_map(
        per_device,
        mesh=mesh,
        in_specs=placed,
        out_specs=(P(None, ("slab", "brick"), None, None), P(None, ("slab", "brick"))),
        check_vma=False,
    )
```

time: 1230 us -> 214 us (0.17)
  the two profiles are of different devices: /device:TPU:8 before, /device:TPU:1 now
where the time goes in v1:
time: 214 us
  starting transfers between devices  58.1 us (27%)
  Pallas kernels  56.5 us (26%)
  other arithmetic  44.9 us (21%)
  waiting for transfers between devices  36.8 us (17%)
  local copies, waits for them, and re-layouts  16.5 us (8%)
    all_to_all x1, starting transfers between devices, per_device(): lax.all_to_all(net, 'brick', split_axis=0, concat_axis=0, tiled=True)  30.4 us
    pallas_call x1, Pallas kernels, per_device(): pl.pallas_call(functools.partial(brick_kernel, width=256), out_shape=(jax...  29.2 us
    pallas_call x1, Pallas kernels, per_device(): pl.pallas_call(functools.partial(pick_kernel, cap=cap), out_shape=jax.Sha...  25.6 us
    all_to_all x1, waiting for transfers between devices, per_device(): lax.all_to_all(jnp.swapaxes(stacked, 0, 1), 'brick', split_axis=0, concat...  24.4 us
    sort x1, other arithmetic, per_device(): lax.sort((key.reshape(-1), flat[3], flat[0], flat[1], flat[2]), num_keys=...  24.1 us
    sort x1, other arithmetic, per_device(): lax.sort((slot.reshape(-1), flat[0], flat[1], flat[2]), num_keys=1, is_st...  16.6 us
    ppermute x4, starting transfers between devices, shift(): return lax.ppermute(block, axis, pairs)  11.8 us
    all_to_all x1, starting transfers between devices, per_device(): lax.all_to_all(packed, ('slab', 'brick'), split_axis=0, concat_axis=0, ti...  11.5 us
  transfers between devices with their start and end apart: 7, of which 3 were waited for; matrix products, arithmetic and copies ran while one was open for 23% of the time, Pallas kernels for 1%

profile of v1, /device:TPU:1, one launch (start us, length us, event | category | flops | bytes accessed | tf_op | source)
XLA Modules:
  0.0 213.6 jit_solution(8358365643923866151)
XLA Ops:
  0.6 1.0 copy.33
  1.6 0.9 copy-done.1
  2.5 0.8 copy-done.7
  3.3 0.7 copy-done.8
  4.0 25.6 %pick_particles.1 = f32[128,8,128]{2,1,0:T(8,128)} custom-call(s32[128]{0:T(128)S(1)} %copy-done.8, f32[3,128,128]{2,1,0:T(8,128)S(1)} %bitcast.57, f32[128,128]{1,0:T(8,128)S(1)} %bitcast.67, s32[256,128]{1,0:T(8,128)S(1)} %bitcast.58), custom_call_target="tpu_custom_call" | custom-call | tf_op jit(solution)/shard_map/pick_particles/pallas_call | solution.py:197
  29.6 11.5 %all-to-all-start = ((f32[128,8,128]{2,1,0:T(8,128)}), f32[128,8,128]{2,1,0:T(8,128)S(1)}, u32[]{:S(2)}, u32[]{:S(2)}) async-start(f32[128,8,128]{2,1,0:T(8,128)} %pick_particles.1), calls=%async_computation | async-start | bytes 1048576 | tf_op jit(solution)/shard_map/all_to_all | solution.py:206
  41.2 1.2 maximum_bitcast_fusion
  42.4 2.7 %copy.20 = f32[8,4,32,512]{3,1,2,0:T(4,128)} copy(f32[8,4,32,512]{3,2,0,1:T(8,128)S(1)} %maximum_bitcast_fusion) | data formatting | bytes 4194304 | tf_op jit(solution)/shard_map/transpose | solution.py:195
  45.1 9.7 %all-to-all-done.arrived_ref = f32[128,8,128]{2,1,0:T(8,128)S(1)} async-done(((f32[128,8,128]{2,1,0:T(8,128)}), f32[128,8,128]{2,1,0:T(8,128)S(1)}, u32[]{:S(2)}, u32[]{:S(2)}) %all-to-all-start) | async-done | bytes 524320 | tf_op jit(solution)/shard_map/all_to_all | solution.py:206
  54.8 4.4 %all-to-all-start.1 = ((f32[8,4,32,512]{3,1,2,0:T(4,128)}), f32[8,4,32,512]{3,1,2,0:T(4,128)}, u32[]{:S(2)}, u32[]{:S(2)}) async-start(f32[8,4,32,512]{3,1,2,0:T(4,128)} %copy.20), calls=%async_computation.1 | async-start | bytes 4194304 | tf_op jit(solution)/shard_map/all_to_all | solution.py:195
  59.2 1.7 block_keys.1
  60.9 24.4 %all-to-all-done.1 = f32[8,4,32,512]{3,1,2,0:T(4,128)} async-done(((f32[8,4,32,512]{3,1,2,0:T(4,128)}), f32[8,4,32,512]{3,1,2,0:T(4,128)}, u32[]{:S(2)}, u32[]{:S(2)}) %all-to-all-start.1) | async-done | bytes 2097184 | tf_op jit(solution)/shard_map/all_to_all | solution.py:195
  85.4 1.5 slice_bitcast_fusion.9
  86.9 1.3 collective-permute-start.3
  88.2 4.6 %collective-permute-start.2 = (f32[8,4,512]{2,1,0:T(4,128)}, f32[8,4,512]{2,1,0:T(4,128)}, u32[]{:S(2)}, u32[]{:S(2)}) collective-permute-start(f32[8,4,512]{2,1,0:T(4,128)} %get-tuple-element.35), channel_id=1, source_target_pairs={{0,1},{1,2},{2,3},{3,4},{4,5},{5,6},{6,7},{8,9},{9,10},{10,11},{11... | collective-permute-start | bytes 196616 | tf_op jit(solution)/shard_map/ppermute | solution.py:180
  92.8 2.2 %copy.25.fluid_ref = f32[8,4,32,512]{3,2,1,0:T(8,128)S(1)} copy(f32[8,4,32,512]{3,1,2,0:T(4,128)} %all-to-all-done.1) | data formatting | bytes 4194304 | tf_op jit(solution)/shard_map/all_to_all | solution.py:195
  95.0 0.8 slice_bitcast_fusion
  95.9 3.6 %collective-permute-start.1 = (f32[4,32,512]{2,1,0:T(8,128)}, f32[4,32,512]{2,1,0:T(8,128)S(1)}, u32[]{:S(2)}, u32[]{:S(2)}) collective-permute-start(f32[4,32,512]{2,1,0:T(8,128)} %get-tuple-element.36), channel_id=1, source_target_pairs={{8,0},{16,8},{24,16},{32,24},{40,32},{48,40},{56,48},{64,56},{72,6... | collective-permute-start | bytes 786440 | tf_op jit(solution)/shard_map/ppermute | solution.py:180
  99.5 2.3 %collective-permute-start = (f32[4,32,512]{2,1,0:T(8,128)}, f32[4,32,512]{2,1,0:T(8,128)S(1)}, u32[]{:S(2)}, u32[]{:S(2)}) collective-permute-start(f32[4,32,512]{2,1,0:T(8,128)} %get-tuple-element.37), channel_id=1, source_target_pairs={{0,8},{8,16},{16,24},{24,32},{32,40},{40,48},{48,56},{56,64},{64,7... | collective-permute-start | bytes 786440 | tf_op jit(solution)/shard_map/ppermute | solution.py:180
  101.8 0.7 slice_bitcast_fusion.5
  102.6 24.1 %sort.60 = (s32[32768]{0:T(1024)S(1)}, f32[32768]{0:T(1024)S(1)}, f32[32768]{0:T(1024)S(1)}, f32[32768]{0:T(1024)}, f32[32768]{0:T(1024)}) sort(s32[32768]{0:T(1024)S(1)} %bitcast.60, f32[32768]{0:T(1024)} %get-tuple-element.41, f32[32768]{0:T(1024)} %get-tuple-element.40, f32[32768]{0:T(1024)S(1)} %get-tuple-element.39, f32[32768]{0:T(1024)S(1)} %get-tuple-element.38), dimensions={0}, to_apply=%region_0.0 | sort | flops 491520 | bytes 1310720 | tf_op jit(solution)/shard_map/sort | solution.py:226
  126.7 0.9 copy-done.3
  127.6 0.9 copy-done.4
  128.5 29.2 %brick_forces.1 = (f32[3,256,128]{2,1,0:T(8,128)S(1)}, s32[256,128]{1,0:T(8,128)S(1)}, f32[8,3,32,512]{3,2,1,0:T(8,128)S(1)}) custom-call(s32[33]{0:T(128)S(1)} %get-tuple-element.16.starts_ref, s32[256,128]{1,0:T(8,128)S(1)} %bitcast.61, f32[256,128]{1,0:T(8,128)S(1)} %bitcast.62, f32[256,128]{1,0:T(8,128)S(1)} %bitcast.63, f32[256,128]{1,0:T(8,128)S(1)} %bitcast.64, ...), custom_call_target="tpu_custom_call" | custom-call | tf_op jit(solution)/shard_map/brick_forces/pallas_call | solution.py:229
  157.7 1.1 copy-done
  158.8 0.7 copy-done.5
  159.5 30.4 %all-to-all-start.2 = ((f32[8,3,32,512]{3,2,1,0:T(8,128)}), f32[8,3,32,512]{3,2,1,0:T(8,128)S(1)}, u32[]{:S(2)}, u32[]{:S(2)}) async-start(f32[8,3,32,512]{3,2,1,0:T(8,128)} %copy-done), calls=%async_computation.2 | async-start | bytes 3145728 | tf_op jit(solution)/shard_map/all_to_all | solution.py:247
  189.9 16.6 %sort.61 = (s32[32768]{0:T(1024)}, f32[32768]{0:T(1024)S(1)}, f32[32768]{0:T(1024)S(1)}, f32[32768]{0:T(1024)S(1)}) sort(s32[32768]{0:T(1024)S(1)} %bitcast.66, f32[32768]{0:T(1024)S(1)} %get-tuple-element.44, f32[32768]{0:T(1024)S(1)} %get-tuple-element.43, f32[32768]{0:T(1024)S(1)} %get-tuple-element.42), dimensions={0}, to_apply=%region_1.0 | sort | flops 491520 | bytes 1048576 | tf_op jit(solution)/shard_map/sort | solution.py:249
  206.6 1.1 pad_maximum_fusion
  207.7 2.6 %all-to-all-done.2 = f32[8,3,32,512]{3,2,1,0:T(8,128)S(1)} async-done(((f32[8,3,32,512]{3,2,1,0:T(8,128)}), f32[8,3,32,512]{3,2,1,0:T(8,128)S(1)}, u32[]{:S(2)}, u32[]{:S(2)}) %all-to-all-start.2) | async-done | bytes 1572896 | tf_op jit(solution)/shard_map/all_to_all | solution.py:247
  210.7 1.3 copy-done.10
  212.0 1.6 fusion
  (23 shorter events, 0.6 us)
Async XLA Ops:
  1.6 0.9 copy-start.1
  2.5 0.8 copy-start.7
  3.3 0.7 copy-start.8
  4.0 37.2 %copy-start.9 = (f32[3,1,256,512]{3,2,1,0:T(8,128)S(1)}, f32[3,1,256,512]{3,2,1,0:T(8,128)}, u32[]{:S(2)}) copy-start(f32[3,1,256,512]{3,2,1,0:T(8,128)} %param.7) | copy-start | bytes 4718596
  29.6 25.2 %all-to-all-start = ((f32[128,8,128]{2,1,0:T(8,128)}), f32[128,8,128]{2,1,0:T(8,128)S(1)}, u32[]{:S(2)}, u32[]{:S(2)}) async-start(f32[128,8,128]{2,1,0:T(8,128)} %pick_particles.1), calls=%async_computation | async-start | bytes 1048576 | tf_op jit(solution)/shard_map/all_to_all | solution.py:206
  45.1 14.1 %copy-start.2 = (s32[32768]{0:T(1024)S(1)}, s32[32768]{0:T(1024)}, u32[]{:S(2)}) copy-start(s32[32768]{0:T(1024)} %param.13) | copy-start | bytes 393220
  54.8 30.6 %all-to-all-start.1 = ((f32[8,4,32,512]{3,1,2,0:T(4,128)}), f32[8,4,32,512]{3,1,2,0:T(4,128)}, u32[]{:S(2)}, u32[]{:S(2)}) async-start(f32[8,4,32,512]{3,1,2,0:T(4,128)} %copy.20), calls=%async_computation.1 | async-start | bytes 4194304 | tf_op jit(solution)/shard_map/all_to_all | solution.py:195
  86.9 39.7 %collective-permute-start.3 = (f32[8,4,512]{2,1,0:T(4,128)}, f32[8,4,512]{2,1,0:T(4,128)}, u32[]{:S(2)}, u32[]{:S(2)}) collective-permute-start(f32[8,4,512]{2,1,0:T(4,128)} %get-tuple-element.34), channel_id=1, source_target_pairs={{1,0},{2,1},{3,2},{4,3},{5,4},{6,5},{7,6},{9,8},{10,9},{11,10},{12... | collective-permute-start | bytes 196616 | tf_op jit(solution)/shard_map/ppermute | solution.py:180
  88.2 38.5 %collective-permute-start.2 = (f32[8,4,512]{2,1,0:T(4,128)}, f32[8,4,512]{2,1,0:T(4,128)}, u32[]{:S(2)}, u32[]{:S(2)}) collective-permute-start(f32[8,4,512]{2,1,0:T(4,128)} %get-tuple-element.35), channel_id=1, source_target_pairs={{0,1},{1,2},{2,3},{3,4},{4,5},{5,6},{6,7},{8,9},{9,10},{10,11},{11... | collective-permute-start | bytes 196616 | tf_op jit(solution)/shard_map/ppermute | solution.py:180
  95.9 30.8 %collective-permute-start.1 = (f32[4,32,512]{2,1,0:T(8,128)}, f32[4,32,512]{2,1,0:T(8,128)S(1)}, u32[]{:S(2)}, u32[]{:S(2)}) collective-permute-start(f32[4,32,512]{2,1,0:T(8,128)} %get-tuple-element.36), channel_id=1, source_target_pairs={{8,0},{16,8},{24,16},{32,24},{40,32},{48,40},{56,48},{64,56},{72,6... | collective-permute-start | bytes 786440 | tf_op jit(solution)/shard_map/ppermute | solution.py:180
  99.5 27.2 %collective-permute-start = (f32[4,32,512]{2,1,0:T(8,128)}, f32[4,32,512]{2,1,0:T(8,128)S(1)}, u32[]{:S(2)}, u32[]{:S(2)}) collective-permute-start(f32[4,32,512]{2,1,0:T(8,128)} %get-tuple-element.37), channel_id=1, source_target_pairs={{0,8},{8,16},{16,24},{24,32},{32,40},{40,48},{48,56},{56,64},{64,7... | collective-permute-start | bytes 786440 | tf_op jit(solution)/shard_map/ppermute | solution.py:180
  126.7 0.9 copy-start.3
  127.6 0.9 copy-start.4
  157.7 1.1 copy-start
  158.8 0.7 copy-start.5
  159.5 30.4 %copy-start.6 = (s32[256,128]{1,0:T(8,128)S(1)}, s32[256,128]{1,0:T(8,128)}, u32[]{:S(2)}) copy-start(s32[256,128]{1,0:T(8,128)} %copy-done.5) | copy-start | bytes 393220
  159.5 50.8 %all-to-all-start.2 = ((f32[8,3,32,512]{3,2,1,0:T(8,128)}), f32[8,3,32,512]{3,2,1,0:T(8,128)S(1)}, u32[]{:S(2)}, u32[]{:S(2)}) async-start(f32[8,3,32,512]{3,2,1,0:T(8,128)} %copy-done), calls=%async_computation.2 | async-start | bytes 3145728 | tf_op jit(solution)/shard_map/all_to_all | solution.py:247
  210.5 1.4 copy-start.10
  210.5 1.5 copy-start.11

commit v2 on v1

--- a/solution.py
+++ b/solution.py
@@ -20,18 +20,60 @@
     return high, mid, low
 
 
-def pick_kernel(counts_ref, pv_ref, coef_ref, rows_ref, out_ref, table, *, cap):
-    me = lax.axis_index("slab") * lax.axis_size("brick") + lax.axis_index("brick")
+def exchange_kernel(
+    counts_ref, pv_ref, coef_ref, rows_ref, u_ref, frac_ref, arrived_ref, bricks_ref, zhalo_ref,
+    table, packed, stage, fluid_send, fluid_recv, part_send, part_recv, halo_send, halo_recv, *, cap, group,
+):
+    n_slab, n_brick = lax.axis_size("slab"), lax.axis_size("brick")
+    devices = n_slab * n_brick
+    slab, brick = lax.axis_index("slab"), lax.axis_index("brick")
+    me = slab * n_brick + brick
+    mesh_id = pl.DeviceIdType.MESH
+
+    def coords(d):
+        return (d // n_brick, d % n_brick)
+
+    barrier = pltpu.get_barrier_semaphore()
+
+    def greet(j, carry):
+        pl.semaphore_signal(barrier, inc=1, device_id=coords((me + j) % devices), device_id_type=mesh_id)
+        return carry
+
+    lax.fori_loop(1, devices, greet, 0)
+
     for c in range(4):
+        for b in range(8):
+            field = frac_ref[b * 32 : (b + 1) * 32, :] if c == 3 else u_ref[c, b * 32 : (b + 1) * 32, :]
+            stage[b, c * 32 : (c + 1) * 32, :] = field
+            if b < 7:
+                stage[b + 1, 128 + c : 129 + c, :] = field[31:32]
+            if b > 0:
+                stage[b - 1, 132 + c : 133 + c, :] = field[0:1]
+        stage[0, 128 + c : 129 + c, :] = jnp.zeros((1, 512), F32)
+        stage[7, 132 + c : 133 + c, :] = jnp.zeros((1, 512), F32)
         whole = coef_ref[...] if c == 3 else pv_ref[c]
         halves = jnp.concatenate([whole[:64], whole[64:]], axis=1)
         for p, piece in enumerate(split3(halves)):
             table[p * 256 + c * 64 : p * 256 + (c + 1) * 64, :] = piece
+
+    pl.semaphore_wait(barrier, devices - 1)
+
+    def chunk(j):
+        to = (brick + j) % n_brick
+        return pltpu.make_async_remote_copy(
+            src_ref=stage.at[to], dst_ref=bricks_ref.at[brick], send_sem=fluid_send.at[to],
+            recv_sem=fluid_recv.at[brick], device_id=(slab, to), device_id_type=mesh_id,
+        )
+
+    for j in range(1, 8):
+        chunk(j).start()
+    bricks_ref[brick] = stage[brick]
+
     r_iota = lax.broadcasted_iota(I32, (256, cap), 0)
     l_iota = lax.broadcasted_iota(I32, (64, cap), 0)
     k_iota = lax.broadcasted_iota(I32, (1, cap), 1)
 
-    def one(t, carry):
+    def pick(t):
         row = jnp.concatenate([rows_ref[pl.ds(2 * t, 1), :], rows_ref[pl.ds(2 * t + 1, 1), :]], axis=1)
         r = (row & 127) + ((row >> 13) << 7)
         l = (row >> 7) & 63
@@ -41,17 +83,89 @@
         mask = l_iota == l
         live = k_iota < counts_ref[t]
         slot = (me * cap + k_iota).astype(F32)
+        values = []
         for c in range(4):
             value = jnp.sum(jnp.where(mask, got[c * 64 : (c + 1) * 64], 0.0), axis=0, keepdims=True)
             if c == 0:
                 value = jnp.where(live, value, slot)
             if c == 3:
                 value = jnp.where(live, value, 0.0)
-            out_ref[t, 2 * c : 2 * c + 1, :] = value[:, :128]
-            out_ref[t, 2 * c + 1 : 2 * c + 2, :] = value[:, 128:]
+            values += [value[:, :128], value[:, 128:]]
+        return jnp.concatenate(values, axis=0)
+
+    def parcel(t):
+        return pltpu.make_async_remote_copy(
+            src_ref=packed.at[t], dst_ref=arrived_ref.at[me], send_sem=part_send, recv_sem=part_recv,
+            device_id=coords(t), device_id_type=mesh_id,
+        )
+
+    def some(i, carry):
+        to = [(me + 1 + i * group + j) % devices for j in range(group)]
+        picked = [pick(t) for t in to]
+        for t, value in zip(to, picked):
+            packed[t] = value
+        for t in to:
+            parcel(t).start()
         return carry
 
-    lax.fori_loop(0, out_ref.shape[0], one, 0, unroll=2)
+    lax.fori_loop(0, devices // group - 1, some, 0)
+    to = [(me + 1 + devices - group + j) % devices for j in range(group)]
+    picked = [pick(t) for t in to]
+    for t, value in zip(to[:-1], picked):
+        packed[t] = value
+    arrived_ref[me] = picked[-1]
+    for t in to[:-1]:
+        parcel(t).start()
+
+    for j in range(1, 8):
+        source = (brick + j) % n_brick
+        pltpu.make_async_remote_copy(
+            src_ref=stage.at[source], dst_ref=bricks_ref.at[source], send_sem=fluid_send.at[source],
+            recv_sem=fluid_recv.at[source], device_id=(slab, source), device_id_type=mesh_id,
+        ).wait_recv()
+
+    def halo(i, to):
+        return pltpu.make_async_remote_copy(
+            src_ref=bricks_ref.at[7 - 7 * i, pl.ds(0, 128)], dst_ref=zhalo_ref.at[i], send_sem=halo_send.at[i],
+            recv_sem=halo_recv.at[i], device_id=(to, brick), device_id_type=mesh_id,
+        )
+
+    up, down = slab < n_slab - 1, slab > 0
+
+    @pl.when(up)
+    def _():
+        halo(0, slab + 1).start()
+
+    @pl.when(down)
+    def _():
+        halo(1, slab - 1).start()
+
+    @pl.when(jnp.logical_not(up))
+    def _():
+        zhalo_ref[1] = jnp.zeros((128, 512), F32)
+
+    @pl.when(jnp.logical_not(down))
+    def _():
+        zhalo_ref[0] = jnp.zeros((128, 512), F32)
+
+    for j in range(1, 8):
+        chunk(j).wait_send()
+    rest = pltpu.make_async_remote_copy(
+        src_ref=packed.at[pl.ds(0, devices - 1)], dst_ref=arrived_ref.at[pl.ds(0, devices - 1)],
+        send_sem=part_send, recv_sem=part_recv, device_id=coords((me + 1) % devices), device_id_type=mesh_id,
+    )
+    rest.wait_send()
+    rest.wait_recv()
+
+    @pl.when(up)
+    def _():
+        halo(0, slab + 1).wait_send()
+        halo(1, slab + 1).wait_recv()
+
+    @pl.when(down)
+    def _():
+        halo(1, slab - 1).wait_send()
+        halo(0, slab - 1).wait_recv()
 
 
 def key_kernel(arrived_ref, cell_ref, key_ref, data_ref, starts_ref):
@@ -82,20 +196,21 @@
 
 
 def brick_kernel(
-    starts_ref, key_ref, coef_ref, p0_ref, p1_ref, p2_ref, fluid_ref, zlo_ref, zhi_ref, xlo_ref, xhi_ref,
+    starts_ref, key_ref, coef_ref, p0_ref, p1_ref, p2_ref, bricks_ref, zhalo_ref,
     force_ref, slot_ref, net_ref, padded, table, deposit, *, width,
 ):
     rows = key_ref.shape[0]
     n = width // 128
     force_ref[...] = jnp.zeros_like(force_ref)
     slot_ref[...] = jnp.where(coef_ref[...] != 0.0, (key_ref[...] >> 12) & 32767, p0_ref[...].astype(I32))
-    for z in range(8):
-        padded[z + 1, :, 8:40, :] = fluid_ref[z]
-        for c in range(4):
-            padded[z + 1, c, 7:8, :] = xlo_ref[z, c : c + 1, :]
-            padded[z + 1, c, 40:41, :] = xhi_ref[z, c : c + 1, :]
-    padded[0, :, 8:40, :] = zlo_ref[...]
-    padded[9, :, 8:40, :] = zhi_ref[...]
+    for c in range(4):
+        own = slice(c * 32, (c + 1) * 32)
+        for z in range(8):
+            padded[z + 1, c, 8:40, :] = bricks_ref[z, own, :]
+            padded[z + 1, c, 7:8, :] = bricks_ref[z, 128 + c : 129 + c, :]
+            padded[z + 1, c, 40:41, :] = bricks_ref[z, 132 + c : 133 + c, :]
+        padded[0, c, 8:40, :] = zhalo_ref[0, own, :]
+        padded[9, c, 8:40, :] = zhalo_ref[1, own, :]
 
     r_iota = lax.broadcasted_iota(I32, (256, width), 0)
     l_iota = lax.broadcasted_iota(I32, (16, width), 0)
@@ -106,7 +221,7 @@
         z, q = b // 4, b % 4
         x8 = pl.multiple_of(q * 8, 8)
         for c in range(4):
-            centre = fluid_ref[z, c, pl.ds(x8, 8), :]
+            centre = padded[z + 1, c, pl.ds(x8 + 8, 8), :]
             for h in range(2):
                 for p, piece in enumerate(split3(centre[:, h * 256 : (h + 1) * 256])):
                     at = p * 64 + c * 16 + h * 8
@@ -174,12 +289,6 @@
     lax.fori_loop(0, 32, block, 0)
 
 
-def shift(block, axis, step):
-    count = lax.axis_size(axis)
-    pairs = [(i, i + step) for i in range(count) if 0 <= i + step < count]
-    return lax.ppermute(block, axis, pairs)
-
-
 def per_device(
     fluid_velocity, porosity, particle_velocity, drag_coef, send_rows, counts, recv_cell
 ):
@@ -191,24 +300,38 @@
     smem = pl.BlockSpec(memory_space=pltpu.SMEM)
     params = pltpu.CompilerParams(vmem_limit_bytes=40 << 20)
 
-    stacked = jnp.concatenate([fluid_velocity[:, 0], porosity], 0).reshape(4, 8, 32, 512)
-    bricks = lax.all_to_all(jnp.swapaxes(stacked, 0, 1), "brick", split_axis=0, concat_axis=0, tiled=True)
-
-    packed = pl.pallas_call(
-        functools.partial(pick_kernel, cap=cap),
-        out_shape=jax.ShapeDtypeStruct((devices, 8, 128), F32),
-        in_specs=[smem, vmem, vmem, vmem],
-        out_specs=vmem,
-        scratch_shapes=[pltpu.VMEM((768, 256), BF16)],
-        compiler_params=params,
-        name="pick_particles",
-    )(counts, particle_velocity.reshape(3, 128, 128), drag_coef.reshape(128, 128), send_rows.reshape(256, 128))
-    arrived = lax.all_to_all(packed, ("slab", "brick"), split_axis=0, concat_axis=0, tiled=True)
-
-    zlo = shift(bricks[7], "slab", 1)
-    zhi = shift(bricks[0], "slab", -1)
-    xlo = shift(bricks[:, :, 31, :], "brick", 1)
-    xhi = shift(bricks[:, :, 0, :], "brick", -1)
+    arrived, bricks, zhalo = pl.pallas_call(
+        functools.partial(exchange_kernel, cap=cap, group=4),
+        out_shape=(
+            jax.ShapeDtypeStruct((devices, 8, 128), F32),
+            jax.ShapeDtypeStruct((8, 136, 512), F32),
+            jax.ShapeDtypeStruct((2, 128, 512), F32),
+        ),
+        in_specs=[smem] + [vmem] * 5,
+        out_specs=(vmem, vmem, vmem),
+        scratch_shapes=[
+            pltpu.VMEM((768, 256), BF16),
+            pltpu.VMEM((devices, 8, 128), F32),
+            pltpu.VMEM((8, 136, 512), F32),
+            pltpu.SemaphoreType.DMA((8,)),
+            pltpu.SemaphoreType.DMA((8,)),
+            pltpu.SemaphoreType.DMA,
+            pltpu.SemaphoreType.DMA,
+            pltpu.SemaphoreType.DMA((2,)),
+            pltpu.SemaphoreType.DMA((2,)),
+        ],
+        compiler_params=pltpu.CompilerParams(
+            vmem_limit_bytes=40 << 20, collective_id=0, has_side_effects=True
+        ),
+        name="exchange",
+    )(
+        counts,
+        particle_velocity.reshape(3, 128, 128),
+        drag_coef.reshape(128, 128),
+        send_rows.reshape(256, 128),
+        fluid_velocity.reshape(3, 256, 512),
+        porosity.reshape(256, 512),
+    )
 
     key, data, starts = pl.pallas_call(
         key_kernel,
@@ -233,7 +356,7 @@
             jax.ShapeDtypeStruct((256, 128), I32),
             jax.ShapeDtypeStruct((8, 3, 32, 512), F32),
         ),
-        in_specs=[smem] + [vmem] * 10,
+        in_specs=[smem] + [vmem] * 7,
         out_specs=(vmem, vmem, vmem),
         scratch_shapes=[
             pltpu.VMEM((10, 4, 48, 512), F32),
@@ -242,7 +365,7 @@
         ],
         compiler_params=params,
         name="brick_forces",
-    )(starts, *[part.reshape(256, 128) for part in ordered], bricks, zlo, zhi, xlo, xhi)
+    )(starts, *[part.reshape(256, 128) for part in ordered], bricks, zhalo)
 
     returned = lax.all_to_all(net, "brick", split_axis=0, concat_axis=0, tiled=True)
     flat = force.reshape(3, -1)

time: 214 us -> 177 us (0.83)
  the two profiles are of different devices: /device:TPU:1 before, /device:TPU:8 now
where the time goes in v2:
time: 177 us; the launch traced here: 175 us
  Pallas kernels  76.3 us (43%)
  other arithmetic  43.7 us (25%)
  starting transfers between devices  41 us (23%)
  local copies, waits for them, and re-layouts  11.7 us (7%)
  waiting for transfers between devices  1.99 us (1%)
    pallas_call x1, Pallas kernels, per_device(): pl.pallas_call(functools.partial(exchange_kernel, cap=cap, group=4), out_...  56.4 us
    all_to_all x1, starting transfers between devices, per_device(): lax.all_to_all(net, 'brick', split_axis=0, concat_axis=0, tiled=True)  41 us
    sort x1, other arithmetic, per_device(): lax.sort((key.reshape(-1), flat[3], flat[0], flat[1], flat[2]), num_keys=...  24.1 us
    pallas_call x1, Pallas kernels, per_device(): pl.pallas_call(functools.partial(brick_kernel, width=256), out_shape=(jax...  18.2 us
    sort x1, other arithmetic, per_device(): lax.sort((slot.reshape(-1), flat[0], flat[1], flat[2]), num_keys=1, is_st...  16.6 us
    unnamed x27, local copies, waits for them, and re-layouts  10.8 us
  transfers between devices with their start and end apart: 1, of which 1 were waited for; matrix products, arithmetic and copies ran while one was open for 10% of the time, Pallas kernels for 0%

profile of v2, /device:TPU:8, one launch (start us, length us, event | category | flops | bytes accessed | tf_op | source)
XLA Modules:
  0.0 175.4 jit_solution(8131539038339555369)
XLA Ops:
  0.6 0.0 copy-start.5
  0.6 1.0 copy.14
  1.6 0.0 copy-start
  1.7 1.4 copy-done
  3.1 0.0 copy-start.2
  3.1 1.0 copy-done.2
  4.1 0.9 copy-done.10
  5.0 0.8 copy-done.11
  5.8 0.7 copy-done.12
  6.5 56.4 %exchange.1 = (f32[128,8,128]{2,1,0:T(8,128)S(1)}, f32[8,136,512]{2,1,0:T(8,128)S(1)}, f32[2,128,512]{2,1,0:T(8,128)S(1)}) custom-call(s32[128]{0:T(128)S(1)} %copy-done.12, f32[3,128,128]{2,1,0:T(8,128)S(1)} %bitcast.45, f32[128,128]{1,0:T(8,128)S(1)} %bitcast.55, s32[256,128]{1,0:T(8,128)S(1)} %bitcast.54, f32[3,256,512]{2,1,0:T(8,128)S(1)} %bitcast.42, ...), custom_call_target="tpu_custom_call" | custom-call | tf_op jit(solution)/shard_map/exchange/pallas_call | solution.py:303
  62.9 0.0 copy-done.5
  62.9 1.7 block_keys.1
  64.6 0.7 slice_bitcast_fusion.3
  65.3 24.1 %sort.60 = (s32[32768]{0:T(1024)S(1)}, f32[32768]{0:T(1024)S(1)}, f32[32768]{0:T(1024)S(1)}, f32[32768]{0:T(1024)}, f32[32768]{0:T(1024)}) sort(s32[32768]{0:T(1024)S(1)} %bitcast.52, f32[32768]{0:T(1024)} %get-tuple-element.41, f32[32768]{0:T(1024)} %get-tuple-element.40, f32[32768]{0:T(1024)S(1)} %get-tuple-element.39, f32[32768]{0:T(1024)S(1)} %get-tuple-element.38), dimensions={0}, to_apply=%region_0.0 | sort | flops 491520 | bytes 1310720 | tf_op jit(solution)/shard_map/sort | solution.py:349
  89.4 0.9 copy-done.6
  90.3 0.9 copy-done.7
  91.2 18.2 %brick_forces.1 = (f32[3,256,128]{2,1,0:T(8,128)S(1)}, s32[256,128]{1,0:T(8,128)S(1)}, f32[8,3,32,512]{3,2,1,0:T(8,128)S(1)}) custom-call(s32[33]{0:T(128)S(1)} %get-tuple-element.20.starts_ref, s32[256,128]{1,0:T(8,128)S(1)} %bitcast.47, f32[256,128]{1,0:T(8,128)S(1)} %bitcast.48, f32[256,128]{1,0:T(8,128)S(1)} %bitcast.49, f32[256,128]{1,0:T(8,128)S(1)} %bitcast.50, ...), custom_call_target="tpu_custom_call" | custom-call | tf_op jit(solution)/shard_map/brick_forces/pallas_call | solution.py:352
  109.5 0.0 copy-start.4
  109.5 1.1 copy-done.4
  110.6 0.7 copy-done.8
  111.3 41.0 %all-to-all-start = ((f32[8,3,32,512]{3,2,1,0:T(8,128)}), f32[8,3,32,512]{3,2,1,0:T(8,128)S(1)}, u32[]{:S(2)}, u32[]{:S(2)}) async-start(f32[8,3,32,512]{3,2,1,0:T(8,128)} %copy-done.4), calls=%async_computation | async-start | bytes 3145728 | tf_op jit(solution)/shard_map/all_to_all | solution.py:370
  152.3 0.0 copy-done.9
  152.3 16.6 %sort.61 = (s32[32768]{0:T(1024)}, f32[32768]{0:T(1024)S(1)}, f32[32768]{0:T(1024)S(1)}, f32[32768]{0:T(1024)S(1)}) sort(s32[32768]{0:T(1024)S(1)} %bitcast.53, f32[32768]{0:T(1024)S(1)} %get-tuple-element.44, f32[32768]{0:T(1024)S(1)} %get-tuple-element.43, f32[32768]{0:T(1024)S(1)} %get-tuple-element.42), dimensions={0}, to_apply=%region_1.0 | sort | flops 491520 | bytes 1048576 | tf_op jit(solution)/shard_map/sort | solution.py:372
  168.9 1.1 pad_maximum_fusion
  170.1 2.0 %all-to-all-done = f32[8,3,32,512]{3,2,1,0:T(8,128)S(1)} async-done(((f32[8,3,32,512]{3,2,1,0:T(8,128)}), f32[8,3,32,512]{3,2,1,0:T(8,128)S(1)}, u32[]{:S(2)}, u32[]{:S(2)}) %all-to-all-start) | async-done | bytes 1572896 | tf_op jit(solution)/shard_map/all_to_all | solution.py:370
  172.0 0.3 multiply_bitcast_fusion
  172.3 0.0 copy-start.1
  172.3 0.0 copy-start.3
  172.3 0.1 copy.9
  172.5 1.3 copy-done.1
  173.7 0.1 copy-done.3
  173.8 1.6 fusion
  (8 shorter events, 0.0 us)
Async XLA Ops:
  0.6 62.2 %copy-start.5 = (s32[32768]{0:T(1024)S(1)}, s32[32768]{0:T(1024)}, u32[]{:S(2)}) copy-start(s32[32768]{0:T(1024)} %param.13) | copy-start | bytes 393220
  1.6 1.4 copy-start
  3.1 1.0 copy-start.2
  4.1 0.9 copy-start.10
  5.0 0.8 copy-start.11
  5.8 0.7 copy-start.12
  89.4 0.9 copy-start.6
  90.3 0.9 copy-start.7
  109.5 1.1 copy-start.4
  110.6 0.7 copy-start.8
  111.3 41.0 %copy-start.9 = (s32[256,128]{1,0:T(8,128)S(1)}, s32[256,128]{1,0:T(8,128)}, u32[]{:S(2)}) copy-start(s32[256,128]{1,0:T(8,128)} %copy-done.8) | copy-start | bytes 393220
  111.3 60.8 %all-to-all-start = ((f32[8,3,32,512]{3,2,1,0:T(8,128)}), f32[8,3,32,512]{3,2,1,0:T(8,128)S(1)}, u32[]{:S(2)}, u32[]{:S(2)}) async-start(f32[8,3,32,512]{3,2,1,0:T(8,128)} %copy-done.4), calls=%async_computation | async-start | bytes 3145728 | tf_op jit(solution)/shard_map/all_to_all | solution.py:370
  172.3 1.4 copy-start.1
  172.3 1.5 copy-start.3

commit v3 on v2

--- a/solution.py
+++ b/solution.py
@@ -69,29 +69,35 @@
         chunk(j).start()
     bricks_ref[brick] = stage[brick]
 
-    r_iota = lax.broadcasted_iota(I32, (256, cap), 0)
+    r_iota = lax.broadcasted_iota(I32, (256, cap), 0).astype(F32).astype(BF16)
+    one, zero = jnp.ones((), BF16), jnp.zeros((), BF16)
     l_iota = lax.broadcasted_iota(I32, (64, cap), 0)
     k_iota = lax.broadcasted_iota(I32, (1, cap), 1)
 
-    def pick(t):
-        row = jnp.concatenate([rows_ref[pl.ds(2 * t, 1), :], rows_ref[pl.ds(2 * t + 1, 1), :]], axis=1)
-        r = (row & 127) + ((row >> 13) << 7)
-        l = (row >> 7) & 63
-        onehot = jnp.where(r_iota == r, 1.0, 0.0).astype(BF16)
-        got = jnp.dot(table[...], onehot, preferred_element_type=F32)
-        got = got[:256] + (got[256:512] + got[512:])
-        mask = l_iota == l
-        live = k_iota < counts_ref[t]
+    def pick(to):
+        onehots, planes, gots, picked = [], [], [], []
+        for t in to:
+            row = jnp.concatenate([rows_ref[pl.ds(2 * t, 1), :], rows_ref[pl.ds(2 * t + 1, 1), :]], axis=1)
+            r = (row & 127) + ((row >> 13) << 7)
+            onehots.append(jnp.where(r_iota == r.astype(F32).astype(BF16), one, zero))
+            planes.append((row >> 7) & 63)
+        for onehot in onehots:
+            gots.append(jnp.dot(table[...], onehot, preferred_element_type=F32))
         slot = (me * cap + k_iota).astype(F32)
-        values = []
-        for c in range(4):
-            value = jnp.sum(jnp.where(mask, got[c * 64 : (c + 1) * 64], 0.0), axis=0, keepdims=True)
-            if c == 0:
-                value = jnp.where(live, value, slot)
-            if c == 3:
-                value = jnp.where(live, value, 0.0)
-            values += [value[:, :128], value[:, 128:]]
-        return jnp.concatenate(values, axis=0)
+        for t, got, l in zip(to, gots, planes):
+            got = got[:256] + (got[256:512] + got[512:])
+            mask = l_iota == l
+            live = k_iota < counts_ref[t]
+            values = []
+            for c in range(4):
+                value = jnp.sum(jnp.where(mask, got[c * 64 : (c + 1) * 64], 0.0), axis=0, keepdims=True)
+                if c == 0:
+                    value = jnp.where(live, value, slot)
+                if c == 3:
+                    value = jnp.where(live, value, 0.0)
+                values += [value[:, :128], value[:, 128:]]
+            picked.append(jnp.concatenate(values, axis=0))
+        return picked
 
     def parcel(t):
         return pltpu.make_async_remote_copy(
@@ -101,7 +107,7 @@
 
     def some(i, carry):
         to = [(me + 1 + i * group + j) % devices for j in range(group)]
-        picked = [pick(t) for t in to]
+        picked = pick(to)
         for t, value in zip(to, picked):
             packed[t] = value
         for t in to:
@@ -110,7 +116,7 @@
 
     lax.fori_loop(0, devices // group - 1, some, 0)
     to = [(me + 1 + devices - group + j) % devices for j in range(group)]
-    picked = [pick(t) for t in to]
+    picked = pick(to)
     for t, value in zip(to[:-1], picked):
         packed[t] = value
     arrived_ref[me] = picked[-1]
@@ -197,7 +203,7 @@
 
 def brick_kernel(
     starts_ref, key_ref, coef_ref, p0_ref, p1_ref, p2_ref, bricks_ref, zhalo_ref,
-    force_ref, slot_ref, net_ref, padded, table, deposit, *, width,
+    force_ref, slot_ref, net_ref, padded, table, deposit, *, width, group,
 ):
     rows = key_ref.shape[0]
     n = width // 128
@@ -214,79 +220,108 @@
 
     r_iota = lax.broadcasted_iota(I32, (256, width), 0)
     l_iota = lax.broadcasted_iota(I32, (16, width), 0)
+    r_iota = r_iota.astype(F32).astype(BF16)
+    l_bf = l_iota.astype(F32).astype(BF16)
     p_iota = lax.broadcasted_iota(I32, (1, width), 1)
     y_iota = lax.broadcasted_iota(I32, (8, 512), 1)
-
-    def block(b, carry):
-        z, q = b // 4, b % 4
-        x8 = pl.multiple_of(q * 8, 8)
-        for c in range(4):
-            centre = padded[z + 1, c, pl.ds(x8 + 8, 8), :]
-            for h in range(2):
-                for p, piece in enumerate(split3(centre[:, h * 256 : (h + 1) * 256])):
-                    at = p * 64 + c * 16 + h * 8
-                    table[at : at + 8, :] = piece.astype(F32)
-        pieces = table[...].astype(BF16)
-        deposit[...] = jnp.zeros_like(deposit)
-        first, end = starts_ref[b], starts_ref[b + 1]
-        row0 = first // 128
+    one, zero = jnp.ones((), BF16), jnp.zeros((), BF16)
+
+    def blocks(g, carry):
+        bs = [g * group + i for i in range(group)]
+        row0s, counts = [], []
+        for i, b in enumerate(bs):
+            z, q = b // 4, b % 4
+            x8 = pl.multiple_of(q * 8, 8)
+            for c in range(4):
+                centre = padded[z + 1, c, pl.ds(x8 + 8, 8), :]
+                for p, piece in enumerate(split3(centre)):
+                    at = p * 64 + c * 16
+                    table[i, at : at + 16, :] = jnp.concatenate([piece[:, :256], piece[:, 256:]], axis=0)
+            deposit[i] = jnp.zeros(deposit.shape[1:], F32)
+            first, end = starts_ref[b], starts_ref[b + 1]
+            row0 = first // 128
+            row0s.append(row0)
+            counts.append(jnp.where(end > first, (end - row0 * 128 + width - 1) // width, 0))
+        windows = counts[0]
+        for c in counts[1:]:
+            windows = jnp.maximum(windows, c)
 
         def window(w, inner):
-            row = row0 + w * n
-            at = jnp.minimum(row, rows - n)
-
-            def line(ref):
-                return jnp.concatenate([ref[pl.ds(at + i, 1), :] for i in range(n)], axis=1)
-
-            key = line(key_ref)
-            valid = ((key >> 27) + 16 == b) & (p_iota >= (row - at) * 128)
-            r = jnp.where(valid, key & 255, -1)
-            l = ((key >> 9) & 7) + ((key >> 8) & 1) * 8
-            onehot = jnp.where(r_iota == r, 1.0, 0.0).astype(BF16)
-            got = jnp.dot(pieces, onehot, preferred_element_type=F32)
-            got = got[:64] + (got[64:128] + got[128:])
-            mask = l_iota == l
-            u = [
-                jnp.sum(jnp.where(mask, got[c * 16 : (c + 1) * 16], 0.0), axis=0, keepdims=True) for c in range(4)
-            ]
-            frac = jnp.where(valid, u[3], 1.0)
-            beta = line(coef_ref) * (1.0 - frac) / (frac * frac)
-            split = []
-            for c, ref in enumerate((p0_ref, p1_ref, p2_ref)):
-                force = jnp.where(valid, beta * (u[c] - line(ref)), 0.0)
-                for i in range(n):
-                    force_ref[c, pl.ds(at + i, 1), :] += force[:, i * 128 : (i + 1) * 128]
-                split.append(split3(force))
-            spread = jnp.concatenate(
-                [jnp.where(mask, split[c][p].astype(F32), 0.0) for p in range(3) for c in range(3)], axis=0
-            ).astype(BF16)
-            deposit[...] += lax.dot_general(
-                spread, onehot, (((1,), (1,)), ((), ())), preferred_element_type=F32
-            )
+            ats, oh, valids, ls, gots = [], [], [], [], []
+
+            def line(ref, at):
+                return jnp.concatenate([ref[pl.ds(at + k, 1), :] for k in range(n)], axis=1)
+
+            for i, b in enumerate(bs):
+                row = row0s[i] + w * n
+                at = jnp.minimum(row, rows - n)
+                key = line(key_ref, at)
+                valid = ((key >> 27) + 16 == b) & (p_iota >= (row - at) * 128)
+                r = jnp.where(valid, key & 255, -1)
+                l = ((key >> 9) & 7) + ((key >> 8) & 1) * 8
+                ats.append(at)
+                oh.append(jnp.where(r_iota == r.astype(F32).astype(BF16), one, zero))
+                valids.append(valid)
+                ls.append(l)
+            for i in range(group):
+                gots.append(jnp.dot(table[i], oh[i], preferred_element_type=F32))
+            spreads = []
+            forces = []
+            for i in range(group):
+                got = gots[i]
+                got = got[:64] + (got[64:128] + got[128:])
+                mask = l_iota == ls[i]
+                u = [
+                    jnp.sum(jnp.where(mask, got[c * 16 : (c + 1) * 16], 0.0), axis=0, keepdims=True) for c in range(4)
+                ]
+                frac = jnp.where(valids[i], u[3], 1.0)
+                beta = line(coef_ref, ats[i]) * (1.0 - frac) / (frac * frac)
+                fs = [
+                    jnp.where(valids[i], beta * (u[c] - line(ref, ats[i])), 0.0)
+                    for c, ref in enumerate((p0_ref, p1_ref, p2_ref))
+                ]
+                forces.append(fs)
+                split = [split3(f) for f in fs]
+                low_mask = l_bf == ls[i].astype(F32).astype(BF16)
+                spreads.append(
+                    jnp.concatenate(
+                        [jnp.where(low_mask, split[c][p], zero) for p in range(3) for c in range(3)], axis=0
+                    )
+                )
+            for i in range(group):
+                deposit[i] += lax.dot_general(
+                    spreads[i], oh[i], (((1,), (1,)), ((), ())), preferred_element_type=F32
+                )
+            for i in range(group):
+                for c in range(3):
+                    for k in range(n):
+                        force_ref[c, pl.ds(ats[i] + k, 1), :] += forces[i][c][:, k * 128 : (k + 1) * 128]
             return inner
 
-        windows = jnp.where(end > first, (end - row0 * 128 + width - 1) // width, 0)
         lax.fori_loop(0, windows, window, 0)
 
-        tall = [padded[z + 1, c, pl.ds(x8, 24), :] for c in range(4)]
-        below = [padded[z, c, pl.ds(x8 + 8, 8), :] for c in range(4)]
-        above = [padded[z + 2, c, pl.ds(x8 + 8, 8), :] for c in range(4)]
-        centre = [t[8:16] for t in tall]
-        sides = [above, below, [t[9:17] for t in tall], [t[7:15] for t in tall]]
-        sides.append([jnp.where(y_iota == 511, 0.0, pltpu.roll(t, 511, 1)) for t in centre])
-        sides.append([jnp.where(y_iota == 0, 0.0, pltpu.roll(t, 1, 1)) for t in centre])
-        total = [jnp.zeros((8, 512), F32) for _ in range(3)]
-        for side in sides:
-            weight = 0.5 * (centre[3] + side[3])
+        for i, b in enumerate(bs):
+            z, q = b // 4, b % 4
+            x8 = pl.multiple_of(q * 8, 8)
+            tall = [padded[z + 1, c, pl.ds(x8, 24), :] for c in range(4)]
+            below = [padded[z, c, pl.ds(x8 + 8, 8), :] for c in range(4)]
+            above = [padded[z + 2, c, pl.ds(x8 + 8, 8), :] for c in range(4)]
+            centre = [t[8:16] for t in tall]
+            sides = [above, below, [t[9:17] for t in tall], [t[7:15] for t in tall]]
+            sides.append([jnp.where(y_iota == 511, 0.0, pltpu.roll(t, 511, 1)) for t in centre])
+            sides.append([jnp.where(y_iota == 0, 0.0, pltpu.roll(t, 1, 1)) for t in centre])
+            total = [jnp.zeros((8, 512), F32) for _ in range(3)]
+            for side in sides:
+                weight = 0.5 * (centre[3] + side[3])
+                for c in range(3):
+                    total[c] = total[c] + weight * (side[c] - centre[c])
+            summed = deposit[i, 0:48, :] + (deposit[i, 48:96, :] + deposit[i, 96:144, :])
             for c in range(3):
-                total[c] = total[c] + weight * (side[c] - centre[c])
-        summed = deposit[0:48, :] + (deposit[48:96, :] + deposit[96:144, :])
-        for c in range(3):
-            left, right = summed[c * 16 : c * 16 + 8], summed[c * 16 + 8 : c * 16 + 16]
-            net_ref[z, c, pl.ds(x8, 8), :] = total[c] - jnp.concatenate([left, right], axis=1)
+                left, right = summed[c * 16 : c * 16 + 8], summed[c * 16 + 8 : c * 16 + 16]
+                net_ref[z, c, pl.ds(x8, 8), :] = total[c] - jnp.concatenate([left, right], axis=1)
         return carry
 
-    lax.fori_loop(0, 32, block, 0)
+    lax.fori_loop(0, 32 // group, blocks, 0)
 
 
 def per_device(
@@ -301,7 +336,7 @@
     params = pltpu.CompilerParams(vmem_limit_bytes=40 << 20)
 
     arrived, bricks, zhalo = pl.pallas_call(
-        functools.partial(exchange_kernel, cap=cap, group=4),
+        functools.partial(exchange_kernel, cap=cap, group=8),
         out_shape=(
             jax.ShapeDtypeStruct((devices, 8, 128), F32),
             jax.ShapeDtypeStruct((8, 136, 512), F32),
@@ -350,7 +385,7 @@
         (key.reshape(-1), flat[3], flat[0], flat[1], flat[2]), num_keys=1, is_stable=False
     )
     force, slot, net = pl.pallas_call(
-        functools.partial(brick_kernel, width=256),
+        functools.partial(brick_kernel, width=256, group=8),
         out_shape=(
             jax.ShapeDtypeStruct((3, 256, 128), F32),
             jax.ShapeDtypeStruct((256, 128), I32),
@@ -360,8 +395,8 @@
         out_specs=(vmem, vmem, vmem),
         scratch_shapes=[
             pltpu.VMEM((10, 4, 48, 512), F32),
-            pltpu.VMEM((192, 256), F32),
-            pltpu.VMEM((144, 256), F32),
+            pltpu.VMEM((8, 192, 256), BF16),
+            pltpu.VMEM((8, 144, 256), F32),
         ],
         compiler_params=params,
         name="brick_forces",

time: 177 us -> 139 us (0.79)
  starting transfers between devices: 41 us -> 12 us
  Pallas kernels: 76.3 us -> 67.5 us
    all_to_all x1, starting transfers between devices: 41 us -> 12 us  [per_device(): lax.all_to_all(net, 'brick', split_axis=0, concat_axis=0, tiled=True)]
    pallas_call x2, Pallas kernels: 74.6 us -> 65.8 us  [the longest x1 56.4 us: per_device(): pl.pallas_call(functools.partial(exchange_kernel, cap=cap, group=8), out_...]
  transfers between devices with their start and end apart: 1 -> 1, of which waited for: 1 -> 1; matrix products, arithmetic and copies ran while one was open for 10% -> 13% of each run, Pallas kernels for 0% -> 0%
where the time goes in v3:
time: 139 us; the launch traced here: 138 us
  Pallas kernels  67.5 us (49%)
  other arithmetic  43.7 us (31%)
  starting transfers between devices  12 us (9%)
  local copies, waits for them, and re-layouts  11.7 us (8%)
  waiting for transfers between devices  2.66 us (2%)
    pallas_call x1, Pallas kernels, per_device(): pl.pallas_call(functools.partial(exchange_kernel, cap=cap, group=8), out_...  56.4 us
    sort x1, other arithmetic, per_device(): lax.sort((key.reshape(-1), flat[3], flat[0], flat[1], flat[2]), num_keys=...  24.1 us
    sort x1, other arithmetic, per_device(): lax.sort((slot.reshape(-1), flat[0], flat[1], flat[2]), num_keys=1, is_st...  16.6 us
    all_to_all x1, starting transfers between devices, per_device(): lax.all_to_all(net, 'brick', split_axis=0, concat_axis=0, tiled=True)  12 us
    unnamed x27, local copies, waits for them, and re-layouts  10.8 us
    pallas_call x1, Pallas kernels, per_device(): pl.pallas_call(functools.partial(brick_kernel, width=256, group=8), out_s...  9.43 us
  transfers between devices with their start and end apart: 1, of which 1 were waited for; matrix products, arithmetic and copies ran while one was open for 13% of the time, Pallas kernels for 0%

profile of v3, /device:TPU:8, one launch (start us, length us, event | category | flops | bytes accessed | tf_op | source)
XLA Modules:
  0.0 138.3 jit_solution(7252615280616802713)
XLA Ops:
  0.6 0.0 copy-start.5
  0.6 1.0 copy.14
  1.6 0.0 copy-start
  1.7 1.4 %copy-done = f32[3,1,256,512]{3,2,1,0:T(8,128)S(1)} copy-done((f32[3,1,256,512]{3,2,1,0:T(8,128)S(1)}, f32[3,1,256,512]{3,2,1,0:T(8,128)}, u32[]{:S(2)}) %copy-start) | copy-done | bytes 1572888
  3.1 0.0 copy-start.2
  3.1 1.0 copy-done.2
  4.1 0.9 copy-done.10
  5.0 0.8 copy-done.11
  5.8 0.7 copy-done.12
  6.5 56.4 %exchange.1 = (f32[128,8,128]{2,1,0:T(8,128)S(1)}, f32[8,136,512]{2,1,0:T(8,128)S(1)}, f32[2,128,512]{2,1,0:T(8,128)S(1)}) custom-call(s32[128]{0:T(128)S(1)} %copy-done.12, f32[3,128,128]{2,1,0:T(8,128)S(1)} %bitcast.45, f32[128,128]{1,0:T(8,128)S(1)} %bitcast.55, s32[256,128]{1,0:T(8,128)S(1)} %bitcast.54, f32[3,256,512]{2,1,0:T(8,128)S(1)} %bitcast.42, ...), custom_call_target="tpu_custom_call" | custom-call | tf_op jit(solution)/shard_map/exchange/pallas_call | solution.py:338
  62.9 0.0 copy-done.5
  62.9 1.7 %block_keys.1 = (s32[256,128]{1,0:T(8,128)S(1)}, f32[4,256,128]{2,1,0:T(8,128)S(1)}, s32[33]{0:T(128)S(1)}) custom-call(f32[128,8,128]{2,1,0:T(8,128)S(1)} %get-tuple-element.19.arrived_ref, s32[256,128]{1,0:T(8,128)S(1)} %bitcast.46), custom_call_target="tpu_custom_call" | custom-call | tf_op jit(solution)/shard_map/block_keys/pallas_call | solution.py:371
  64.6 0.7 slice_bitcast_fusion.3
  65.4 24.1 %sort.60 = (s32[32768]{0:T(1024)S(1)}, f32[32768]{0:T(1024)S(1)}, f32[32768]{0:T(1024)S(1)}, f32[32768]{0:T(1024)}, f32[32768]{0:T(1024)}) sort(s32[32768]{0:T(1024)S(1)} %bitcast.52, f32[32768]{0:T(1024)} %get-tuple-element.41, f32[32768]{0:T(1024)} %get-tuple-element.40, f32[32768]{0:T(1024)S(1)} %get-tuple-element.39, f32[32768]{0:T(1024)S(1)} %get-tuple-element.38), dimensions={0}, to_apply=%region_0.0 | sort | flops 491520 | bytes 1310720 | tf_op jit(solution)/shard_map/sort | solution.py:384
  89.4 0.9 copy-done.6
  90.4 0.9 copy-done.7
  91.3 9.4 %brick_forces.1 = (f32[3,256,128]{2,1,0:T(8,128)S(1)}, s32[256,128]{1,0:T(8,128)S(1)}, f32[8,3,32,512]{3,2,1,0:T(8,128)S(1)}) custom-call(s32[33]{0:T(128)S(1)} %get-tuple-element.20.starts_ref, s32[256,128]{1,0:T(8,128)S(1)} %bitcast.47, f32[256,128]{1,0:T(8,128)S(1)} %bitcast.48, f32[256,128]{1,0:T(8,128)S(1)} %bitcast.49, f32[256,128]{1,0:T(8,128)S(1)} %bitcast.50, ...), custom_call_target="tpu_custom_call" | custom-call | tf_op jit(solution)/shard_map/brick_forces/pallas_call | solution.py:387
  100.7 0.0 copy-start.4
  100.7 1.1 copy-done.4
  101.8 0.7 copy-done.8
  102.5 12.0 %all-to-all-start = ((f32[8,3,32,512]{3,2,1,0:T(8,128)}), f32[8,3,32,512]{3,2,1,0:T(8,128)S(1)}, u32[]{:S(2)}, u32[]{:S(2)}) async-start(f32[8,3,32,512]{3,2,1,0:T(8,128)} %copy-done.4), calls=%async_computation | async-start | bytes 3145728 | tf_op jit(solution)/shard_map/all_to_all | solution.py:405
  114.5 0.0 copy-done.9
  114.5 16.6 %sort.61 = (s32[32768]{0:T(1024)}, f32[32768]{0:T(1024)S(1)}, f32[32768]{0:T(1024)S(1)}, f32[32768]{0:T(1024)S(1)}) sort(s32[32768]{0:T(1024)S(1)} %bitcast.53, f32[32768]{0:T(1024)S(1)} %get-tuple-element.44, f32[32768]{0:T(1024)S(1)} %get-tuple-element.43, f32[32768]{0:T(1024)S(1)} %get-tuple-element.42), dimensions={0}, to_apply=%region_1.0 | sort | flops 491520 | bytes 1048576 | tf_op jit(solution)/shard_map/sort | solution.py:407
  131.1 1.1 pad_maximum_fusion
  132.3 2.7 %all-to-all-done = f32[8,3,32,512]{3,2,1,0:T(8,128)S(1)} async-done(((f32[8,3,32,512]{3,2,1,0:T(8,128)}), f32[8,3,32,512]{3,2,1,0:T(8,128)S(1)}, u32[]{:S(2)}, u32[]{:S(2)}) %all-to-all-start) | async-done | bytes 1572896 | tf_op jit(solution)/shard_map/all_to_all | solution.py:405
  134.9 0.3 multiply_bitcast_fusion
  135.2 0.0 copy-start.1
  135.2 0.0 copy-start.3
  135.2 0.1 copy.9
  135.3 1.3 copy-done.1
  136.6 0.1 copy-done.3
  136.7 1.6 %fusion = f32[3,1,256,512]{3,2,0,1:T(8,128)} fusion(f32[3,8,32,512]{3,2,1,0:T(8,128)S(1)} %copy.9, f32[3,1,256,512]{3,2,1,0:T(8,128)S(1)} %copy-done.1, f32[256,512]{1,0:T(8,128)S(1)} %bitcast.44), kind=kLoop, calls=%fused_computation.1 | loop fusion | flops 786432 | bytes 5242880 | tf_op jit(solution)/shard_map/add | solution.py:410
  (8 shorter events, 0.0 us)
Async XLA Ops:
  0.6 62.2 %copy-start.5 = (s32[32768]{0:T(1024)S(1)}, s32[32768]{0:T(1024)}, u32[]{:S(2)}) copy-start(s32[32768]{0:T(1024)} %param.13) | copy-start | bytes 393220
  1.6 1.4 %copy-start = (f32[3,1,256,512]{3,2,1,0:T(8,128)S(1)}, f32[3,1,256,512]{3,2,1,0:T(8,128)}, u32[]{:S(2)}) copy-start(f32[3,1,256,512]{3,2,1,0:T(8,128)} %param.7) | copy-start | bytes 4718596
  3.1 1.0 copy-start.2
  4.1 0.9 copy-start.10
  5.0 0.8 copy-start.11
  5.8 0.7 copy-start.12
  89.4 0.9 copy-start.6
  90.3 0.9 copy-start.7
  100.7 1.1 copy-start.4
  101.8 0.7 copy-start.8
  102.5 12.0 %copy-start.9 = (s32[256,128]{1,0:T(8,128)S(1)}, s32[256,128]{1,0:T(8,128)}, u32[]{:S(2)}) copy-start(s32[256,128]{1,0:T(8,128)} %copy-done.8) | copy-start | bytes 393220
  102.5 32.4 %all-to-all-start = ((f32[8,3,32,512]{3,2,1,0:T(8,128)}), f32[8,3,32,512]{3,2,1,0:T(8,128)S(1)}, u32[]{:S(2)}, u32[]{:S(2)}) async-start(f32[8,3,32,512]{3,2,1,0:T(8,128)} %copy-done.4), calls=%async_computation | async-start | bytes 3145728 | tf_op jit(solution)/shard_map/all_to_all | solution.py:405
  135.2 1.4 %copy-start.1 = (f32[3,1,256,512]{3,2,1,0:T(8,128)S(1)}, f32[3,1,256,512]{3,2,1,0:T(8,128)}, u32[]{:S(2)}) copy-start(f32[3,1,256,512]{3,2,1,0:T(8,128)} %param.7) | copy-start | bytes 4718596
  135.2 1.5 %copy-start.3 = (f32[1,256,512]{2,1,0:T(8,128)S(1)}, f32[1,256,512]{2,1,0:T(8,128)}, u32[]{:S(2)}) copy-start(f32[1,256,512]{2,1,0:T(8,128)} %param.8) | copy-start | bytes 1572868

commit v4 on v3

--- a/solution.py
+++ b/solution.py
@@ -21,8 +21,8 @@
 
 
 def exchange_kernel(
-    counts_ref, pv_ref, coef_ref, rows_ref, u_ref, frac_ref, arrived_ref, bricks_ref, zhalo_ref,
-    table, packed, stage, fluid_send, fluid_recv, part_send, part_recv, halo_send, halo_recv, *, cap, group,
+    counts_ref, pv_ref, coef_ref, rows_ref, u_ref, frac_ref, arrived_ref, stage,
+    table, packed, part_send, part_recv, *, cap, group,
 ):
     n_slab, n_brick = lax.axis_size("slab"), lax.axis_size("brick")
     devices = n_slab * n_brick
@@ -57,17 +57,6 @@
             table[p * 256 + c * 64 : p * 256 + (c + 1) * 64, :] = piece
 
     pl.semaphore_wait(barrier, devices - 1)
-
-    def chunk(j):
-        to = (brick + j) % n_brick
-        return pltpu.make_async_remote_copy(
-            src_ref=stage.at[to], dst_ref=bricks_ref.at[brick], send_sem=fluid_send.at[to],
-            recv_sem=fluid_recv.at[brick], device_id=(slab, to), device_id_type=mesh_id,
-        )
-
-    for j in range(1, 8):
-        chunk(j).start()
-    bricks_ref[brick] = stage[brick]
 
     r_iota = lax.broadcasted_iota(I32, (256, cap), 0).astype(F32).astype(BF16)
     one, zero = jnp.ones((), BF16), jnp.zeros((), BF16)
@@ -123,55 +112,12 @@
     for t in to[:-1]:
         parcel(t).start()
 
-    for j in range(1, 8):
-        source = (brick + j) % n_brick
-        pltpu.make_async_remote_copy(
-            src_ref=stage.at[source], dst_ref=bricks_ref.at[source], send_sem=fluid_send.at[source],
-            recv_sem=fluid_recv.at[source], device_id=(slab, source), device_id_type=mesh_id,
-        ).wait_recv()
-
-    def halo(i, to):
-        return pltpu.make_async_remote_copy(
-            src_ref=bricks_ref.at[7 - 7 * i, pl.ds(0, 128)], dst_ref=zhalo_ref.at[i], send_sem=halo_send.at[i],
-            recv_sem=halo_recv.at[i], device_id=(to, brick), device_id_type=mesh_id,
-        )
-
-    up, down = slab < n_slab - 1, slab > 0
-
-    @pl.when(up)
-    def _():
-        halo(0, slab + 1).start()
-
-    @pl.when(down)
-    def _():
-        halo(1, slab - 1).start()
-
-    @pl.when(jnp.logical_not(up))
-    def _():
-        zhalo_ref[1] = jnp.zeros((128, 512), F32)
-
-    @pl.when(jnp.logical_not(down))
-    def _():
-        zhalo_ref[0] = jnp.zeros((128, 512), F32)
-
-    for j in range(1, 8):
-        chunk(j).wait_send()
     rest = pltpu.make_async_remote_copy(
         src_ref=packed.at[pl.ds(0, devices - 1)], dst_ref=arrived_ref.at[pl.ds(0, devices - 1)],
         send_sem=part_send, recv_sem=part_recv, device_id=coords((me + 1) % devices), device_id_type=mesh_id,
     )
     rest.wait_send()
     rest.wait_recv()
-
-    @pl.when(up)
-    def _():
-        halo(0, slab + 1).wait_send()
-        halo(1, slab + 1).wait_recv()
-
-    @pl.when(down)
-    def _():
-        halo(1, slab - 1).wait_send()
-        halo(0, slab - 1).wait_recv()
 
 
 def key_kernel(arrived_ref, cell_ref, key_ref, data_ref, starts_ref):
@@ -202,7 +148,7 @@
 
 
 def brick_kernel(
-    starts_ref, key_ref, coef_ref, p0_ref, p1_ref, p2_ref, bricks_ref, zhalo_ref,
+    starts_ref, key_ref, coef_ref, p0_ref, p1_ref, p2_ref, bricks_ref,
     force_ref, slot_ref, net_ref, padded, table, deposit, *, width, group,
 ):
     rows = key_ref.shape[0]
@@ -215,8 +161,8 @@
             padded[z + 1, c, 8:40, :] = bricks_ref[z, own, :]
             padded[z + 1, c, 7:8, :] = bricks_ref[z, 128 + c : 129 + c, :]
             padded[z + 1, c, 40:41, :] = bricks_ref[z, 132 + c : 133 + c, :]
-        padded[0, c, 8:40, :] = zhalo_ref[0, own, :]
-        padded[9, c, 8:40, :] = zhalo_ref[1, own, :]
+        padded[0, c, 8:40, :] = bricks_ref[0, own, :]
+        padded[9, c, 8:40, :] = bricks_ref[7, own, :]
 
     r_iota = lax.broadcasted_iota(I32, (256, width), 0)
     l_iota = lax.broadcasted_iota(I32, (16, width), 0)
@@ -335,25 +281,24 @@
     smem = pl.BlockSpec(memory_space=pltpu.SMEM)
     params = pltpu.CompilerParams(vmem_limit_bytes=40 << 20)
 
-    arrived, bricks, zhalo = pl.pallas_call(
+    ends = [(d, d + 1) for d in range(n_brick - 1, devices - 1, n_brick)]
+    ends += [(target, source) for source, target in ends]
+    next_velocity = lax.ppermute(fluid_velocity, ("slab", "brick"), ends)
+    next_porosity = lax.ppermute(porosity, ("slab", "brick"), ends)
+
+    arrived, staged = pl.pallas_call(
         functools.partial(exchange_kernel, cap=cap, group=8),
         out_shape=(
             jax.ShapeDtypeStruct((devices, 8, 128), F32),
             jax.ShapeDtypeStruct((8, 136, 512), F32),
-            jax.ShapeDtypeStruct((2, 128, 512), F32),
         ),
         in_specs=[smem] + [vmem] * 5,
-        out_specs=(vmem, vmem, vmem),
+        out_specs=(vmem, vmem),
         scratch_shapes=[
             pltpu.VMEM((768, 256), BF16),
             pltpu.VMEM((devices, 8, 128), F32),
-            pltpu.VMEM((8, 136, 512), F32),
-            pltpu.SemaphoreType.DMA((8,)),
-            pltpu.SemaphoreType.DMA((8,)),
             pltpu.SemaphoreType.DMA,
             pltpu.SemaphoreType.DMA,
-            pltpu.SemaphoreType.DMA((2,)),
-            pltpu.SemaphoreType.DMA((2,)),
         ],
         compiler_params=pltpu.CompilerParams(
             vmem_limit_bytes=40 << 20, collective_id=0, has_side_effects=True
@@ -367,6 +312,8 @@
         fluid_velocity.reshape(3, 256, 512),
         porosity.reshape(256, 512),
     )
+
+    bricks = lax.all_to_all(staged, "brick", split_axis=0, concat_axis=0, tiled=True)
 
     key, data, starts = pl.pallas_call(
         key_kernel,
@@ -391,7 +338,7 @@
             jax.ShapeDtypeStruct((256, 128), I32),
             jax.ShapeDtypeStruct((8, 3, 32, 512), F32),
         ),
-        in_specs=[smem] + [vmem] * 7,
+        in_specs=[smem] + [vmem] * 6,
         out_specs=(vmem, vmem, vmem),
         scratch_shapes=[
             pltpu.VMEM((10, 4, 48, 512), F32),
@@ -400,14 +347,17 @@
         ],
         compiler_params=params,
         name="brick_forces",
-    )(starts, *[part.reshape(256, 128) for part in ordered], bricks, zhalo)
+    )(starts, *[part.reshape(256, 128) for part in ordered], bricks)
 
     returned = lax.all_to_all(net, "brick", split_axis=0, concat_axis=0, tiled=True)
     flat = force.reshape(3, -1)
     back = lax.sort((slot.reshape(-1), flat[0], flat[1], flat[2]), num_keys=1, is_stable=False)
     slot_force = jnp.stack(back[1:])
     returned = jnp.swapaxes(returned, 0, 1).reshape(fluid_velocity.shape)
-    new_velocity = fluid_velocity + time_step * returned / porosity
+    brick = lax.axis_index("brick")
+    face = 0.5 * (porosity + next_porosity) * (next_velocity - fluid_velocity)
+    face = jnp.where((brick == 0) | (brick == n_brick - 1), face, 0.0)
+    new_velocity = fluid_velocity + time_step * (returned + face) / porosity
     return (new_velocity, slot_force)
 
 

time: 139 us -> 150 us (1.079)
  waiting for transfers between devices: 2.66 us -> 25 us
  Pallas kernels: 67.5 us -> 45.7 us
  starting transfers between devices: 12 us -> 18.8 us
  other arithmetic: 43.7 us -> 46.5 us
    pallas_call x1, Pallas kernels: 56.4 us -> 30.8 us  [per_device(): pl.pallas_call(functools.partial(exchange_kernel, cap=cap, group=8), out_...]
    ppermute x0 -> x2, waiting for transfers between devices: none -> 20.7 us  [the longest x1 20.7 us: per_device(): next_porosity = lax.ppermute(porosity, ('slab', 'brick'), ends)]
    ppermute x0 -> x2, starting transfers between devices: none -> 9.97 us  [the longest x1 7.39 us: per_device(): next_porosity = lax.ppermute(porosity, ('slab', 'brick'), ends)]
    all_to_all x1, starting transfers between devices: 12 us -> 3.59 us  [per_device(): lax.all_to_all(net, 'brick', split_axis=0, concat_axis=0, tiled=True)]
    all_to_all x0 -> x1, starting transfers between devices: none -> 5.22 us  [per_device(): lax.all_to_all(staged, 'brick', split_axis=0, concat_axis=0, tiled=True)]
    pallas_call x1, Pallas kernels: 9.43 us -> 13.2 us  [per_device(): pl.pallas_call(functools.partial(brick_kernel, width=256, group=8), out_s...]
    all_to_all x1, waiting for transfers between devices: 2.66 us -> 4.38 us  [per_device(): lax.all_to_all(net, 'brick', split_axis=0, concat_axis=0, tiled=True)]
    mul x1, other arithmetic: 0.25 us -> 1.92 us  [per_device(): face = 0.5 * (porosity + next_porosity) * (next_velocity - fluid_velocity)]
  transfers between devices with their start and end apart: 1 -> 4, of which waited for: 1 -> 2; matrix products, arithmetic and copies ran while one was open for 13% -> 30% of each run, Pallas kernels for 0% -> 10%
where the time goes in v4:
time: 150 us; the launch traced here: 149 us
  other arithmetic  46.5 us (31%)
  Pallas kernels  45.7 us (30%)
  waiting for transfers between devices  25 us (17%)
  starting transfers between devices  18.8 us (13%)
  local copies, waits for them, and re-layouts  12.5 us (8%)
    pallas_call x1, Pallas kernels, per_device(): pl.pallas_call(functools.partial(exchange_kernel, cap=cap, group=8), out_...  30.8 us
    sort x1, other arithmetic, per_device(): lax.sort((key.reshape(-1), flat[3], flat[0], flat[1], flat[2]), num_keys=...  23.5 us
    ppermute x1, waiting for transfers between devices, per_device(): next_porosity = lax.ppermute(porosity, ('slab', 'brick'), ends)  20.7 us
    sort x1, other arithmetic, per_device(): lax.sort((slot.reshape(-1), flat[0], flat[1], flat[2]), num_keys=1, is_st...  16.6 us
    pallas_call x1, Pallas kernels, per_device(): pl.pallas_call(functools.partial(brick_kernel, width=256, group=8), out_s...  13.2 us
    unnamed x25, local copies, waits for them, and re-layouts  10.4 us
    ppermute x1, starting transfers between devices, per_device(): next_porosity = lax.ppermute(porosity, ('slab', 'brick'), ends)  7.39 us
    all_to_all x1, starting transfers between devices, per_device(): lax.all_to_all(staged, 'brick', split_axis=0, concat_axis=0, tiled=True)  5.22 us
  transfers between devices with their start and end apart: 4, of which 2 were waited for; matrix products, arithmetic and copies ran while one was open for 30% of the time, Pallas kernels for 10%

profile of v4, /device:TPU:8, one launch (start us, length us, event | category | flops | bytes accessed | tf_op | source)
XLA Modules:
  0.0 149.3 jit_solution(6446346880118229659)
XLA Ops:
  0.6 1.0 copy.16
  1.6 0.0 copy-start
  1.6 1.4 copy-done
  3.0 1.0 copy-done.2
  4.1 0.9 copy-done.8
  5.0 0.8 copy-done.9
  5.8 0.7 copy-done.10
  6.5 30.8 %exchange.1 = (f32[128,8,128]{2,1,0:T(8,128)S(1)}, f32[8,136,512]{2,1,0:T(8,128)S(1)}) custom-call(s32[128]{0:T(128)S(1)} %copy-done.10, f32[3,128,128]{2,1,0:T(8,128)S(1)} %bitcast.51, f32[128,128]{1,0:T(8,128)S(1)} %bitcast.61, s32[256,128]{1,0:T(8,128)S(1)} %bitcast.60, f32[3,256,512]{2,1,0:T(8,128)S(1)} %bitcast.48, f32[256,512]{1,0:T(8,128)S(1)} %bitcast.49), custom_call_target="tpu_custom_call" | custom-call | tf_op jit(solution)/shard_map/exchange/pallas_call | solution.py:289
  37.3 1.4 copy-done.4
  38.6 5.2 %all-to-all-start = ((f32[8,136,512]{2,1,0:T(8,128)}), f32[8,136,512]{2,1,0:T(8,128)S(1)}, u32[]{:S(2)}, u32[]{:S(2)}) async-start(f32[8,136,512]{2,1,0:T(8,128)} %copy-done.4), calls=%async_computation | async-start | bytes 4456448 | tf_op jit(solution)/shard_map/all_to_all | solution.py:316
  43.9 7.4 %collective-permute-start = (f32[1,256,512]{2,1,0:T(8,128)S(1)}, f32[1,256,512]{2,1,0:T(8,128)}, u32[]{:S(2)}, u32[]{:S(2)}) collective-permute-start(f32[1,256,512]{2,1,0:T(8,128)S(1)} %copy-done.3), channel_id=1, source_target_pairs={{7,8},{15,16},{23,24},{31,32},{39,40},{47,48},{55,56},{63,64},{71,... | collective-permute-start | bytes 1572872 | tf_op jit(solution)/shard_map/ppermute | solution.py:287
  51.3 2.6 %collective-permute-start.1 = (f32[3,1,256,512]{3,2,0,1:T(8,128)}, f32[3,1,256,512]{3,2,0,1:T(8,128)}, u32[]{:S(2)}, u32[]{:S(2)}) collective-permute-start(f32[3,1,256,512]{3,2,0,1:T(8,128)} %bitcast.47), channel_id=1, source_target_pairs={{7,8},{15,16},{23,24},{31,32},{39,40},{47,48},{55,56},{63,64},{71,... | collective-permute-start | bytes 4718600 | tf_op jit(solution)/shard_map/ppermute | solution.py:286
  53.9 1.7 %block_keys.1 = (s32[256,128]{1,0:T(8,128)S(1)}, f32[4,256,128]{2,1,0:T(8,128)S(1)}, s32[33]{0:T(128)S(1)}) custom-call(f32[128,8,128]{2,1,0:T(8,128)S(1)} %get-tuple-element.18.arrived_ref, s32[256,128]{1,0:T(8,128)S(1)} %bitcast.52), custom_call_target="tpu_custom_call" | custom-call | tf_op jit(solution)/shard_map/block_keys/pallas_call | solution.py:318
  55.6 0.0 copy-start.6
  55.6 0.8 copy-done.6
  56.4 1.9 %slice_bitcast_fusion.3 = (f32[32768]{0:T(1024)}, f32[32768]{0:T(1024)}, f32[32768]{0:T(1024)}, f32[32768]{0:T(1024)}) fusion(f32[4,256,128]{2,1,0:T(8,128)} %copy-done.6), kind=kLoop, calls=%fused_computation.10 | loop fusion | bytes 1048576 | tf_op jit(solution)/shard_map/squeeze | solution.py:332
  58.3 23.5 %sort.60 = (s32[32768]{0:T(1024)S(1)}, f32[32768]{0:T(1024)S(1)}, f32[32768]{0:T(1024)S(1)}, f32[32768]{0:T(1024)S(1)}, f32[32768]{0:T(1024)S(1)}) sort(s32[32768]{0:T(1024)S(1)} %bitcast.58, f32[32768]{0:T(1024)} %get-tuple-element.39, f32[32768]{0:T(1024)} %get-tuple-element.38, f32[32768]{0:T(1024)} %get-tuple-element.37, f32[32768]{0:T(1024)} %get-tuple-element.36), dimensions={0}, to_apply=%region_0.0 | sort | flops 491520 | bytes 1310720 | tf_op jit(solution)/shard_map/sort | solution.py:331
  81.8 20.7 %collective-permute-done = f32[1,256,512]{2,1,0:T(8,128)} collective-permute-done((f32[1,256,512]{2,1,0:T(8,128)S(1)}, f32[1,256,512]{2,1,0:T(8,128)}, u32[]{:S(2)}, u32[]{:S(2)}) %collective-permute-start) | collective-permute-done | bytes 524320 | tf_op jit(solution)/shard_map/ppermute | solution.py:287
  102.5 1.9 %multiply_bitcast_fusion = f32[256,512]{1,0:T(8,128)} fusion(f32[1,256,512]{2,1,0:T(8,128)S(1)} %copy-done.3, f32[1,256,512]{2,1,0:T(8,128)} %collective-permute-done), kind=kLoop, calls=%fused_computation.5 | loop fusion | flops 262144 | bytes 1572864 | tf_op jit(solution)/shard_map/mul | solution.py:358
  104.4 0.0 all-to-all-done.bricks_ref
  104.4 13.2 %brick_forces.1 = (f32[3,256,128]{2,1,0:T(8,128)S(1)}, s32[256,128]{1,0:T(8,128)S(1)}, f32[8,3,32,512]{3,2,1,0:T(8,128)S(1)}) custom-call(s32[33]{0:T(128)S(1)} %get-tuple-element.19.starts_ref, s32[256,128]{1,0:T(8,128)S(1)} %bitcast.53, f32[256,128]{1,0:T(8,128)S(1)} %bitcast.54, f32[256,128]{1,0:T(8,128)S(1)} %bitcast.55, f32[256,128]{1,0:T(8,128)S(1)} %bitcast.56, ...), custom_call_target="tpu_custom_call" | custom-call | tf_op jit(solution)/shard_map/brick_forces/pallas_call | solution.py:334
  117.6 0.0 copy-start.5
  117.6 1.1 copy-done.5
  118.7 3.6 %all-to-all-start.1 = ((f32[8,3,32,512]{3,2,1,0:T(8,128)}), f32[8,3,32,512]{3,2,1,0:T(8,128)S(1)}, u32[]{:S(2)}, u32[]{:S(2)}) async-start(f32[8,3,32,512]{3,2,1,0:T(8,128)} %copy-done.5), calls=%async_computation.1 | async-start | bytes 3145728 | tf_op jit(solution)/shard_map/all_to_all | solution.py:352
  122.3 16.6 %sort.61 = (s32[32768]{0:T(1024)}, f32[32768]{0:T(1024)S(1)}, f32[32768]{0:T(1024)S(1)}, f32[32768]{0:T(1024)S(1)}) sort(s32[32768]{0:T(1024)S(1)} %bitcast.59, f32[32768]{0:T(1024)S(1)} %get-tuple-element.42, f32[32768]{0:T(1024)S(1)} %get-tuple-element.41, f32[32768]{0:T(1024)S(1)} %get-tuple-element.40), dimensions={0}, to_apply=%region_1.0 | sort | flops 491520 | bytes 1048576 | tf_op jit(solution)/shard_map/sort | solution.py:354
  139.0 1.1 pad_maximum_fusion
  140.1 4.4 %all-to-all-done.1 = f32[8,3,32,512]{3,2,1,0:T(8,128)S(1)} async-done(((f32[8,3,32,512]{3,2,1,0:T(8,128)}), f32[8,3,32,512]{3,2,1,0:T(8,128)S(1)}, u32[]{:S(2)}, u32[]{:S(2)}) %all-to-all-start.1) | async-done | bytes 1572896 | tf_op jit(solution)/shard_map/all_to_all | solution.py:352
  144.5 0.2 copy.9
  144.7 0.0 collective-permute-done.1
  144.7 1.2 copy-done.1
  145.9 0.1 copy-done.11
  146.0 3.2 %fusion.2 = f32[3,1,256,512]{3,2,0,1:T(8,128)} fusion(f32[3,8,32,512]{3,2,1,0:T(8,128)S(1)} %copy.9, f32[3,1,256,512]{3,2,0,1:T(8,128)} %collective-permute-done.1, f32[256,512]{1,0:T(8,128)S(1)} %bitcast.50, f32[256,512]{1,0:T(8,128)S(1)} %copy-done.11, pred[]{:T(512)S(6)} %or.3, f32[3,1,256,512]{3,2,1,0:T(8,128)S(1)} %copy-done.1), kind=kLoop, calls=%fused_computation.3 | loop fusion | flops 2752512 | bytes 7340033 | tf_op jit(solution)/shard_map/add | solution.py:360
  (12 shorter events, 0.0 us)
Async XLA Ops:
  1.6 1.4 copy-start
  3.0 1.0 copy-start.2
  4.0 0.9 copy-start.8
  5.0 0.8 copy-start.9
  5.8 0.7 copy-start.10
  37.3 1.4 copy-start.4
  38.6 5.2 %copy-start.3 = (f32[1,256,512]{2,1,0:T(8,128)S(1)}, f32[1,256,512]{2,1,0:T(8,128)}, u32[]{:S(2)}) copy-start(f32[1,256,512]{2,1,0:T(8,128)} %param.8) | copy-start | bytes 1572868
  38.6 15.2 %copy-start.7 = (s32[32768]{0:T(1024)S(1)}, s32[32768]{0:T(1024)}, u32[]{:S(2)}) copy-start(s32[32768]{0:T(1024)} %param.13) | copy-start | bytes 393220
  38.6 65.8 %all-to-all-start = ((f32[8,136,512]{2,1,0:T(8,128)}), f32[8,136,512]{2,1,0:T(8,128)S(1)}, u32[]{:S(2)}, u32[]{:S(2)}) async-start(f32[8,136,512]{2,1,0:T(8,128)} %copy-done.4), calls=%async_computation | async-start | bytes 4456448 | tf_op jit(solution)/shard_map/all_to_all | solution.py:316
  43.9 58.6 %collective-permute-start = (f32[1,256,512]{2,1,0:T(8,128)S(1)}, f32[1,256,512]{2,1,0:T(8,128)}, u32[]{:S(2)}, u32[]{:S(2)}) collective-permute-start(f32[1,256,512]{2,1,0:T(8,128)S(1)} %copy-done.3), channel_id=1, source_target_pairs={{7,8},{15,16},{23,24},{31,32},{39,40},{47,48},{55,56},{63,64},{71,... | collective-permute-start | bytes 1572872 | tf_op jit(solution)/shard_map/ppermute | solution.py:287
  51.3 93.4 %collective-permute-start.1 = (f32[3,1,256,512]{3,2,0,1:T(8,128)}, f32[3,1,256,512]{3,2,0,1:T(8,128)}, u32[]{:S(2)}, u32[]{:S(2)}) collective-permute-start(f32[3,1,256,512]{3,2,0,1:T(8,128)} %bitcast.47), channel_id=1, source_target_pairs={{7,8},{15,16},{23,24},{31,32},{39,40},{47,48},{55,56},{63,64},{71,... | collective-permute-start | bytes 4718600 | tf_op jit(solution)/shard_map/ppermute | solution.py:286
  55.6 0.8 copy-start.6
  117.6 1.1 copy-start.5
  118.7 25.8 %all-to-all-start.1 = ((f32[8,3,32,512]{3,2,1,0:T(8,128)}), f32[8,3,32,512]{3,2,1,0:T(8,128)S(1)}, u32[]{:S(2)}, u32[]{:S(2)}) async-start(f32[8,3,32,512]{3,2,1,0:T(8,128)} %copy-done.5), calls=%async_computation.1 | async-start | bytes 3145728 | tf_op jit(solution)/shard_map/all_to_all | solution.py:352
  144.5 1.4 copy-start.1
  144.5 1.5 %copy-start.11 = (f32[256,512]{1,0:T(8,128)S(1)}, f32[256,512]{1,0:T(8,128)}, u32[]{:S(2)}) copy-start(f32[256,512]{1,0:T(8,128)} %multiply_bitcast_fusion) | copy-start | bytes 1572868

commit v5 on v4

--- a/solution.py
+++ b/solution.py
@@ -21,9 +21,18 @@
 
 
 def exchange_kernel(
-    counts_ref, pv_ref, coef_ref, rows_ref, u_ref, frac_ref, arrived_ref, stage,
-    table, packed, part_send, part_recv, *, cap, group,
+    counts_ref, pv_hbm, coef_hbm, rows_hbm, u_hbm, frac_hbm, cell_hbm,
+    stage_hbm, starts_ref, key_ref, p0_ref, p1_ref, p2_ref, drag_ref,
+    pv_ref, coef_ref, rows_ref, u_ref, frac_ref, cell_ref, particles,
+    stage, table, packed, arrived_ref, load_sem, stage_sem, part_send, part_recv, *, cap, group,
 ):
+    pairs = (
+        (u_hbm, u_ref), (frac_hbm, frac_ref), (pv_hbm, pv_ref), (coef_hbm, coef_ref), (rows_hbm, rows_ref),
+        (cell_hbm, cell_ref),
+    )
+    loads = [pltpu.make_async_copy(source, target, load_sem.at[i]) for i, (source, target) in enumerate(pairs)]
+    for load in loads:
+        load.start()
     n_slab, n_brick = lax.axis_size("slab"), lax.axis_size("brick")
     devices = n_slab * n_brick
     slab, brick = lax.axis_index("slab"), lax.axis_index("brick")
@@ -41,6 +50,8 @@
 
     lax.fori_loop(1, devices, greet, 0)
 
+    loads[0].wait()
+    loads[1].wait()
     for c in range(4):
         for b in range(8):
             field = frac_ref[b * 32 : (b + 1) * 32, :] if c == 3 else u_ref[c, b * 32 : (b + 1) * 32, :]
@@ -51,7 +62,16 @@
                 stage[b - 1, 132 + c : 133 + c, :] = field[0:1]
         stage[0, 128 + c : 129 + c, :] = jnp.zeros((1, 512), F32)
         stage[7, 132 + c : 133 + c, :] = jnp.zeros((1, 512), F32)
-        whole = coef_ref[...] if c == 3 else pv_ref[c]
+    saved = pltpu.make_async_copy(stage, stage_hbm, stage_sem)
+    saved.start()
+    for load in loads[2:]:
+        load.wait()
+    for l in range(128):
+        part = pv_ref[:, l * 128 : (l + 1) * 128]
+        for c in range(3):
+            particles[c, l : l + 1, :] = part[c : c + 1]
+    for c in range(4):
+        whole = coef_ref[...] if c == 3 else particles[c]
         halves = jnp.concatenate([whole[:64], whole[64:]], axis=1)
         for p, piece in enumerate(split3(halves)):
             table[p * 256 + c * 64 : p * 256 + (c + 1) * 64, :] = piece
@@ -118,18 +138,17 @@
     )
     rest.wait_send()
     rest.wait_recv()
-
-
-def key_kernel(arrived_ref, cell_ref, key_ref, data_ref, starts_ref):
+    saved.wait()
+
     tiles = cell_ref.shape[0] // 8
     place = lax.broadcasted_iota(I32, (8, 128), 0) * 128 + lax.broadcasted_iota(I32, (8, 128), 1)
 
-    def one(j, sums):
+    def keys(j, sums):
         parts = [arrived_ref[4 * j + i] for i in range(4)]
         rows = pl.ds(pl.multiple_of(8 * j, 8), 8)
-        for c in range(4):
+        for c, ref in enumerate((p0_ref, p1_ref, p2_ref, drag_ref)):
             value = jnp.concatenate([part[2 * c : 2 * c + 2] for part in parts], axis=0)
-            data_ref[c, rows, :] = value
+            ref[rows, :] = value
         live = value != 0.0
         cell = cell_ref[rows, :]
         block = cell >> 12
@@ -139,8 +158,8 @@
         block = jnp.where(live, block, 32)
         return tuple(s + jnp.where(block < b + 1, 1, 0) for b, s in enumerate(sums))
 
-    sums = lax.fori_loop(0, tiles, one, tuple(jnp.zeros((8, 128), I32) for _ in range(32)))
-    tail = (cell_ref[tiles * 8 - 8 :, :] == 131071) & (data_ref[3, tiles * 8 - 8 :, :] != 0.0) & (place == 1023)
+    sums = lax.fori_loop(0, tiles, keys, tuple(jnp.zeros((8, 128), I32) for _ in range(32)))
+    tail = (cell_ref[tiles * 8 - 8 :, :] == 131071) & (drag_ref[tiles * 8 - 8 :, :] != 0.0) & (place == 1023)
     starts_ref[0] = 0
     for b in range(32):
         starts_ref[b + 1] = jnp.sum(sums[b])
@@ -148,12 +167,25 @@
 
 
 def brick_kernel(
-    starts_ref, key_ref, coef_ref, p0_ref, p1_ref, p2_ref, bricks_ref,
-    force_ref, slot_ref, net_ref, padded, table, deposit, *, width, group,
+    starts_ref, key_hbm, coef_hbm, p0_hbm, p1_hbm, p2_hbm, bricks_hbm,
+    f0_ref, f1_ref, f2_ref, slot_ref, net_hbm,
+    key_ref, coef_ref, p0_ref, p1_ref, p2_ref, bricks_ref, net_ref, padded, table, deposit, load_sem, net_sem,
+    *, width, group,
 ):
     rows = key_ref.shape[0]
     n = width // 128
-    force_ref[...] = jnp.zeros_like(force_ref)
+    pairs = (
+        (bricks_hbm, bricks_ref), (key_hbm, key_ref), (coef_hbm, coef_ref), (p0_hbm, p0_ref), (p1_hbm, p1_ref),
+        (p2_hbm, p2_ref),
+    )
+    loads = [pltpu.make_async_copy(source, target, load_sem.at[i]) for i, (source, target) in enumerate(pairs)]
+    for load in loads:
+        load.start()
+    force_refs = (f0_ref, f1_ref, f2_ref)
+    for ref in force_refs:
+        ref[...] = jnp.zeros_like(ref)
+    for load in loads:
+        load.wait()
     slot_ref[...] = jnp.where(coef_ref[...] != 0.0, (key_ref[...] >> 12) & 32767, p0_ref[...].astype(I32))
     for c in range(4):
         own = slice(c * 32, (c + 1) * 32)
@@ -241,7 +273,7 @@
             for i in range(group):
                 for c in range(3):
                     for k in range(n):
-                        force_ref[c, pl.ds(ats[i] + k, 1), :] += forces[i][c][:, k * 128 : (k + 1) * 128]
+                        force_refs[c][pl.ds(ats[i] + k, 1), :] += forces[i][c][:, k * 128 : (k + 1) * 128]
             return inner
 
         lax.fori_loop(0, windows, window, 0)
@@ -265,9 +297,14 @@
             for c in range(3):
                 left, right = summed[c * 16 : c * 16 + 8], summed[c * 16 + 8 : c * 16 + 16]
                 net_ref[z, c, pl.ds(x8, 8), :] = total[c] - jnp.concatenate([left, right], axis=1)
+        planes = pl.ds(g * (group // 4), group // 4)
+        pltpu.make_async_copy(net_ref.at[planes], net_hbm.at[planes], net_sem.at[g]).start()
         return carry
 
     lax.fori_loop(0, 32 // group, blocks, 0)
+    for g in range(32 // group):
+        planes = pl.ds(g * (group // 4), group // 4)
+        pltpu.make_async_copy(net_ref.at[planes], net_hbm.at[planes], net_sem.at[g]).wait()
 
 
 def per_device(
@@ -279,84 +316,96 @@
     cap = send_rows.shape[0] // devices
     vmem = pl.BlockSpec(memory_space=pltpu.VMEM)
     smem = pl.BlockSpec(memory_space=pltpu.SMEM)
-    params = pltpu.CompilerParams(vmem_limit_bytes=40 << 20)
-
+    params = pltpu.CompilerParams(vmem_limit_bytes=60 << 20)
     ends = [(d, d + 1) for d in range(n_brick - 1, devices - 1, n_brick)]
     ends += [(target, source) for source, target in ends]
     next_velocity = lax.ppermute(fluid_velocity, ("slab", "brick"), ends)
     next_porosity = lax.ppermute(porosity, ("slab", "brick"), ends)
 
-    arrived, staged = pl.pallas_call(
+    square = jax.ShapeDtypeStruct((256, 128), F32)
+    hbm = pl.BlockSpec(memory_space=pl.ANY)
+    staged, starts, key, p0, p1, p2, drag = pl.pallas_call(
         functools.partial(exchange_kernel, cap=cap, group=8),
         out_shape=(
-            jax.ShapeDtypeStruct((devices, 8, 128), F32),
             jax.ShapeDtypeStruct((8, 136, 512), F32),
+            jax.ShapeDtypeStruct((33,), I32),
+            jax.ShapeDtypeStruct((256, 128), I32),
+            square, square, square, square,
         ),
-        in_specs=[smem] + [vmem] * 5,
-        out_specs=(vmem, vmem),
+        in_specs=[smem] + [hbm] * 6,
+        out_specs=(hbm, smem) + (vmem,) * 5,
         scratch_shapes=[
+            pltpu.VMEM((3, 16384), F32),
+            pltpu.VMEM((128, 128), F32),
+            pltpu.VMEM((256, 128), I32),
+            pltpu.VMEM((3, 256, 512), F32),
+            pltpu.VMEM((256, 512), F32),
+            pltpu.VMEM((256, 128), I32),
+            pltpu.VMEM((3, 128, 128), F32),
+            pltpu.VMEM((8, 136, 512), F32),
             pltpu.VMEM((768, 256), BF16),
             pltpu.VMEM((devices, 8, 128), F32),
+            pltpu.VMEM((devices, 8, 128), F32),
+            pltpu.SemaphoreType.DMA((6,)),
+            pltpu.SemaphoreType.DMA,
             pltpu.SemaphoreType.DMA,
             pltpu.SemaphoreType.DMA,
         ],
         compiler_params=pltpu.CompilerParams(
-            vmem_limit_bytes=40 << 20, collective_id=0, has_side_effects=True
+            vmem_limit_bytes=60 << 20, collective_id=0, has_side_effects=True
         ),
         name="exchange",
     )(
         counts,
-        particle_velocity.reshape(3, 128, 128),
+        particle_velocity,
         drag_coef.reshape(128, 128),
         send_rows.reshape(256, 128),
         fluid_velocity.reshape(3, 256, 512),
         porosity.reshape(256, 512),
+        recv_cell.reshape(256, 128),
     )
 
     bricks = lax.all_to_all(staged, "brick", split_axis=0, concat_axis=0, tiled=True)
-
-    key, data, starts = pl.pallas_call(
-        key_kernel,
-        out_shape=(
-            jax.ShapeDtypeStruct((256, 128), I32),
-            jax.ShapeDtypeStruct((4, 256, 128), F32),
-            jax.ShapeDtypeStruct((33,), I32),
-        ),
-        in_specs=[vmem, vmem],
-        out_specs=(vmem, vmem, smem),
-        compiler_params=params,
-        name="block_keys",
-    )(arrived, recv_cell.reshape(256, 128))
-    flat = data.reshape(4, -1)
     ordered = lax.sort(
-        (key.reshape(-1), flat[3], flat[0], flat[1], flat[2]), num_keys=1, is_stable=False
-    )
-    force, slot, net = pl.pallas_call(
+        [part.reshape(-1) for part in (key, drag, p0, p1, p2)], num_keys=1, is_stable=False
+    )
+    f0, f1, f2, slot, net = pl.pallas_call(
         functools.partial(brick_kernel, width=256, group=8),
         out_shape=(
-            jax.ShapeDtypeStruct((3, 256, 128), F32),
+            square, square, square,
             jax.ShapeDtypeStruct((256, 128), I32),
             jax.ShapeDtypeStruct((8, 3, 32, 512), F32),
         ),
-        in_specs=[smem] + [vmem] * 6,
-        out_specs=(vmem, vmem, vmem),
+        in_specs=[smem] + [hbm] * 6,
+        out_specs=(vmem,) * 4 + (hbm,),
         scratch_shapes=[
+            pltpu.VMEM((256, 128), I32),
+            pltpu.VMEM((256, 128), F32),
+            pltpu.VMEM((256, 128), F32),
+            pltpu.VMEM((256, 128), F32),
+            pltpu.VMEM((256, 128), F32),
+            pltpu.VMEM((8, 136, 512), F32),
+            pltpu.VMEM((8, 3, 32, 512), F32),
             pltpu.VMEM((10, 4, 48, 512), F32),
             pltpu.VMEM((8, 192, 256), BF16),
             pltpu.VMEM((8, 144, 256), F32),
+            pltpu.SemaphoreType.DMA((6,)),
+            pltpu.SemaphoreType.DMA((4,)),
         ],
         compiler_params=params,
         name="brick_forces",
     )(starts, *[part.reshape(256, 128) for part in ordered], bricks)
 
     returned = lax.all_to_all(net, "brick", split_axis=0, concat_axis=0, tiled=True)
-    flat = force.reshape(3, -1)
-    back = lax.sort((slot.reshape(-1), flat[0], flat[1], flat[2]), num_keys=1, is_stable=False)
+    back = lax.sort([part.reshape(-1) for part in (slot, f0, f1, f2)], num_keys=1, is_stable=False)
     slot_force = jnp.stack(back[1:])
-    returned = jnp.swapaxes(returned, 0, 1).reshape(fluid_velocity.shape)
+    slot_force, next_velocity, next_porosity = lax.optimization_barrier(
+        (slot_force, next_velocity, next_porosity)
+    )
     brick = lax.axis_index("brick")
     face = 0.5 * (porosity + next_porosity) * (next_velocity - fluid_velocity)
     face = jnp.where((brick == 0) | (brick == n_brick - 1), face, 0.0)
+    returned = jnp.swapaxes(returned, 0, 1).reshape(fluid_velocity.shape)
     new_velocity = fluid_velocity + time_step * (returned + face) / porosity
     return (new_velocity, slot_force)
 

time: 150 us -> 137 us (0.913)
  local copies, waits for them, and re-layouts: 12.5 us -> 2.81 us
  waiting for transfers between devices: 25 us -> 15.5 us
  Pallas kernels: 45.7 us -> 52.2 us
    ppermute x1, waiting for transfers between devices: 20.7 us -> 0.01 us  [per_device(): next_porosity = lax.ppermute(porosity, ('slab', 'brick'), ends)]
    ppermute x1, waiting for transfers between devices: 0.01 us -> 15.5 us  [per_device(): next_velocity = lax.ppermute(fluid_velocity, ('slab', 'brick'), ends)]
    unnamed x25 -> x18, local copies, waits for them, and re-layouts: 10.4 us -> 2.63 us
    pallas_call x1, Pallas kernels: 13.2 us -> 19.3 us  [per_device(): pl.pallas_call(functools.partial(brick_kernel, width=256, group=8), out_s...]
    all_to_all x1, waiting for transfers between devices: 4.38 us -> 0.01 us  [per_device(): lax.all_to_all(net, 'brick', split_axis=0, concat_axis=0, tiled=True)]
    pallas_call x1, Pallas kernels: 30.8 us -> 32.9 us  [per_device(): pl.pallas_call(functools.partial(exchange_kernel, cap=cap, group=8), out_...]
    squeeze x2 -> x0, local copies, waits for them, and re-layouts: 1.91 us -> none  [per_device(): flat[2]]
    mul x1, other arithmetic: 1.92 us -> 0.09 us  [per_device(): face = 0.5 * (porosity + next_porosity) * (next_velocity - fluid_velocity)]
  transfers between devices with their start and end apart: 4 -> 4, of which waited for: 2 -> 1; matrix products, arithmetic and copies ran while one was open for 30% -> 31% of each run, Pallas kernels for 10% -> 14%
where the time goes in v5:
time: 137 us; the launch traced here: 136 us
  Pallas kernels  52.2 us (38%)
  other arithmetic  45.4 us (33%)
  starting transfers between devices  19.1 us (14%)
  waiting for transfers between devices  15.5 us (11%)
  local copies, waits for them, and re-layouts  2.81 us (2%)
    pallas_call x1, Pallas kernels, per_device(): pl.pallas_call(functools.partial(exchange_kernel, cap=cap, group=8), out_...  32.9 us
    sort x1, other arithmetic, per_device(): lax.sort([part.reshape(-1) for part in (key, drag, p0, p1, p2)], num_keys...  24.3 us
    pallas_call x1, Pallas kernels, per_device(): pl.pallas_call(functools.partial(brick_kernel, width=256, group=8), out_s...  19.3 us
    sort x1, other arithmetic, per_device(): lax.sort([part.reshape(-1) for part in (slot, f0, f1, f2)], num_keys=1, i...  16.6 us
    ppermute x1, waiting for transfers between devices, per_device(): next_velocity = lax.ppermute(fluid_velocity, ('slab', 'brick'), ends)  15.5 us
    ppermute x1, starting transfers between devices, per_device(): next_porosity = lax.ppermute(porosity, ('slab', 'brick'), ends)  7.39 us
    all_to_all x1, starting transfers between devices, per_device(): lax.all_to_all(staged, 'brick', split_axis=0, concat_axis=0, tiled=True)  5.23 us
    all_to_all x1, starting transfers between devices, per_device(): lax.all_to_all(net, 'brick', split_axis=0, concat_axis=0, tiled=True)  3.95 us
  transfers between devices with their start and end apart: 4, of which 1 were waited for; matrix products, arithmetic and copies ran while one was open for 31% of the time, Pallas kernels for 14%

profile of v5, /device:TPU:8, one launch (start us, length us, event | category | flops | bytes accessed | tf_op | source)
XLA Modules:
  0.0 135.8 jit_solution(17966553528272365181)
XLA Ops:
  0.6 32.9 %exchange.1 = (f32[8,136,512]{2,1,0:T(8,128)}, s32[33]{0:T(128)}, s32[256,128]{1,0:T(8,128)}, f32[256,128]{1,0:T(8,128)}, f32[256,128]{1,0:T(8,128)}, /*index=5*/f32[256,128]{1,0:T(8,128)}, f32[256,128]{1,0:T(8,128)}) custom-call(s32[128]{0:T(128)} %counts_ref.1, f32[3,16384]{1,0:T(4,128)} %pv_hbm.1, f32[128,128]{1,0:T(8,128)} %bitcast.61, ...), custom_call_target="tpu_custom_call" | custom-call | tf_op jit(solution)/shard_map/exchange/pallas_call | solution.py:327
  33.5 0.0 copy-start.2
  33.5 0.0 copy-start.3
  33.5 0.0 copy-start.4
  33.5 5.2 %all-to-all-start = ((f32[8,136,512]{2,1,0:T(8,128)}), f32[8,136,512]{2,1,0:T(8,128)S(1)}, u32[]{:S(2)}, u32[]{:S(2)}) async-start(f32[8,136,512]{2,1,0:T(8,128)} %get-tuple-element.36), calls=%async_computation | async-start | bytes 4456448 | tf_op jit(solution)/shard_map/all_to_all | solution.py:368
  38.8 0.0 copy-done.2
  38.8 7.4 %collective-permute-start.1 = (f32[1,256,512]{2,1,0:T(8,128)S(1)}, f32[1,256,512]{2,1,0:T(8,128)S(1)}, u32[]{:S(2)}, u32[]{:S(2)}) collective-permute-start(f32[1,256,512]{2,1,0:T(8,128)S(1)} %copy-done.2), channel_id=1, source_target_pairs={{7,8},{15,16},{23,24},{31,32},{39,40},{47,48},{55,56},{63,64},{71,... | collective-permute-start | bytes 1572872 | tf_op jit(solution)/shard_map/ppermute | solution.py:323
  46.2 2.6 %collective-permute-start = (f32[3,1,256,512]{3,2,0,1:T(8,128)}, f32[3,1,256,512]{3,2,0,1:T(8,128)}, u32[]{:S(2)}, u32[]{:S(2)}) collective-permute-start(f32[3,1,256,512]{3,2,0,1:T(8,128)} %bitcast.38), channel_id=1, source_target_pairs={{7,8},{15,16},{23,24},{31,32},{39,40},{47,48},{55,56},{63,64},{71,... | collective-permute-start | bytes 4718600 | tf_op jit(solution)/shard_map/ppermute | solution.py:322
  48.8 0.0 copy-done.3
  48.8 0.0 copy-done.4
  48.8 24.3 %sort.60 = (s32[32768]{0:T(1024)}, f32[32768]{0:T(1024)}, f32[32768]{0:T(1024)}, f32[32768]{0:T(1024)}, f32[32768]{0:T(1024)}) sort(s32[32768]{0:T(1024)S(1)} %bitcast.44, f32[32768]{0:T(1024)} %bitcast.48, f32[32768]{0:T(1024)S(1)} %bitcast.45, f32[32768]{0:T(1024)} %bitcast.46, f32[32768]{0:T(1024)} %bitcast.47), dimensions={0}, to_apply=%region_0.0 | sort | flops 491520 | bytes 1310720 | tf_op jit(solution)/shard_map/sort | solution.py:369
  73.0 0.0 all-to-all-done.bricks_hbm
  73.1 1.4 %copy-done = f32[8,136,512]{2,1,0:T(8,128)} copy-done((f32[8,136,512]{2,1,0:T(8,128)}, f32[8,136,512]{2,1,0:T(8,128)S(1)}, u32[]{:S(2)}) %copy-start) | copy-done | bytes 2228248
  74.4 19.3 %brick_forces.1 = (f32[256,128]{1,0:T(8,128)}, f32[256,128]{1,0:T(8,128)}, f32[256,128]{1,0:T(8,128)}, s32[256,128]{1,0:T(8,128)}, f32[8,3,32,512]{3,2,1,0:T(8,128)}) custom-call(s32[33]{0:T(128)} %get-tuple-element.25.starts_ref, s32[256,128]{1,0:T(8,128)} %bitcast.49, f32[256,128]{1,0:T(8,128)} %bitcast.50, f32[256,128]{1,0:T(8,128)} %bitcast.51, ...), custom_call_target="tpu_custom_call" | custom-call | tf_op jit(solution)/shard_map/brick_forces/pallas_call | solution.py:372
  93.8 0.0 copy-start.5
  93.8 0.0 copy-start.6
  93.8 0.0 copy-start.7
  93.8 0.0 copy-start.8
  93.8 3.9 %all-to-all-start.1 = ((f32[8,3,32,512]{3,2,1,0:T(8,128)}), f32[8,3,32,512]{3,2,1,0:T(8,128)S(1)}, u32[]{:S(2)}, u32[]{:S(2)}) async-start(f32[8,3,32,512]{3,2,1,0:T(8,128)} %get-tuple-element.37), calls=%async_computation.1 | async-start | bytes 3145728 | tf_op jit(solution)/shard_map/all_to_all | solution.py:399
  97.8 0.0 copy-done.5
  97.8 0.0 copy-done.6
  97.8 0.0 copy-done.7
  97.8 16.6 %sort.61 = (s32[32768]{0:T(1024)}, f32[32768]{0:T(1024)S(1)}, f32[32768]{0:T(1024)S(1)}, f32[32768]{0:T(1024)S(1)}) sort(s32[32768]{0:T(1024)S(1)} %bitcast.60, f32[32768]{0:T(1024)S(1)} %bitcast.57, f32[32768]{0:T(1024)S(1)} %bitcast.58, f32[32768]{0:T(1024)S(1)} %bitcast.59), dimensions={0}, to_apply=%region_1.0 | sort | flops 491520 | bytes 1048576 | tf_op jit(solution)/shard_map/sort | solution.py:400
  114.5 1.1 pad_maximum_fusion
  115.6 0.0 collective-permute-done.1
  115.6 15.5 %collective-permute-done = f32[3,1,256,512]{3,2,0,1:T(8,128)} collective-permute-done((f32[3,1,256,512]{3,2,0,1:T(8,128)}, f32[3,1,256,512]{3,2,0,1:T(8,128)}, u32[]{:S(2)}, u32[]{:S(2)}) %collective-permute-start) | collective-permute-done | bytes 1572896 | tf_op jit(solution)/shard_map/ppermute | solution.py:322
  131.1 0.1 multiply_bitcast_fusion
  131.2 0.0 all-to-all-done.1
  131.2 0.0 copy-start.1
  131.2 0.2 copy.9
  131.4 1.2 copy-done.1
  132.6 3.2 %fusion.2 = f32[3,1,256,512]{3,2,0,1:T(8,128)} fusion(f32[3,8,32,512]{3,2,1,0:T(8,128)S(1)} %copy.9, f32[3,1,256,512]{3,2,0,1:T(8,128)} %collective-permute-done, f32[256,512]{1,0:T(8,128)S(1)} %bitcast.40, f32[256,512]{1,0:T(8,128)S(1)} %multiply_bitcast_fusion, pred[]{:T(512)S(6)} %or.3, f32[3,1,256,512]{3,2,1,0:T(8,128)S(1)} %copy-done.1), kind=kLoop, calls=%fused_computation.3 | loop fusion | flops 2752512 | bytes 7340033 | tf_op jit(solution)/shard_map/add | solution.py:409
  (2 shorter events, 0.0 us)
Async XLA Ops:
  33.5 5.3 %copy-start.2 = (f32[1,256,512]{2,1,0:T(8,128)S(1)}, f32[1,256,512]{2,1,0:T(8,128)}, u32[]{:S(2)}) copy-start(f32[1,256,512]{2,1,0:T(8,128)} %param.8) | copy-start | bytes 1572868
  33.5 15.3 %copy-start.3 = (s32[256,128]{1,0:T(8,128)S(1)}, s32[256,128]{1,0:T(8,128)}, u32[]{:S(2)}) copy-start(s32[256,128]{1,0:T(8,128)} %get-tuple-element.26) | copy-start | bytes 393220
  33.5 15.3 %copy-start.4 = (f32[256,128]{1,0:T(8,128)S(1)}, f32[256,128]{1,0:T(8,128)}, u32[]{:S(2)}) copy-start(f32[256,128]{1,0:T(8,128)} %get-tuple-element.28) | copy-start | bytes 393220
  33.5 39.5 %all-to-all-start = ((f32[8,136,512]{2,1,0:T(8,128)}), f32[8,136,512]{2,1,0:T(8,128)S(1)}, u32[]{:S(2)}, u32[]{:S(2)}) async-start(f32[8,136,512]{2,1,0:T(8,128)} %get-tuple-element.36), calls=%async_computation | async-start | bytes 4456448 | tf_op jit(solution)/shard_map/all_to_all | solution.py:368
  38.8 76.8 %collective-permute-start.1 = (f32[1,256,512]{2,1,0:T(8,128)S(1)}, f32[1,256,512]{2,1,0:T(8,128)S(1)}, u32[]{:S(2)}, u32[]{:S(2)}) collective-permute-start(f32[1,256,512]{2,1,0:T(8,128)S(1)} %copy-done.2), channel_id=1, source_target_pairs={{7,8},{15,16},{23,24},{31,32},{39,40},{47,48},{55,56},{63,64},{71,... | collective-permute-start | bytes 1572872 | tf_op jit(solution)/shard_map/ppermute | solution.py:323
  46.2 84.9 %collective-permute-start = (f32[3,1,256,512]{3,2,0,1:T(8,128)}, f32[3,1,256,512]{3,2,0,1:T(8,128)}, u32[]{:S(2)}, u32[]{:S(2)}) collective-permute-start(f32[3,1,256,512]{3,2,0,1:T(8,128)} %bitcast.38), channel_id=1, source_target_pairs={{7,8},{15,16},{23,24},{31,32},{39,40},{47,48},{55,56},{63,64},{71,... | collective-permute-start | bytes 4718600 | tf_op jit(solution)/shard_map/ppermute | solution.py:322
  73.1 1.4 %copy-start = (f32[8,136,512]{2,1,0:T(8,128)}, f32[8,136,512]{2,1,0:T(8,128)S(1)}, u32[]{:S(2)}) copy-start(f32[8,136,512]{2,1,0:T(8,128)S(1)} %all-to-all-done.bricks_hbm) | copy-start | bytes 6684676
  93.8 4.0 %copy-start.5 = (f32[256,128]{1,0:T(8,128)S(1)}, f32[256,128]{1,0:T(8,128)}, u32[]{:S(2)}) copy-start(f32[256,128]{1,0:T(8,128)} %get-tuple-element.39) | copy-start | bytes 393220
  93.8 4.0 %copy-start.6 = (f32[256,128]{1,0:T(8,128)S(1)}, f32[256,128]{1,0:T(8,128)}, u32[]{:S(2)}) copy-start(f32[256,128]{1,0:T(8,128)} %get-tuple-element.40) | copy-start | bytes 393220
  93.8 4.0 %copy-start.7 = (f32[256,128]{1,0:T(8,128)S(1)}, f32[256,128]{1,0:T(8,128)}, u32[]{:S(2)}) copy-start(f32[256,128]{1,0:T(8,128)} %get-tuple-element.41) | copy-start | bytes 393220
  93.8 4.0 %copy-start.8 = (s32[256,128]{1,0:T(8,128)S(1)}, s32[256,128]{1,0:T(8,128)}, u32[]{:S(2)}) copy-start(s32[256,128]{1,0:T(8,128)} %get-tuple-element.38) | copy-start | bytes 393220
  93.8 37.4 %all-to-all-start.1 = ((f32[8,3,32,512]{3,2,1,0:T(8,128)}), f32[8,3,32,512]{3,2,1,0:T(8,128)S(1)}, u32[]{:S(2)}, u32[]{:S(2)}) async-start(f32[8,3,32,512]{3,2,1,0:T(8,128)} %get-tuple-element.37), calls=%async_computation.1 | async-start | bytes 3145728 | tf_op jit(solution)/shard_map/all_to_all | solution.py:399
  131.2 1.4 %copy-start.1 = (f32[3,1,256,512]{3,2,1,0:T(8,128)S(1)}, f32[3,1,256,512]{3,2,1,0:T(8,128)}, u32[]{:S(2)}) copy-start(f32[3,1,256,512]{3,2,1,0:T(8,128)} %param.7) | copy-start | bytes 4718596

commit v6 on v5

--- a/solution.py
+++ b/solution.py
@@ -22,9 +22,10 @@
 
 def exchange_kernel(
     counts_ref, pv_hbm, coef_hbm, rows_hbm, u_hbm, frac_hbm, cell_hbm,
-    stage_hbm, starts_ref, key_ref, p0_ref, p1_ref, p2_ref, drag_ref,
+    stage_hbm, zhalo_ref, starts_ref, key_ref, p0_ref, p1_ref, p2_ref, drag_ref,
     pv_ref, coef_ref, rows_ref, u_ref, frac_ref, cell_ref, particles,
-    stage, table, packed, arrived_ref, load_sem, stage_sem, part_send, part_recv, *, cap, group,
+    stage, table, packed, arrived_ref, load_sem, stage_sem, part_send, part_recv, halo_send, halo_recv,
+    *, cap, group,
 ):
     pairs = (
         (u_hbm, u_ref), (frac_hbm, frac_ref), (pv_hbm, pv_ref), (coef_hbm, coef_ref), (rows_hbm, rows_ref),
@@ -78,6 +79,26 @@
 
     pl.semaphore_wait(barrier, devices - 1)
 
+    def halo(i, b):
+        return pltpu.make_async_remote_copy(
+            src_ref=stage.at[b, pl.ds(0, 128)], dst_ref=zhalo_ref.at[i], send_sem=halo_send.at[i, b],
+            recv_sem=halo_recv.at[i], device_id=((slab + 1, b), (slab - 1, b))[i], device_id_type=mesh_id,
+        )
+
+    up, down = slab < n_slab - 1, slab > 0
+    gives = (up & (brick == n_brick - 1), down & (brick == 0))
+    gets = (down, up)
+    for i in range(2):
+
+        @pl.when(gives[i])
+        def _():
+            for b in range(8):
+                halo(i, b).start()
+
+        @pl.when(jnp.logical_not(gets[i]))
+        def _():
+            zhalo_ref[i] = jnp.zeros((128, 512), F32)
+
     r_iota = lax.broadcasted_iota(I32, (256, cap), 0).astype(F32).astype(BF16)
     one, zero = jnp.ones((), BF16), jnp.zeros((), BF16)
     l_iota = lax.broadcasted_iota(I32, (64, cap), 0)
@@ -139,6 +160,17 @@
     rest.wait_send()
     rest.wait_recv()
     saved.wait()
+    for i in range(2):
+
+        @pl.when(gives[i])
+        def _():
+            for b in range(8):
+                halo(i, b).wait_send()
+
+        @pl.when(gets[i])
+        def _():
+            halo(i, 0).wait_recv()
+
 
     tiles = cell_ref.shape[0] // 8
     place = lax.broadcasted_iota(I32, (8, 128), 0) * 128 + lax.broadcasted_iota(I32, (8, 128), 1)
@@ -167,16 +199,16 @@
 
 
 def brick_kernel(
-    starts_ref, key_hbm, coef_hbm, p0_hbm, p1_hbm, p2_hbm, bricks_hbm,
+    starts_ref, key_hbm, coef_hbm, p0_hbm, p1_hbm, p2_hbm, bricks_hbm, zhalo_hbm,
     f0_ref, f1_ref, f2_ref, slot_ref, net_hbm,
-    key_ref, coef_ref, p0_ref, p1_ref, p2_ref, bricks_ref, net_ref, padded, table, deposit, load_sem, net_sem,
+    key_ref, coef_ref, p0_ref, p1_ref, p2_ref, bricks_ref, zhalo_ref, net_ref, padded, table, deposit, load_sem, net_sem,
     *, width, group,
 ):
     rows = key_ref.shape[0]
     n = width // 128
     pairs = (
         (bricks_hbm, bricks_ref), (key_hbm, key_ref), (coef_hbm, coef_ref), (p0_hbm, p0_ref), (p1_hbm, p1_ref),
-        (p2_hbm, p2_ref),
+        (p2_hbm, p2_ref), (zhalo_hbm, zhalo_ref),
     )
     loads = [pltpu.make_async_copy(source, target, load_sem.at[i]) for i, (source, target) in enumerate(pairs)]
     for load in loads:
@@ -193,8 +225,8 @@
             padded[z + 1, c, 8:40, :] = bricks_ref[z, own, :]
             padded[z + 1, c, 7:8, :] = bricks_ref[z, 128 + c : 129 + c, :]
             padded[z + 1, c, 40:41, :] = bricks_ref[z, 132 + c : 133 + c, :]
-        padded[0, c, 8:40, :] = bricks_ref[0, own, :]
-        padded[9, c, 8:40, :] = bricks_ref[7, own, :]
+        padded[0, c, 8:40, :] = zhalo_ref[0, own, :]
+        padded[9, c, 8:40, :] = zhalo_ref[1, own, :]
 
     r_iota = lax.broadcasted_iota(I32, (256, width), 0)
     l_iota = lax.broadcasted_iota(I32, (16, width), 0)
@@ -317,23 +349,19 @@
     vmem = pl.BlockSpec(memory_space=pltpu.VMEM)
     smem = pl.BlockSpec(memory_space=pltpu.SMEM)
     params = pltpu.CompilerParams(vmem_limit_bytes=60 << 20)
-    ends = [(d, d + 1) for d in range(n_brick - 1, devices - 1, n_brick)]
-    ends += [(target, source) for source, target in ends]
-    next_velocity = lax.ppermute(fluid_velocity, ("slab", "brick"), ends)
-    next_porosity = lax.ppermute(porosity, ("slab", "brick"), ends)
-
     square = jax.ShapeDtypeStruct((256, 128), F32)
     hbm = pl.BlockSpec(memory_space=pl.ANY)
-    staged, starts, key, p0, p1, p2, drag = pl.pallas_call(
+    staged, zhalo, starts, key, p0, p1, p2, drag = pl.pallas_call(
         functools.partial(exchange_kernel, cap=cap, group=8),
         out_shape=(
             jax.ShapeDtypeStruct((8, 136, 512), F32),
+            jax.ShapeDtypeStruct((2, 128, 512), F32),
             jax.ShapeDtypeStruct((33,), I32),
             jax.ShapeDtypeStruct((256, 128), I32),
             square, square, square, square,
         ),
         in_specs=[smem] + [hbm] * 6,
-        out_specs=(hbm, smem) + (vmem,) * 5,
+        out_specs=(hbm, vmem, smem) + (vmem,) * 5,
         scratch_shapes=[
             pltpu.VMEM((3, 16384), F32),
             pltpu.VMEM((128, 128), F32),
@@ -350,6 +378,8 @@
             pltpu.SemaphoreType.DMA,
             pltpu.SemaphoreType.DMA,
             pltpu.SemaphoreType.DMA,
+            pltpu.SemaphoreType.DMA((2, 8)),
+            pltpu.SemaphoreType.DMA((2,)),
         ],
         compiler_params=pltpu.CompilerParams(
             vmem_limit_bytes=60 << 20, collective_id=0, has_side_effects=True
@@ -376,7 +406,7 @@
             jax.ShapeDtypeStruct((256, 128), I32),
             jax.ShapeDtypeStruct((8, 3, 32, 512), F32),
         ),
-        in_specs=[smem] + [hbm] * 6,
+        in_specs=[smem] + [hbm] * 7,
         out_specs=(vmem,) * 4 + (hbm,),
         scratch_shapes=[
             pltpu.VMEM((256, 128), I32),
@@ -385,28 +415,23 @@
             pltpu.VMEM((256, 128), F32),
             pltpu.VMEM((256, 128), F32),
             pltpu.VMEM((8, 136, 512), F32),
+            pltpu.VMEM((2, 128, 512), F32),
             pltpu.VMEM((8, 3, 32, 512), F32),
             pltpu.VMEM((10, 4, 48, 512), F32),
             pltpu.VMEM((8, 192, 256), BF16),
             pltpu.VMEM((8, 144, 256), F32),
-            pltpu.SemaphoreType.DMA((6,)),
+            pltpu.SemaphoreType.DMA((7,)),
             pltpu.SemaphoreType.DMA((4,)),
         ],
         compiler_params=params,
         name="brick_forces",
-    )(starts, *[part.reshape(256, 128) for part in ordered], bricks)
+    )(starts, *[part.reshape(256, 128) for part in ordered], bricks, zhalo)
 
     returned = lax.all_to_all(net, "brick", split_axis=0, concat_axis=0, tiled=True)
     back = lax.sort([part.reshape(-1) for part in (slot, f0, f1, f2)], num_keys=1, is_stable=False)
     slot_force = jnp.stack(back[1:])
-    slot_force, next_velocity, next_porosity = lax.optimization_barrier(
-        (slot_force, next_velocity, next_porosity)
-    )
-    brick = lax.axis_index("brick")
-    face = 0.5 * (porosity + next_porosity) * (next_velocity - fluid_velocity)
-    face = jnp.where((brick == 0) | (brick == n_brick - 1), face, 0.0)
     returned = jnp.swapaxes(returned, 0, 1).reshape(fluid_velocity.shape)
-    new_velocity = fluid_velocity + time_step * (returned + face) / porosity
+    new_velocity = fluid_velocity + time_step * returned / porosity
     return (new_velocity, slot_force)
 
 

time: 137 us -> 129 us (0.942)
  the two profiles are of different devices: /device:TPU:8 before, /device:TPU:1 now
where the time goes in v6:
time: 129 us
  Pallas kernels  61.5 us (48%)
  other arithmetic  42.9 us (33%)
  starting transfers between devices  13.7 us (11%)
  waiting for transfers between devices  7 us (5%)
  local copies, waits for them, and re-layouts  2.92 us (2%)
    pallas_call x1, Pallas kernels, per_device(): pl.pallas_call(functools.partial(exchange_kernel, cap=cap, group=8), out_...  44.9 us
    sort x1, other arithmetic, per_device(): lax.sort([part.reshape(-1) for part in (key, drag, p0, p1, p2)], num_keys...  23.3 us
    sort x1, other arithmetic, per_device(): lax.sort([part.reshape(-1) for part in (slot, f0, f1, f2)], num_keys=1, i...  16.6 us
    pallas_call x1, Pallas kernels, per_device(): pl.pallas_call(functools.partial(brick_kernel, width=256, group=8), out_s...  16.6 us
    all_to_all x1, starting transfers between devices, per_device(): lax.all_to_all(net, 'brick', split_axis=0, concat_axis=0, tiled=True)  7.84 us
    all_to_all x1, starting transfers between devices, per_device(): lax.all_to_all(staged, 'brick', split_axis=0, concat_axis=0, tiled=True)  5.9 us
    all_to_all x1, waiting for transfers between devices, per_device(): lax.all_to_all(staged, 'brick', split_axis=0, concat_axis=0, tiled=True)  4.26 us
    unnamed x24, local copies, waits for them, and re-layouts  2.8 us
  transfers between devices with their start and end apart: 2, of which 2 were waited for; matrix products, arithmetic and copies ran while one was open for 32% of the time, Pallas kernels for 0%

profile of v6, /device:TPU:1, one launch (start us, length us, event | category | flops | bytes accessed | tf_op | source)
XLA Modules:
  0.0 128.9 jit_solution(10342995516268154059)
XLA Ops:
  0.6 44.9 %exchange.1 = (f32[8,136,512]{2,1,0:T(8,128)}, f32[2,128,512]{2,1,0:T(8,128)}, s32[33]{0:T(128)}, s32[256,128]{1,0:T(8,128)}, f32[256,128]{1,0:T(8,128)}, /*inde...) custom-call(s32[128]{0:T(128)} %counts_ref.1, f32[3,16384]{1,0:T(4,128)} %pv_hbm.1, f32[128,128]{1,0:T(8,128)} %bitcast.54, ...), custom_call_target="tpu_custom_call" | custom-call | tf_op jit(solution)/shard_map/exchange/pallas_call | solution.py:354
  45.6 0.0 copy-start.3
  45.6 0.0 copy-start.4
  45.6 0.0 copy-start.5
  45.6 0.0 copy-start.6
  45.6 0.0 copy-start.7
  45.6 5.9 %all-to-all-start = ((f32[8,136,512]{2,1,0:T(8,128)}), f32[8,136,512]{2,1,0:T(8,128)S(1)}, u32[]{:S(2)}, u32[]{:S(2)}) async-start(f32[8,136,512]{2,1,0:T(8,128)} %get-tuple-element.34), calls=%async_computation | async-start | bytes 4456448 | tf_op jit(solution)/shard_map/all_to_all | solution.py:398
  51.5 0.0 copy-done.3
  51.5 0.0 copy-done.4
  51.5 0.0 copy-done.5
  51.5 0.0 copy-done.6
  51.5 0.0 copy-done.7
  51.6 23.3 %sort.60 = (s32[32768]{0:T(1024)}, f32[32768]{0:T(1024)}, f32[32768]{0:T(1024)}, f32[32768]{0:T(1024)}, f32[32768]{0:T(1024)}) sort(s32[32768]{0:T(1024)S(1)} %bitcast.42, f32[32768]{0:T(1024)S(1)} %bitcast.46, f32[32768]{0:T(1024)S(1)} %bitcast.43, f32[32768]{0:T(1024)S(1)} %bitcast.44, f32[32768]{0:T(1024)S(1)} %bitcast.45), dimensions={0}, to_apply=%region_0.0 | sort | flops 491520 | bytes 1310720 | tf_op jit(solution)/shard_map/sort | solution.py:399
  74.8 4.3 %all-to-all-done.bricks_hbm = f32[8,136,512]{2,1,0:T(8,128)S(1)} async-done(((f32[8,136,512]{2,1,0:T(8,128)}), f32[8,136,512]{2,1,0:T(8,128)S(1)}, u32[]{:S(2)}, u32[]{:S(2)}) %all-to-all-start) | async-done | bytes 2228256 | tf_op jit(solution)/shard_map/all_to_all | solution.py:398
  79.1 1.4 %copy-done = f32[8,136,512]{2,1,0:T(8,128)} copy-done((f32[8,136,512]{2,1,0:T(8,128)}, f32[8,136,512]{2,1,0:T(8,128)S(1)}, u32[]{:S(2)}) %copy-start) | copy-done | bytes 2228248
  80.5 16.6 %brick_forces.1 = (f32[256,128]{1,0:T(8,128)}, f32[256,128]{1,0:T(8,128)}, f32[256,128]{1,0:T(8,128)}, s32[256,128]{1,0:T(8,128)}, f32[8,3,32,512]{3,2,1,0:T(8,128)}) custom-call(s32[33]{0:T(128)} %get-tuple-element.23.starts_ref, s32[256,128]{1,0:T(8,128)} %bitcast.37, f32[256,128]{1,0:T(8,128)} %bitcast.38, f32[256,128]{1,0:T(8,128)} %bitcast.39, ...), custom_call_target="tpu_custom_call" | custom-call | tf_op jit(solution)/shard_map/brick_forces/pallas_call | solution.py:402
  97.1 0.0 copy-start.8
  97.1 0.0 copy-start.9
  97.1 0.0 copy-start.10
  97.1 0.0 copy-start.11
  97.1 7.8 %all-to-all-start.1 = ((f32[8,3,32,512]{3,2,1,0:T(8,128)}), f32[8,3,32,512]{3,2,1,0:T(8,128)S(1)}, u32[]{:S(2)}, u32[]{:S(2)}) async-start(f32[8,3,32,512]{3,2,1,0:T(8,128)} %get-tuple-element.36), calls=%async_computation.1 | async-start | bytes 3145728 | tf_op jit(solution)/shard_map/all_to_all | solution.py:430
  105.0 0.0 copy-done.8
  105.0 16.6 %sort.61 = (s32[32768]{0:T(1024)}, f32[32768]{0:T(1024)S(1)}, f32[32768]{0:T(1024)S(1)}, f32[32768]{0:T(1024)S(1)}) sort(s32[32768]{0:T(1024)S(1)} %bitcast.53, f32[32768]{0:T(1024)S(1)} %bitcast.50, f32[32768]{0:T(1024)S(1)} %bitcast.51, f32[32768]{0:T(1024)S(1)} %bitcast.52), dimensions={0}, to_apply=%region_1.0 | sort | flops 491520 | bytes 1048576 | tf_op jit(solution)/shard_map/sort | solution.py:431
  121.7 1.1 pad_maximum_fusion
  122.8 2.7 %all-to-all-done.1 = f32[8,3,32,512]{3,2,1,0:T(8,128)S(1)} async-done(((f32[8,3,32,512]{3,2,1,0:T(8,128)}), f32[8,3,32,512]{3,2,1,0:T(8,128)S(1)}, u32[]{:S(2)}, u32[]{:S(2)}) %all-to-all-start.1) | async-done | bytes 1572896 | tf_op jit(solution)/shard_map/all_to_all | solution.py:430
  125.5 0.2 multiply_bitcast_fusion
  125.8 0.0 copy-start.1
  125.8 0.0 copy-start.2
  125.8 0.1 copy.9
  125.9 1.3 copy-done.1
  127.2 0.1 copy-done.2
  127.3 1.6 %fusion = f32[3,1,256,512]{3,2,0,1:T(8,128)} fusion(f32[3,8,32,512]{3,2,1,0:T(8,128)S(1)} %copy.9, f32[3,1,256,512]{3,2,1,0:T(8,128)S(1)} %copy-done.1, f32[256,512]{1,0:T(8,128)S(1)} %bitcast.33), kind=kLoop, calls=%fused_computation.1 | loop fusion | flops 786432 | bytes 5242880 | tf_op jit(solution)/shard_map/add | solution.py:434
  (4 shorter events, 0.0 us)
Async XLA Ops:
  45.6 6.0 %copy-start.3 = (s32[256,128]{1,0:T(8,128)S(1)}, s32[256,128]{1,0:T(8,128)}, u32[]{:S(2)}) copy-start(s32[256,128]{1,0:T(8,128)} %get-tuple-element.24) | copy-start | bytes 393220
  45.6 5.9 %copy-start.4 = (f32[256,128]{1,0:T(8,128)S(1)}, f32[256,128]{1,0:T(8,128)}, u32[]{:S(2)}) copy-start(f32[256,128]{1,0:T(8,128)} %get-tuple-element.26) | copy-start | bytes 393220
  45.6 5.9 %copy-start.5 = (f32[256,128]{1,0:T(8,128)S(1)}, f32[256,128]{1,0:T(8,128)}, u32[]{:S(2)}) copy-start(f32[256,128]{1,0:T(8,128)} %get-tuple-element.27) | copy-start | bytes 393220
  45.6 5.9 %copy-start.6 = (f32[256,128]{1,0:T(8,128)S(1)}, f32[256,128]{1,0:T(8,128)}, u32[]{:S(2)}) copy-start(f32[256,128]{1,0:T(8,128)} %get-tuple-element.28) | copy-start | bytes 393220
  45.6 5.9 %copy-start.7 = (f32[256,128]{1,0:T(8,128)S(1)}, f32[256,128]{1,0:T(8,128)}, u32[]{:S(2)}) copy-start(f32[256,128]{1,0:T(8,128)} %get-tuple-element.25) | copy-start | bytes 393220
  45.6 33.5 %all-to-all-start = ((f32[8,136,512]{2,1,0:T(8,128)}), f32[8,136,512]{2,1,0:T(8,128)S(1)}, u32[]{:S(2)}, u32[]{:S(2)}) async-start(f32[8,136,512]{2,1,0:T(8,128)} %get-tuple-element.34), calls=%async_computation | async-start | bytes 4456448 | tf_op jit(solution)/shard_map/all_to_all | solution.py:398
  79.1 1.4 %copy-start = (f32[8,136,512]{2,1,0:T(8,128)}, f32[8,136,512]{2,1,0:T(8,128)S(1)}, u32[]{:S(2)}) copy-start(f32[8,136,512]{2,1,0:T(8,128)S(1)} %all-to-all-done.bricks_hbm) | copy-start | bytes 6684676
  97.1 7.9 %copy-start.8 = (f32[256,128]{1,0:T(8,128)S(1)}, f32[256,128]{1,0:T(8,128)}, u32[]{:S(2)}) copy-start(f32[256,128]{1,0:T(8,128)} %get-tuple-element.38) | copy-start | bytes 393220
  97.1 7.9 %copy-start.9 = (f32[256,128]{1,0:T(8,128)S(1)}, f32[256,128]{1,0:T(8,128)}, u32[]{:S(2)}) copy-start(f32[256,128]{1,0:T(8,128)} %get-tuple-element.39) | copy-start | bytes 393220
  97.1 7.9 %copy-start.10 = (f32[256,128]{1,0:T(8,128)S(1)}, f32[256,128]{1,0:T(8,128)}, u32[]{:S(2)}) copy-start(f32[256,128]{1,0:T(8,128)} %get-tuple-element.40) | copy-start | bytes 393220
  97.1 7.9 %copy-start.11 = (s32[256,128]{1,0:T(8,128)S(1)}, s32[256,128]{1,0:T(8,128)}, u32[]{:S(2)}) copy-start(s32[256,128]{1,0:T(8,128)} %get-tuple-element.37) | copy-start | bytes 393220
  97.1 28.4 %all-to-all-start.1 = ((f32[8,3,32,512]{3,2,1,0:T(8,128)}), f32[8,3,32,512]{3,2,1,0:T(8,128)S(1)}, u32[]{:S(2)}, u32[]{:S(2)}) async-start(f32[8,3,32,512]{3,2,1,0:T(8,128)} %get-tuple-element.36), calls=%async_computation.1 | async-start | bytes 3145728 | tf_op jit(solution)/shard_map/all_to_all | solution.py:430
  125.8 1.4 %copy-start.1 = (f32[3,1,256,512]{3,2,1,0:T(8,128)S(1)}, f32[3,1,256,512]{3,2,1,0:T(8,128)}, u32[]{:S(2)}) copy-start(f32[3,1,256,512]{3,2,1,0:T(8,128)} %param.7) | copy-start | bytes 4718596
  125.8 1.5 %copy-start.2 = (f32[1,256,512]{2,1,0:T(8,128)S(1)}, f32[1,256,512]{2,1,0:T(8,128)}, u32[]{:S(2)}) copy-start(f32[1,256,512]{2,1,0:T(8,128)} %param.8) | copy-start | bytes 1572868

commit v7 on v5

--- a/solution.py
+++ b/solution.py
@@ -167,41 +167,21 @@
 
 
 def brick_kernel(
-    starts_ref, key_hbm, coef_hbm, p0_hbm, p1_hbm, p2_hbm, bricks_hbm,
-    f0_ref, f1_ref, f2_ref, slot_ref, net_hbm,
-    key_ref, coef_ref, p0_ref, p1_ref, p2_ref, bricks_ref, net_ref, padded, table, deposit, load_sem, net_sem,
-    *, width, group,
+    starts_ref, key_ref, coef_ref, p0_ref, p1_ref, p2_ref, bricks_ref,
+    f0_ref, f1_ref, f2_ref, slot_ref, sum_ref, table, deposit, *, width, group,
 ):
     rows = key_ref.shape[0]
     n = width // 128
-    pairs = (
-        (bricks_hbm, bricks_ref), (key_hbm, key_ref), (coef_hbm, coef_ref), (p0_hbm, p0_ref), (p1_hbm, p1_ref),
-        (p2_hbm, p2_ref),
-    )
-    loads = [pltpu.make_async_copy(source, target, load_sem.at[i]) for i, (source, target) in enumerate(pairs)]
-    for load in loads:
-        load.start()
     force_refs = (f0_ref, f1_ref, f2_ref)
     for ref in force_refs:
         ref[...] = jnp.zeros_like(ref)
-    for load in loads:
-        load.wait()
     slot_ref[...] = jnp.where(coef_ref[...] != 0.0, (key_ref[...] >> 12) & 32767, p0_ref[...].astype(I32))
-    for c in range(4):
-        own = slice(c * 32, (c + 1) * 32)
-        for z in range(8):
-            padded[z + 1, c, 8:40, :] = bricks_ref[z, own, :]
-            padded[z + 1, c, 7:8, :] = bricks_ref[z, 128 + c : 129 + c, :]
-            padded[z + 1, c, 40:41, :] = bricks_ref[z, 132 + c : 133 + c, :]
-        padded[0, c, 8:40, :] = bricks_ref[0, own, :]
-        padded[9, c, 8:40, :] = bricks_ref[7, own, :]
 
     r_iota = lax.broadcasted_iota(I32, (256, width), 0)
     l_iota = lax.broadcasted_iota(I32, (16, width), 0)
     r_iota = r_iota.astype(F32).astype(BF16)
     l_bf = l_iota.astype(F32).astype(BF16)
     p_iota = lax.broadcasted_iota(I32, (1, width), 1)
-    y_iota = lax.broadcasted_iota(I32, (8, 512), 1)
     one, zero = jnp.ones((), BF16), jnp.zeros((), BF16)
 
     def blocks(g, carry):
@@ -211,7 +191,7 @@
             z, q = b // 4, b % 4
             x8 = pl.multiple_of(q * 8, 8)
             for c in range(4):
-                centre = padded[z + 1, c, pl.ds(x8 + 8, 8), :]
+                centre = bricks_ref[z, pl.ds(pl.multiple_of(c * 32 + x8, 8), 8), :]
                 for p, piece in enumerate(split3(centre)):
                     at = p * 64 + c * 16
                     table[i, at : at + 16, :] = jnp.concatenate([piece[:, :256], piece[:, 256:]], axis=0)
@@ -281,9 +261,31 @@
         for i, b in enumerate(bs):
             z, q = b // 4, b % 4
             x8 = pl.multiple_of(q * 8, 8)
-            tall = [padded[z + 1, c, pl.ds(x8, 24), :] for c in range(4)]
-            below = [padded[z, c, pl.ds(x8 + 8, 8), :] for c in range(4)]
-            above = [padded[z + 2, c, pl.ds(x8 + 8, 8), :] for c in range(4)]
+            summed = deposit[i, 0:48, :] + (deposit[i, 48:96, :] + deposit[i, 96:144, :])
+            for c in range(3):
+                left, right = summed[c * 16 : c * 16 + 8], summed[c * 16 + 8 : c * 16 + 16]
+                sum_ref[z, c, pl.ds(x8, 8), :] = jnp.concatenate([left, right], axis=1)
+        return carry
+
+    lax.fori_loop(0, 32 // group, blocks, 0)
+
+
+def viscous_kernel(bricks_ref, below_ref, above_ref, sum_ref, net_ref, padded):
+    for c in range(4):
+        own = slice(c * 32, (c + 1) * 32)
+        for z in range(8):
+            padded[z + 1, c, 8:40, :] = bricks_ref[z, own, :]
+            padded[z + 1, c, 7:8, :] = bricks_ref[z, 128 + c : 129 + c, :]
+            padded[z + 1, c, 40:41, :] = bricks_ref[z, 132 + c : 133 + c, :]
+        padded[0, c, 8:40, :] = below_ref[own, :]
+        padded[9, c, 8:40, :] = above_ref[own, :]
+    y_iota = lax.broadcasted_iota(I32, (8, 512), 1)
+
+    def plane(z, carry):
+        for x8 in range(0, 32, 8):
+            tall = [padded[z + 1, c, x8 : x8 + 24, :] for c in range(4)]
+            below = [padded[z, c, x8 + 8 : x8 + 16, :] for c in range(4)]
+            above = [padded[z + 2, c, x8 + 8 : x8 + 16, :] for c in range(4)]
             centre = [t[8:16] for t in tall]
             sides = [above, below, [t[9:17] for t in tall], [t[7:15] for t in tall]]
             sides.append([jnp.where(y_iota == 511, 0.0, pltpu.roll(t, 511, 1)) for t in centre])
@@ -293,18 +295,11 @@
                 weight = 0.5 * (centre[3] + side[3])
                 for c in range(3):
                     total[c] = total[c] + weight * (side[c] - centre[c])
-            summed = deposit[i, 0:48, :] + (deposit[i, 48:96, :] + deposit[i, 96:144, :])
             for c in range(3):
-                left, right = summed[c * 16 : c * 16 + 8], summed[c * 16 + 8 : c * 16 + 16]
-                net_ref[z, c, pl.ds(x8, 8), :] = total[c] - jnp.concatenate([left, right], axis=1)
-        planes = pl.ds(g * (group // 4), group // 4)
-        pltpu.make_async_copy(net_ref.at[planes], net_hbm.at[planes], net_sem.at[g]).start()
+                net_ref[z, c, x8 : x8 + 8, :] = total[c] - sum_ref[z, c, x8 : x8 + 8, :]
         return carry
 
-    lax.fori_loop(0, 32 // group, blocks, 0)
-    for g in range(32 // group):
-        planes = pl.ds(g * (group // 4), group // 4)
-        pltpu.make_async_copy(net_ref.at[planes], net_hbm.at[planes], net_sem.at[g]).wait()
+    lax.fori_loop(0, 8, plane, 0)
 
 
 def per_device(
@@ -316,12 +311,7 @@
     cap = send_rows.shape[0] // devices
     vmem = pl.BlockSpec(memory_space=pltpu.VMEM)
     smem = pl.BlockSpec(memory_space=pltpu.SMEM)
-    params = pltpu.CompilerParams(vmem_limit_bytes=60 << 20)
-    ends = [(d, d + 1) for d in range(n_brick - 1, devices - 1, n_brick)]
-    ends += [(target, source) for source, target in ends]
-    next_velocity = lax.ppermute(fluid_velocity, ("slab", "brick"), ends)
-    next_porosity = lax.ppermute(porosity, ("slab", "brick"), ends)
-
+    params = pltpu.CompilerParams(vmem_limit_bytes=32 << 20)
     square = jax.ShapeDtypeStruct((256, 128), F32)
     hbm = pl.BlockSpec(memory_space=pl.ANY)
     staged, starts, key, p0, p1, p2, drag = pl.pallas_call(
@@ -369,44 +359,38 @@
     ordered = lax.sort(
         [part.reshape(-1) for part in (key, drag, p0, p1, p2)], num_keys=1, is_stable=False
     )
-    f0, f1, f2, slot, net = pl.pallas_call(
+    below = lax.ppermute(bricks[7, :128], "slab", [(i, i + 1) for i in range(n_slab - 1)])
+    above = lax.ppermute(bricks[0, :128], "slab", [(i + 1, i) for i in range(n_slab - 1)])
+    f0, f1, f2, slot, summed = pl.pallas_call(
         functools.partial(brick_kernel, width=256, group=8),
         out_shape=(
             square, square, square,
             jax.ShapeDtypeStruct((256, 128), I32),
             jax.ShapeDtypeStruct((8, 3, 32, 512), F32),
         ),
-        in_specs=[smem] + [hbm] * 6,
-        out_specs=(vmem,) * 4 + (hbm,),
-        scratch_shapes=[
-            pltpu.VMEM((256, 128), I32),
-            pltpu.VMEM((256, 128), F32),
-            pltpu.VMEM((256, 128), F32),
-            pltpu.VMEM((256, 128), F32),
-            pltpu.VMEM((256, 128), F32),
-            pltpu.VMEM((8, 136, 512), F32),
-            pltpu.VMEM((8, 3, 32, 512), F32),
-            pltpu.VMEM((10, 4, 48, 512), F32),
-            pltpu.VMEM((8, 192, 256), BF16),
-            pltpu.VMEM((8, 144, 256), F32),
-            pltpu.SemaphoreType.DMA((6,)),
-            pltpu.SemaphoreType.DMA((4,)),
-        ],
+        in_specs=[smem] + [vmem] * 6,
+        out_specs=(vmem,) * 5,
+        scratch_shapes=[pltpu.VMEM((8, 192, 256), BF16), pltpu.VMEM((8, 144, 256), F32)],
         compiler_params=params,
+        cost_estimate=pl.CostEstimate(flops=30_000_000_000, bytes_accessed=6_000_000, transcendentals=0),
         name="brick_forces",
     )(starts, *[part.reshape(256, 128) for part in ordered], bricks)
-
+    net = pl.pallas_call(
+        viscous_kernel,
+        out_shape=jax.ShapeDtypeStruct((8, 3, 32, 512), F32),
+        in_specs=[vmem] * 4,
+        out_specs=vmem,
+        scratch_shapes=[pltpu.VMEM((10, 4, 48, 512), F32)],
+        compiler_params=params,
+        name="viscous",
+    )(bricks, below, above, summed)
+
+    slot, f0, f1, f2, net = lax.optimization_barrier((slot, f0, f1, f2, net))
     returned = lax.all_to_all(net, "brick", split_axis=0, concat_axis=0, tiled=True)
     back = lax.sort([part.reshape(-1) for part in (slot, f0, f1, f2)], num_keys=1, is_stable=False)
     slot_force = jnp.stack(back[1:])
-    slot_force, next_velocity, next_porosity = lax.optimization_barrier(
-        (slot_force, next_velocity, next_porosity)
-    )
-    brick = lax.axis_index("brick")
-    face = 0.5 * (porosity + next_porosity) * (next_velocity - fluid_velocity)
-    face = jnp.where((brick == 0) | (brick == n_brick - 1), face, 0.0)
     returned = jnp.swapaxes(returned, 0, 1).reshape(fluid_velocity.shape)
-    new_velocity = fluid_velocity + time_step * (returned + face) / porosity
+    new_velocity = fluid_velocity + time_step * returned / porosity
     return (new_velocity, slot_force)
 
 

time: 137 us -> 120 us (0.88)
  waiting for transfers between devices: 15.5 us -> 8.24 us
  other arithmetic: 45.4 us -> 42.1 us
  Pallas kernels: 52.2 us -> 49.1 us
  starting transfers between devices: 19.1 us -> 16.5 us
    ppermute x2, waiting for transfers between devices: 15.5 us -> 0.01 us  [the longest x1 0.01 us: per_device(): lax.ppermute(bricks[7, :128], 'slab', [(i, i + 1) for i in range(n_slab -...]
    pallas_call x1, Pallas kernels: 19.3 us -> 13.9 us  [per_device(): pl.pallas_call(functools.partial(brick_kernel, width=256, group=8), out_s...]
    all_to_all x1, waiting for transfers between devices: 0.01 us -> 5.07 us  [per_device(): lax.all_to_all(staged, 'brick', split_axis=0, concat_axis=0, tiled=True)]
    ppermute x2, starting transfers between devices: 9.97 us -> 6.46 us  [the longest x1 4.54 us: per_device(): lax.ppermute(bricks[0, :128], 'slab', [(i + 1, i) for i in range(n_slab -...]
    all_to_all x1, waiting for transfers between devices: 0.01 us -> 3.17 us  [per_device(): lax.all_to_all(net, 'brick', split_axis=0, concat_axis=0, tiled=True)]
    pallas_call x0 -> x1, Pallas kernels: none -> 2.3 us  [per_device(): pl.pallas_call(viscous_kernel, out_shape=jax.ShapeDtypeStruct((8, 3, 32,...]
    sort x1, other arithmetic: 24.3 us -> 22.5 us  [per_device(): lax.sort([part.reshape(-1) for part in (key, drag, p0, p1, p2)], num_keys...]
    add x1, other arithmetic: 3.23 us -> 1.57 us  [per_device(): new_velocity = fluid_velocity + time_step * returned / porosity]
  transfers between devices with their start and end apart: 4 -> 4, of which waited for: 1 -> 2; matrix products, arithmetic and copies ran while one was open for 31% -> 34% of each run, Pallas kernels for 14% -> 12%
where the time goes in v7:
time: 120 us; the launch traced here: 119 us
  Pallas kernels  49.1 us (41%)
  other arithmetic  42.1 us (35%)
  starting transfers between devices  16.5 us (14%)
  waiting for transfers between devices  8.24 us (7%)
  local copies, waits for them, and re-layouts  2.69 us (2%)
    pallas_call x1, Pallas kernels, per_device(): pl.pallas_call(functools.partial(exchange_kernel, cap=cap, group=8), out_...  32.9 us
    sort x1, other arithmetic, per_device(): lax.sort([part.reshape(-1) for part in (key, drag, p0, p1, p2)], num_keys...  22.5 us
    sort x1, other arithmetic, per_device(): lax.sort([part.reshape(-1) for part in (slot, f0, f1, f2)], num_keys=1, i...  16.6 us
    pallas_call x1, Pallas kernels, per_device(): pl.pallas_call(functools.partial(brick_kernel, width=256, group=8), out_s...  13.9 us
    all_to_all x1, starting transfers between devices, per_device(): lax.all_to_all(staged, 'brick', split_axis=0, concat_axis=0, tiled=True)  5.23 us
    all_to_all x1, waiting for transfers between devices, per_device(): lax.all_to_all(staged, 'brick', split_axis=0, concat_axis=0, tiled=True)  5.07 us
    all_to_all x1, starting transfers between devices, per_device(): lax.all_to_all(net, 'brick', split_axis=0, concat_axis=0, tiled=True)  4.76 us
    ppermute x1, starting transfers between devices, per_device(): lax.ppermute(bricks[0, :128], 'slab', [(i + 1, i) for i in range(n_slab -...  4.54 us
  transfers between devices with their start and end apart: 4, of which 2 were waited for; matrix products, arithmetic and copies ran while one was open for 34% of the time, Pallas kernels for 12%

profile of v7, /device:TPU:8, one launch (start us, length us, event | category | flops | bytes accessed | tf_op | source)
XLA Modules:
  0.0 119.3 jit_solution(2026411475788197345)
XLA Ops:
  0.6 32.9 %exchange.1 = (f32[8,136,512]{2,1,0:T(8,128)}, s32[33]{0:T(128)}, s32[256,128]{1,0:T(8,128)}, f32[256,128]{1,0:T(8,128)}, f32[256,128]{1,0:T(8,128)}, /*index=5*/f32[256,128]{1,0:T(8,128)}, f32[256,128]{1,0:T(8,128)}) custom-call(s32[128]{0:T(128)} %counts_ref.1, f32[3,16384]{1,0:T(4,128)} %pv_hbm.1, f32[128,128]{1,0:T(8,128)} %bitcast.58, ...), custom_call_target="tpu_custom_call" | custom-call | tf_op jit(solution)/shard_map/exchange/pallas_call | solution.py:317
  33.5 0.0 copy-start.4
  33.5 0.0 copy-start.5
  33.6 0.0 copy-start.6
  33.6 0.0 copy-start.7
  33.6 0.0 copy-start.8
  33.6 5.2 %all-to-all-start = ((f32[8,136,512]{2,1,0:T(8,128)}), f32[8,136,512]{2,1,0:T(8,128)S(1)}, u32[]{:S(2)}, u32[]{:S(2)}) async-start(f32[8,136,512]{2,1,0:T(8,128)} %get-tuple-element.38), calls=%async_computation | async-start | bytes 4456448 | tf_op jit(solution)/shard_map/all_to_all | solution.py:358
  38.8 0.0 copy-done.4
  38.8 0.0 copy-done.5
  38.9 0.0 copy-done.6
  38.9 0.0 copy-done.7
  38.9 22.5 %sort.60 = (s32[32768]{0:T(1024)S(1)}, f32[32768]{0:T(1024)S(1)}, f32[32768]{0:T(1024)S(1)}, f32[32768]{0:T(1024)S(1)}, f32[32768]{0:T(1024)S(1)}) sort(s32[32768]{0:T(1024)S(1)} %bitcast.50, f32[32768]{0:T(1024)S(1)} %bitcast.54, f32[32768]{0:T(1024)S(1)} %bitcast.51, f32[32768]{0:T(1024)S(1)} %bitcast.52, f32[32768]{0:T(1024)S(1)} %bitcast.53), dimensions={0}, to_apply=%region_0.0 | sort | flops 491520 | bytes 1310720 | tf_op jit(solution)/shard_map/sort | solution.py:359
  61.4 5.1 %all-to-all-done.bricks_ref = f32[8,136,512]{2,1,0:T(8,128)S(1)} async-done(((f32[8,136,512]{2,1,0:T(8,128)}), f32[8,136,512]{2,1,0:T(8,128)S(1)}, u32[]{:S(2)}, u32[]{:S(2)}) %all-to-all-start) | async-done | bytes 2228256 | tf_op jit(solution)/shard_map/all_to_all | solution.py:358
  66.5 1.9 %collective-permute-start = (f32[128,512]{1,0:T(8,128)S(1)}, f32[128,512]{1,0:T(8,128)S(1)}, u32[]{:S(2)}, u32[]{:S(2)}) collective-permute-start(f32[128,512]{1,0:T(8,128)S(1)} %get-tuple-element.55), channel_id=1, source_target_pairs={{0,8},{8,16},{16,24},{24,32},{32,40},{40,48},{48,56},{56,64},{64,7... | collective-permute-start | bytes 786440 | tf_op jit(solution)/shard_map/ppermute | solution.py:362
  68.4 4.5 %collective-permute-start.1 = (f32[128,512]{1,0:T(8,128)S(1)}, f32[128,512]{1,0:T(8,128)S(1)}, u32[]{:S(2)}, u32[]{:S(2)}) collective-permute-start(f32[128,512]{1,0:T(8,128)S(1)} %get-tuple-element.54), channel_id=1, source_target_pairs={{8,0},{16,8},{24,16},{32,24},{40,32},{48,40},{56,48},{64,56},{72,6... | collective-permute-start | bytes 786440 | tf_op jit(solution)/shard_map/ppermute | solution.py:363
  73.0 13.9 %brick_forces.1 = (f32[256,128]{1,0:T(8,128)S(1)}, f32[256,128]{1,0:T(8,128)S(1)}, f32[256,128]{1,0:T(8,128)S(1)}, s32[256,128]{1,0:T(8,128)S(1)}, f32[8,3,32,512]{3,2,1,0:T(8,128)S(1)}) custom-call(s32[33]{0:T(128)S(1)} %copy-done.1, s32[256,128]{1,0:T(8,128)S(1)} %bitcast.39, f32[256,128]{1,0:T(8,128)S(1)} %bitcast.40, f32[256,128]{1,0:T(8,128)S(1)} %bitcast.41, ...), custom_call_target="tpu_custom_call" | custom-call | flops 30000001024 | bytes 6000000 | tf_op jit(solution)/shard_map/brick_forces/pallas_call | solution.py:364
  86.8 0.0 collective-permute-done.below_ref
  86.8 0.0 collective-permute-done.1.above_ref
  86.8 2.3 %viscous.1 = f32[8,3,32,512]{3,2,1,0:T(8,128)S(1)} custom-call(f32[8,136,512]{2,1,0:T(8,128)S(1)} %all-to-all-done.bricks_ref, f32[128,512]{1,0:T(8,128)S(1)} %collective-permute-done.below_ref, f32[128,512]{1,0:T(8,128)S(1)} %collective-permute-done.1.above_ref, f32[8,3,32,512]{3,2,1,0:T(8,128)S(1)} %get-tuple-element.43.sum_ref), custom_call_target="tpu_custom_call" | custom-call | tf_op jit(solution)/shard_map/viscous/pallas_call | solution.py:378
  89.2 0.0 copy-start
  89.2 1.1 copy-done
  90.3 4.8 %all-to-all-start.1 = ((f32[8,3,32,512]{3,2,1,0:T(8,128)}), f32[8,3,32,512]{3,2,1,0:T(8,128)S(1)}, u32[]{:S(2)}, u32[]{:S(2)}) async-start(f32[8,3,32,512]{3,2,1,0:T(8,128)} %copy-done), calls=%async_computation.1 | async-start | bytes 3145728 | tf_op jit(solution)/shard_map/all_to_all | solution.py:389
  95.1 16.6 %sort.61 = (s32[32768]{0:T(1024)}, f32[32768]{0:T(1024)S(1)}, f32[32768]{0:T(1024)S(1)}, f32[32768]{0:T(1024)S(1)}) sort(s32[32768]{0:T(1024)S(1)} %bitcast.38, f32[32768]{0:T(1024)S(1)} %bitcast.35, f32[32768]{0:T(1024)S(1)} %bitcast.36, f32[32768]{0:T(1024)S(1)} %bitcast.37), dimensions={0}, to_apply=%region_1.0 | sort | flops 491520 | bytes 1048576 | tf_op jit(solution)/shard_map/sort | solution.py:390
  111.7 1.1 pad_maximum_fusion
  112.8 3.2 %all-to-all-done.1 = f32[8,3,32,512]{3,2,1,0:T(8,128)S(1)} async-done(((f32[8,3,32,512]{3,2,1,0:T(8,128)}), f32[8,3,32,512]{3,2,1,0:T(8,128)S(1)}, u32[]{:S(2)}, u32[]{:S(2)}) %all-to-all-start.1) | async-done | bytes 1572896 | tf_op jit(solution)/shard_map/all_to_all | solution.py:389
  116.0 0.2 multiply_bitcast_fusion
  116.3 0.0 copy-start.2
  116.3 0.0 copy-start.3
  116.3 0.1 copy.9
  116.4 1.3 %copy-done.2 = f32[3,1,256,512]{3,2,1,0:T(8,128)S(1)} copy-done((f32[3,1,256,512]{3,2,1,0:T(8,128)S(1)}, f32[3,1,256,512]{3,2,1,0:T(8,128)}, u32[]{:S(2)}) %copy-start.2) | copy-done | bytes 1572888
  117.7 0.1 copy-done.3
  117.8 1.6 %fusion = f32[3,1,256,512]{3,2,0,1:T(8,128)} fusion(f32[3,8,32,512]{3,2,1,0:T(8,128)S(1)} %copy.9, f32[3,1,256,512]{3,2,1,0:T(8,128)S(1)} %copy-done.2, f32[256,512]{1,0:T(8,128)S(1)} %bitcast.46), kind=kLoop, calls=%fused_computation.1 | loop fusion | flops 786432 | bytes 5242880 | tf_op jit(solution)/shard_map/add | solution.py:393
  (4 shorter events, 0.0 us)
Async XLA Ops:
  33.5 5.3 %copy-start.4 = (s32[256,128]{1,0:T(8,128)S(1)}, s32[256,128]{1,0:T(8,128)}, u32[]{:S(2)}) copy-start(s32[256,128]{1,0:T(8,128)} %get-tuple-element.28) | copy-start | bytes 393220
  33.5 5.3 %copy-start.5 = (f32[256,128]{1,0:T(8,128)S(1)}, f32[256,128]{1,0:T(8,128)}, u32[]{:S(2)}) copy-start(f32[256,128]{1,0:T(8,128)} %get-tuple-element.30) | copy-start | bytes 393220
  33.6 5.3 %copy-start.6 = (f32[256,128]{1,0:T(8,128)S(1)}, f32[256,128]{1,0:T(8,128)}, u32[]{:S(2)}) copy-start(f32[256,128]{1,0:T(8,128)} %get-tuple-element.31) | copy-start | bytes 393220
  33.6 5.3 %copy-start.7 = (f32[256,128]{1,0:T(8,128)S(1)}, f32[256,128]{1,0:T(8,128)}, u32[]{:S(2)}) copy-start(f32[256,128]{1,0:T(8,128)} %get-tuple-element.32) | copy-start | bytes 393220
  33.6 5.3 %copy-start.8 = (f32[256,128]{1,0:T(8,128)S(1)}, f32[256,128]{1,0:T(8,128)}, u32[]{:S(2)}) copy-start(f32[256,128]{1,0:T(8,128)} %get-tuple-element.29) | copy-start | bytes 393220
  33.6 32.8 %all-to-all-start = ((f32[8,136,512]{2,1,0:T(8,128)}), f32[8,136,512]{2,1,0:T(8,128)S(1)}, u32[]{:S(2)}, u32[]{:S(2)}) async-start(f32[8,136,512]{2,1,0:T(8,128)} %get-tuple-element.38), calls=%async_computation | async-start | bytes 4456448 | tf_op jit(solution)/shard_map/all_to_all | solution.py:358
  38.8 34.1 %copy-start.1 = (s32[33]{0:T(128)S(1)}, s32[33]{0:T(128)}, u32[]{:S(2)}) copy-start(s32[33]{0:T(128)} %get-tuple-element.27.starts_ref) | copy-start | bytes 400
  66.5 20.4 %collective-permute-start = (f32[128,512]{1,0:T(8,128)S(1)}, f32[128,512]{1,0:T(8,128)S(1)}, u32[]{:S(2)}, u32[]{:S(2)}) collective-permute-start(f32[128,512]{1,0:T(8,128)S(1)} %get-tuple-element.55), channel_id=1, source_target_pairs={{0,8},{8,16},{16,24},{24,32},{32,40},{40,48},{48,56},{56,64},{64,7... | collective-permute-start | bytes 786440 | tf_op jit(solution)/shard_map/ppermute | solution.py:362
  68.4 18.4 %collective-permute-start.1 = (f32[128,512]{1,0:T(8,128)S(1)}, f32[128,512]{1,0:T(8,128)S(1)}, u32[]{:S(2)}, u32[]{:S(2)}) collective-permute-start(f32[128,512]{1,0:T(8,128)S(1)} %get-tuple-element.54), channel_id=1, source_target_pairs={{8,0},{16,8},{24,16},{32,24},{40,32},{48,40},{56,48},{64,56},{72,6... | collective-permute-start | bytes 786440 | tf_op jit(solution)/shard_map/ppermute | solution.py:363
  89.2 1.1 copy-start
  90.3 25.7 %all-to-all-start.1 = ((f32[8,3,32,512]{3,2,1,0:T(8,128)}), f32[8,3,32,512]{3,2,1,0:T(8,128)S(1)}, u32[]{:S(2)}, u32[]{:S(2)}) async-start(f32[8,3,32,512]{3,2,1,0:T(8,128)} %copy-done), calls=%async_computation.1 | async-start | bytes 3145728 | tf_op jit(solution)/shard_map/all_to_all | solution.py:389
  116.3 1.4 %copy-start.2 = (f32[3,1,256,512]{3,2,1,0:T(8,128)S(1)}, f32[3,1,256,512]{3,2,1,0:T(8,128)}, u32[]{:S(2)}) copy-start(f32[3,1,256,512]{3,2,1,0:T(8,128)} %param.7) | copy-start | bytes 4718596
  116.3 1.5 %copy-start.3 = (f32[1,256,512]{2,1,0:T(8,128)S(1)}, f32[1,256,512]{2,1,0:T(8,128)}, u32[]{:S(2)}) copy-start(f32[1,256,512]{2,1,0:T(8,128)} %param.8) | copy-start | bytes 1572868

commit v8 on v7

--- a/solution.py
+++ b/solution.py
@@ -22,9 +22,10 @@
 
 def exchange_kernel(
     counts_ref, pv_hbm, coef_hbm, rows_hbm, u_hbm, frac_hbm, cell_hbm,
-    stage_hbm, starts_ref, key_ref, p0_ref, p1_ref, p2_ref, drag_ref,
+    stage_hbm, rest_ref, starts_ref, key_ref, p0_ref, p1_ref, p2_ref, drag_ref,
     pv_ref, coef_ref, rows_ref, u_ref, frac_ref, cell_ref, particles,
-    stage, table, packed, arrived_ref, load_sem, stage_sem, part_send, part_recv, *, cap, group,
+    stage, table, packed, arrived_ref, load_sem, stage_sem, part_send, part_recv, rest_send, rest_recv,
+    *, cap, group,
 ):
     pairs = (
         (u_hbm, u_ref), (frac_hbm, frac_ref), (pv_hbm, pv_ref), (coef_hbm, coef_ref), (rows_hbm, rows_ref),
@@ -62,7 +63,7 @@
                 stage[b - 1, 132 + c : 133 + c, :] = field[0:1]
         stage[0, 128 + c : 129 + c, :] = jnp.zeros((1, 512), F32)
         stage[7, 132 + c : 133 + c, :] = jnp.zeros((1, 512), F32)
-    saved = pltpu.make_async_copy(stage, stage_hbm, stage_sem)
+    saved = pltpu.make_async_copy(stage.at[:, pl.ds(0, 96)], stage_hbm, stage_sem)
     saved.start()
     for load in loads[2:]:
         load.wait()
@@ -75,8 +76,6 @@
         halves = jnp.concatenate([whole[:64], whole[64:]], axis=1)
         for p, piece in enumerate(split3(halves)):
             table[p * 256 + c * 64 : p * 256 + (c + 1) * 64, :] = piece
-
-    pl.semaphore_wait(barrier, devices - 1)
 
     r_iota = lax.broadcasted_iota(I32, (256, cap), 0).astype(F32).astype(BF16)
     one, zero = jnp.ones((), BF16), jnp.zeros((), BF16)
@@ -114,16 +113,34 @@
             device_id=coords(t), device_id_type=mesh_id,
         )
 
+    def other(j):
+        to = (brick + j) % n_brick
+        return pltpu.make_async_remote_copy(
+            src_ref=stage.at[to, pl.ds(96, 40)], dst_ref=rest_ref.at[brick], send_sem=rest_send.at[to],
+            recv_sem=rest_recv.at[brick], device_id=(slab, to), device_id_type=mesh_id,
+        )
+
+    def fill(i, carry):
+        to = [(me + 1 + i * group + j) % devices for j in range(group)]
+        for t, value in zip(to, pick(to)):
+            packed[t] = value
+        return carry
+
+    def send(i, carry):
+        for j in range(group):
+            parcel((me + 1 + i * group + j) % devices).start()
+        return carry
+
     def some(i, carry):
-        to = [(me + 1 + i * group + j) % devices for j in range(group)]
-        picked = pick(to)
-        for t, value in zip(to, picked):
-            packed[t] = value
-        for t in to:
-            parcel(t).start()
-        return carry
-
-    lax.fori_loop(0, devices // group - 1, some, 0)
+        return send(i, fill(i, carry))
+
+    rest_ref[brick] = stage[brick, 96:136]
+    lax.fori_loop(0, 2, fill, 0)
+    pl.semaphore_wait(barrier, devices - 1)
+    for j in range(1, 8):
+        other(j).start()
+    lax.fori_loop(0, 2, send, 0)
+    lax.fori_loop(2, devices // group - 1, some, 0)
     to = [(me + 1 + devices - group + j) % devices for j in range(group)]
     picked = pick(to)
     for t, value in zip(to[:-1], picked):
@@ -139,6 +156,13 @@
     rest.wait_send()
     rest.wait_recv()
     saved.wait()
+    for j in range(1, 8):
+        other(j).wait_send()
+        source = (brick + j) % n_brick
+        pltpu.make_async_remote_copy(
+            src_ref=stage.at[source, pl.ds(96, 40)], dst_ref=rest_ref.at[source], send_sem=rest_send.at[source],
+            recv_sem=rest_recv.at[source], device_id=(slab, source), device_id_type=mesh_id,
+        ).wait_recv()
 
     tiles = cell_ref.shape[0] // 8
     place = lax.broadcasted_iota(I32, (8, 128), 0) * 128 + lax.broadcasted_iota(I32, (8, 128), 1)
@@ -167,7 +191,7 @@
 
 
 def brick_kernel(
-    starts_ref, key_ref, coef_ref, p0_ref, p1_ref, p2_ref, bricks_ref,
+    starts_ref, key_ref, coef_ref, p0_ref, p1_ref, p2_ref, bricks_ref, rest_ref,
     f0_ref, f1_ref, f2_ref, slot_ref, sum_ref, table, deposit, *, width, group,
 ):
     rows = key_ref.shape[0]
@@ -191,7 +215,8 @@
             z, q = b // 4, b % 4
             x8 = pl.multiple_of(q * 8, 8)
             for c in range(4):
-                centre = bricks_ref[z, pl.ds(pl.multiple_of(c * 32 + x8, 8), 8), :]
+                ref, at = (rest_ref, x8) if c == 3 else (bricks_ref, pl.multiple_of(c * 32 + x8, 8))
+                centre = ref[z, pl.ds(at, 8), :]
                 for p, piece in enumerate(split3(centre)):
                     at = p * 64 + c * 16
                     table[i, at : at + 16, :] = jnp.concatenate([piece[:, :256], piece[:, 256:]], axis=0)
@@ -270,13 +295,13 @@
     lax.fori_loop(0, 32 // group, blocks, 0)
 
 
-def viscous_kernel(bricks_ref, below_ref, above_ref, sum_ref, net_ref, padded):
+def viscous_kernel(bricks_ref, rest_ref, below_ref, above_ref, sum_ref, net_ref, padded):
     for c in range(4):
         own = slice(c * 32, (c + 1) * 32)
         for z in range(8):
-            padded[z + 1, c, 8:40, :] = bricks_ref[z, own, :]
-            padded[z + 1, c, 7:8, :] = bricks_ref[z, 128 + c : 129 + c, :]
-            padded[z + 1, c, 40:41, :] = bricks_ref[z, 132 + c : 133 + c, :]
+            padded[z + 1, c, 8:40, :] = rest_ref[z, 0:32, :] if c == 3 else bricks_ref[z, own, :]
+            padded[z + 1, c, 7:8, :] = rest_ref[z, 32 + c : 33 + c, :]
+            padded[z + 1, c, 40:41, :] = rest_ref[z, 36 + c : 37 + c, :]
         padded[0, c, 8:40, :] = below_ref[own, :]
         padded[9, c, 8:40, :] = above_ref[own, :]
     y_iota = lax.broadcasted_iota(I32, (8, 512), 1)
@@ -314,16 +339,17 @@
     params = pltpu.CompilerParams(vmem_limit_bytes=32 << 20)
     square = jax.ShapeDtypeStruct((256, 128), F32)
     hbm = pl.BlockSpec(memory_space=pl.ANY)
-    staged, starts, key, p0, p1, p2, drag = pl.pallas_call(
+    staged, others, starts, key, p0, p1, p2, drag = pl.pallas_call(
         functools.partial(exchange_kernel, cap=cap, group=8),
         out_shape=(
-            jax.ShapeDtypeStruct((8, 136, 512), F32),
+            jax.ShapeDtypeStruct((8, 96, 512), F32),
+            jax.ShapeDtypeStruct((8, 40, 512), F32),
             jax.ShapeDtypeStruct((33,), I32),
             jax.ShapeDtypeStruct((256, 128), I32),
             square, square, square, square,
         ),
         in_specs=[smem] + [hbm] * 6,
-        out_specs=(hbm, smem) + (vmem,) * 5,
+        out_specs=(hbm, vmem, smem) + (vmem,) * 5,
         scratch_shapes=[
             pltpu.VMEM((3, 16384), F32),
             pltpu.VMEM((128, 128), F32),
@@ -340,6 +366,8 @@
             pltpu.SemaphoreType.DMA,
             pltpu.SemaphoreType.DMA,
             pltpu.SemaphoreType.DMA,
+            pltpu.SemaphoreType.DMA((8,)),
+            pltpu.SemaphoreType.DMA((8,)),
         ],
         compiler_params=pltpu.CompilerParams(
             vmem_limit_bytes=60 << 20, collective_id=0, has_side_effects=True
@@ -359,8 +387,9 @@
     ordered = lax.sort(
         [part.reshape(-1) for part in (key, drag, p0, p1, p2)], num_keys=1, is_stable=False
     )
-    below = lax.ppermute(bricks[7, :128], "slab", [(i, i + 1) for i in range(n_slab - 1)])
-    above = lax.ppermute(bricks[0, :128], "slab", [(i + 1, i) for i in range(n_slab - 1)])
+    top, bottom = [jnp.concatenate([bricks[z], others[z, :32]]) for z in (7, 0)]
+    below = lax.ppermute(top, "slab", [(i, i + 1) for i in range(n_slab - 1)])
+    above = lax.ppermute(bottom, "slab", [(i + 1, i) for i in range(n_slab - 1)])
     f0, f1, f2, slot, summed = pl.pallas_call(
         functools.partial(brick_kernel, width=256, group=8),
         out_shape=(
@@ -368,22 +397,22 @@
             jax.ShapeDtypeStruct((256, 128), I32),
             jax.ShapeDtypeStruct((8, 3, 32, 512), F32),
         ),
-        in_specs=[smem] + [vmem] * 6,
+        in_specs=[smem] + [vmem] * 7,
         out_specs=(vmem,) * 5,
         scratch_shapes=[pltpu.VMEM((8, 192, 256), BF16), pltpu.VMEM((8, 144, 256), F32)],
         compiler_params=params,
         cost_estimate=pl.CostEstimate(flops=30_000_000_000, bytes_accessed=6_000_000, transcendentals=0),
         name="brick_forces",
-    )(starts, *[part.reshape(256, 128) for part in ordered], bricks)
+    )(starts, *[part.reshape(256, 128) for part in ordered], bricks, others)
     net = pl.pallas_call(
         viscous_kernel,
         out_shape=jax.ShapeDtypeStruct((8, 3, 32, 512), F32),
-        in_specs=[vmem] * 4,
+        in_specs=[vmem] * 5,
         out_specs=vmem,
         scratch_shapes=[pltpu.VMEM((10, 4, 48, 512), F32)],
         compiler_params=params,
         name="viscous",
-    )(bricks, below, above, summed)
+    )(bricks, others, below, above, summed)
 
     slot, f0, f1, f2, net = lax.optimization_barrier((slot, f0, f1, f2, net))
     returned = lax.all_to_all(net, "brick", split_axis=0, concat_axis=0, tiled=True)

time: 120 us -> 113 us (0.942)
  waiting for transfers between devices: 8.24 us -> 0.01 us
  starting transfers between devices: 16.5 us -> 24.3 us
  Pallas kernels: 49.1 us -> 43.1 us
    all_to_all x1, starting transfers between devices: 4.76 us -> 13.1 us  [per_device(): lax.all_to_all(net, 'brick', split_axis=0, concat_axis=0, tiled=True)]
    pallas_call x1, Pallas kernels: 13.9 us -> 7.87 us  [per_device(): pl.pallas_call(functools.partial(brick_kernel, width=256, group=8), out_s...]
    all_to_all x1, waiting for transfers between devices: 5.07 us -> 0.01 us  [per_device(): lax.all_to_all(staged, 'brick', split_axis=0, concat_axis=0, tiled=True)]
    all_to_all x1, waiting for transfers between devices: 3.17 us -> 0.01 us  [per_device(): lax.all_to_all(net, 'brick', split_axis=0, concat_axis=0, tiled=True)]
  transfers between devices with their start and end apart: 4 -> 4, of which waited for: 2 -> 0; matrix products, arithmetic and copies ran while one was open for 34% -> 36% of each run, Pallas kernels for 12% -> 7%
where the time goes in v8:
time: 113 us; the launch traced here: 112 us
  Pallas kernels  43.1 us (38%)
  other arithmetic  42.1 us (37%)
  starting transfers between devices  24.3 us (22%)
  local copies, waits for them, and re-layouts  1.56 us (1%)
    pallas_call x1, Pallas kernels, per_device(): pl.pallas_call(functools.partial(exchange_kernel, cap=cap, group=8), out_...  31.8 us
    sort x1, other arithmetic, per_device(): lax.sort([part.reshape(-1) for part in (key, drag, p0, p1, p2)], num_keys...  22.5 us
    sort x1, other arithmetic, per_device(): lax.sort([part.reshape(-1) for part in (slot, f0, f1, f2)], num_keys=1, i...  16.6 us
    all_to_all x1, starting transfers between devices, per_device(): lax.all_to_all(net, 'brick', split_axis=0, concat_axis=0, tiled=True)  13.1 us
    pallas_call x1, Pallas kernels, per_device(): pl.pallas_call(functools.partial(brick_kernel, width=256, group=8), out_s...  7.87 us
    all_to_all x1, starting transfers between devices, per_device(): lax.all_to_all(staged, 'brick', split_axis=0, concat_axis=0, tiled=True)  4.66 us
    ppermute x1, starting transfers between devices, per_device(): lax.ppermute(bottom, 'slab', [(i + 1, i) for i in range(n_slab - 1)])  4.54 us
    pallas_call x1, Pallas kernels, per_device(): pl.pallas_call(viscous_kernel, out_shape=jax.ShapeDtypeStruct((8, 3, 32,...  3.48 us
  transfers between devices with their start and end apart: 4, of which 0 were waited for; matrix products, arithmetic and copies ran while one was open for 36% of the time, Pallas kernels for 7%

profile of v8, /device:TPU:8, one launch (start us, length us, event | category | flops | bytes accessed | tf_op | source)
XLA Modules:
  0.0 111.9 jit_solution(9695290940328211516)
XLA Ops:
  0.6 31.8 %exchange.1 = (f32[8,96,512]{2,1,0:T(8,128)}, f32[8,40,512]{2,1,0:T(8,128)}, s32[33]{0:T(128)}, s32[256,128]{1,0:T(8,128)}, f32[256,128]{1,0:T(8,128)}, /*index=...) custom-call(s32[128]{0:T(128)} %counts_ref.1, f32[3,16384]{1,0:T(4,128)} %pv_hbm.1, f32[128,128]{1,0:T(8,128)} %bitcast.62, ...), custom_call_target="tpu_custom_call" | custom-call | tf_op jit(solution)/shard_map/exchange/pallas_call | solution.py:342
  32.4 0.0 copy-start.4
  32.4 0.0 copy-start.5
  32.4 0.0 copy-start.6
  32.4 0.0 copy-start.7
  32.4 0.0 copy-start.8
  32.5 4.7 %all-to-all-start = ((f32[8,96,512]{2,1,0:T(8,128)}), f32[8,96,512]{2,1,0:T(8,128)S(1)}, u32[]{:S(2)}, u32[]{:S(2)}) async-start(f32[8,96,512]{2,1,0:T(8,128)} %get-tuple-element.39), calls=%async_computation | async-start | bytes 3145728 | tf_op jit(solution)/shard_map/all_to_all | solution.py:386
  37.1 0.0 copy-done.4
  37.1 0.0 copy-done.5
  37.2 0.0 copy-done.6
  37.2 0.0 copy-done.7
  37.2 0.0 copy-done.8
  37.2 22.5 %sort.60 = (s32[32768]{0:T(1024)S(1)}, f32[32768]{0:T(1024)S(1)}, f32[32768]{0:T(1024)S(1)}, f32[32768]{0:T(1024)S(1)}, f32[32768]{0:T(1024)S(1)}) sort(s32[32768]{0:T(1024)S(1)} %bitcast.54, f32[32768]{0:T(1024)S(1)} %bitcast.58, f32[32768]{0:T(1024)S(1)} %bitcast.55, f32[32768]{0:T(1024)S(1)} %bitcast.56, f32[32768]{0:T(1024)S(1)} %bitcast.57), dimensions={0}, to_apply=%region_0.0 | sort | flops 491520 | bytes 1310720 | tf_op jit(solution)/shard_map/sort | solution.py:387
  59.7 0.0 all-to-all-done.bricks_ref
  59.8 1.9 %collective-permute-start = (f32[128,512]{1,0:T(8,128)S(1)}, f32[128,512]{1,0:T(8,128)S(1)}, u32[]{:S(2)}, u32[]{:S(2)}) collective-permute-start(f32[128,512]{1,0:T(8,128)S(1)} %pad_maximum_fusion.1), channel_id=1, source_target_pairs={{0,8},{8,16},{16,24},{24,32},{32,40},{40,48},{48,56},{56,64},{64,7... | collective-permute-start | bytes 786440 | tf_op jit(solution)/shard_map/ppermute | solution.py:391
  61.7 4.5 %collective-permute-start.1 = (f32[128,512]{1,0:T(8,128)S(1)}, f32[128,512]{1,0:T(8,128)S(1)}, u32[]{:S(2)}, u32[]{:S(2)}) collective-permute-start(f32[128,512]{1,0:T(8,128)S(1)} %pad_maximum_fusion.2), channel_id=1, source_target_pairs={{8,0},{16,8},{24,16},{32,24},{40,32},{48,40},{56,48},{64,56},{72,6... | collective-permute-start | bytes 786440 | tf_op jit(solution)/shard_map/ppermute | solution.py:392
  66.3 0.0 copy-done.1
  66.3 7.9 %brick_forces.1 = (f32[256,128]{1,0:T(8,128)S(1)}, f32[256,128]{1,0:T(8,128)S(1)}, f32[256,128]{1,0:T(8,128)S(1)}, s32[256,128]{1,0:T(8,128)S(1)}, f32[8,3,32,512]{3,2,1,0:T(8,128)S(1)}) custom-call(s32[33]{0:T(128)S(1)} %copy-done.1, s32[256,128]{1,0:T(8,128)S(1)} %bitcast.43, f32[256,128]{1,0:T(8,128)S(1)} %bitcast.44, f32[256,128]{1,0:T(8,128)S(1)} %bitcast.45, ...), custom_call_target="tpu_custom_call" | custom-call | flops 30000001024 | bytes 6000000 | tf_op jit(solution)/shard_map/brick_forces/pallas_call | solution.py:393
  74.2 0.0 collective-permute-done.below_ref
  74.2 0.0 collective-permute-done.1.above_ref
  74.2 3.5 %viscous.1 = f32[8,3,32,512]{3,2,1,0:T(8,128)} custom-call(f32[8,96,512]{2,1,0:T(8,128)S(1)} %all-to-all-done.bricks_ref, f32[8,40,512]{2,1,0:T(8,128)S(1)} %copy-done, f32[128,512]{1,0:T(8,128)S(1)} %collective-permute-done.below_ref, f32[128,512]{1,0:T(8,128)S(1)} %collective-permute-done.1.above_ref, f32[8,3,32,512]{3,2,1,0:T(8,128)S(1)} %get-tuple-element.45.sum_ref), custom_call_target="tpu_custom_call" | custom-call | tf_op jit(solution)/shard_map/viscous/pallas_call | solution.py:407
  77.7 13.1 %all-to-all-start.1 = ((f32[8,3,32,512]{3,2,1,0:T(8,128)}), f32[8,3,32,512]{3,2,1,0:T(8,128)S(1)}, u32[]{:S(2)}, u32[]{:S(2)}) async-start(f32[8,3,32,512]{3,2,1,0:T(8,128)} %viscous.1), calls=%async_computation.1 | async-start | bytes 3145728 | tf_op jit(solution)/shard_map/all_to_all | solution.py:418
  90.8 16.6 %sort.61 = (s32[32768]{0:T(1024)}, f32[32768]{0:T(1024)S(1)}, f32[32768]{0:T(1024)S(1)}, f32[32768]{0:T(1024)S(1)}) sort(s32[32768]{0:T(1024)S(1)} %bitcast.42, f32[32768]{0:T(1024)S(1)} %bitcast.39, f32[32768]{0:T(1024)S(1)} %bitcast.40, f32[32768]{0:T(1024)S(1)} %bitcast.41), dimensions={0}, to_apply=%region_1.0 | sort | flops 491520 | bytes 1048576 | tf_op jit(solution)/shard_map/sort | solution.py:419
  107.5 1.1 %pad_maximum_fusion = f32[3,32768]{1,0:T(4,128)} fusion(f32[1,32768]{1,0:T(1,128)S(1)} %bitcast.61, f32[1,32768]{1,0:T(1,128)S(1)} %bitcast.60, f32[1,32768]{1,0:T(1,128)S(1)} %bitcast.59), kind=kLoop, calls=%fused_computation.3 | loop fusion | flops 196608 | bytes 786432 | tf_op jit(solution)/shard_map/stack | solution.py:420
  108.6 0.0 all-to-all-done.1
  108.6 0.3 multiply_bitcast_fusion
  108.9 0.0 copy-start.2
  108.9 0.0 copy-start.3
  108.9 0.1 copy.9
  109.0 1.3 %copy-done.2 = f32[3,1,256,512]{3,2,1,0:T(8,128)S(1)} copy-done((f32[3,1,256,512]{3,2,1,0:T(8,128)S(1)}, f32[3,1,256,512]{3,2,1,0:T(8,128)}, u32[]{:S(2)}) %copy-start.2) | copy-done | bytes 1572888
  110.3 0.1 copy-done.3
  110.4 1.6 %fusion = f32[3,1,256,512]{3,2,0,1:T(8,128)} fusion(f32[3,8,32,512]{3,2,1,0:T(8,128)S(1)} %copy.9, f32[3,1,256,512]{3,2,1,0:T(8,128)S(1)} %copy-done.2, f32[256,512]{1,0:T(8,128)S(1)} %bitcast.50), kind=kLoop, calls=%fused_computation.1 | loop fusion | flops 786432 | bytes 5242880 | tf_op jit(solution)/shard_map/add | solution.py:422
  (7 shorter events, 0.1 us)
Async XLA Ops:
  32.4 4.7 %copy-start.4 = (s32[256,128]{1,0:T(8,128)S(1)}, s32[256,128]{1,0:T(8,128)}, u32[]{:S(2)}) copy-start(s32[256,128]{1,0:T(8,128)} %get-tuple-element.29) | copy-start | bytes 393220
  32.4 4.7 %copy-start.5 = (f32[256,128]{1,0:T(8,128)S(1)}, f32[256,128]{1,0:T(8,128)}, u32[]{:S(2)}) copy-start(f32[256,128]{1,0:T(8,128)} %get-tuple-element.31) | copy-start | bytes 393220
  32.4 4.7 %copy-start.6 = (f32[256,128]{1,0:T(8,128)S(1)}, f32[256,128]{1,0:T(8,128)}, u32[]{:S(2)}) copy-start(f32[256,128]{1,0:T(8,128)} %get-tuple-element.32) | copy-start | bytes 393220
  32.4 4.7 %copy-start.7 = (f32[256,128]{1,0:T(8,128)S(1)}, f32[256,128]{1,0:T(8,128)}, u32[]{:S(2)}) copy-start(f32[256,128]{1,0:T(8,128)} %get-tuple-element.33) | copy-start | bytes 393220
  32.4 4.7 %copy-start.8 = (f32[256,128]{1,0:T(8,128)S(1)}, f32[256,128]{1,0:T(8,128)}, u32[]{:S(2)}) copy-start(f32[256,128]{1,0:T(8,128)} %get-tuple-element.30) | copy-start | bytes 393220
  32.5 27.2 %copy-start = (f32[8,40,512]{2,1,0:T(8,128)S(1)}, f32[8,40,512]{2,1,0:T(8,128)}, u32[]{:S(2)}) copy-start(f32[8,40,512]{2,1,0:T(8,128)} %get-tuple-element.40.rest_ref) | copy-start | bytes 1966084
  32.5 27.2 %all-to-all-start = ((f32[8,96,512]{2,1,0:T(8,128)}), f32[8,96,512]{2,1,0:T(8,128)S(1)}, u32[]{:S(2)}, u32[]{:S(2)}) async-start(f32[8,96,512]{2,1,0:T(8,128)} %get-tuple-element.39), calls=%async_computation | async-start | bytes 3145728 | tf_op jit(solution)/shard_map/all_to_all | solution.py:386
  37.1 29.1 %copy-start.1 = (s32[33]{0:T(128)S(1)}, s32[33]{0:T(128)}, u32[]{:S(2)}) copy-start(s32[33]{0:T(128)} %get-tuple-element.28.starts_ref) | copy-start | bytes 400
  59.8 14.4 %collective-permute-start = (f32[128,512]{1,0:T(8,128)S(1)}, f32[128,512]{1,0:T(8,128)S(1)}, u32[]{:S(2)}, u32[]{:S(2)}) collective-permute-start(f32[128,512]{1,0:T(8,128)S(1)} %pad_maximum_fusion.1), channel_id=1, source_target_pairs={{0,8},{8,16},{16,24},{24,32},{32,40},{40,48},{48,56},{56,64},{64,7... | collective-permute-start | bytes 786440 | tf_op jit(solution)/shard_map/ppermute | solution.py:391
  61.7 12.5 %collective-permute-start.1 = (f32[128,512]{1,0:T(8,128)S(1)}, f32[128,512]{1,0:T(8,128)S(1)}, u32[]{:S(2)}, u32[]{:S(2)}) collective-permute-start(f32[128,512]{1,0:T(8,128)S(1)} %pad_maximum_fusion.2), channel_id=1, source_target_pairs={{8,0},{16,8},{24,16},{32,24},{40,32},{48,40},{56,48},{64,56},{72,6... | collective-permute-start | bytes 786440 | tf_op jit(solution)/shard_map/ppermute | solution.py:392
  77.7 30.9 %all-to-all-start.1 = ((f32[8,3,32,512]{3,2,1,0:T(8,128)}), f32[8,3,32,512]{3,2,1,0:T(8,128)S(1)}, u32[]{:S(2)}, u32[]{:S(2)}) async-start(f32[8,3,32,512]{3,2,1,0:T(8,128)} %viscous.1), calls=%async_computation.1 | async-start | bytes 3145728 | tf_op jit(solution)/shard_map/all_to_all | solution.py:418
  108.9 1.4 %copy-start.2 = (f32[3,1,256,512]{3,2,1,0:T(8,128)S(1)}, f32[3,1,256,512]{3,2,1,0:T(8,128)}, u32[]{:S(2)}) copy-start(f32[3,1,256,512]{3,2,1,0:T(8,128)} %param.7) | copy-start | bytes 4718596
  108.9 1.5 %copy-start.3 = (f32[1,256,512]{2,1,0:T(8,128)S(1)}, f32[1,256,512]{2,1,0:T(8,128)}, u32[]{:S(2)}) copy-start(f32[1,256,512]{2,1,0:T(8,128)} %param.8) | copy-start | bytes 1572868

commit v9 on v8

--- a/solution.py
+++ b/solution.py
@@ -135,12 +135,12 @@
         return send(i, fill(i, carry))
 
     rest_ref[brick] = stage[brick, 96:136]
-    lax.fori_loop(0, 2, fill, 0)
+    fill(0, 0)
     pl.semaphore_wait(barrier, devices - 1)
     for j in range(1, 8):
         other(j).start()
-    lax.fori_loop(0, 2, send, 0)
-    lax.fori_loop(2, devices // group - 1, some, 0)
+    send(0, 0)
+    lax.fori_loop(1, devices // group - 1, some, 0)
     to = [(me + 1 + devices - group + j) % devices for j in range(group)]
     picked = pick(to)
     for t, value in zip(to[:-1], picked):
@@ -149,6 +149,16 @@
     for t in to[:-1]:
         parcel(t).start()
 
+    tiles = cell_ref.shape[0] // 8
+    place = lax.broadcasted_iota(I32, (8, 128), 0) * 128 + lax.broadcasted_iota(I32, (8, 128), 1)
+
+    def early(j, carry):
+        rows = pl.ds(pl.multiple_of(8 * j, 8), 8)
+        cell = cell_ref[rows, :]
+        key_ref[rows, :] = (((cell >> 12) - 16) << 27) + ((j * 1024 + place) << 12) + (cell & 4095)
+        return carry
+
+    lax.fori_loop(0, tiles, early, 0, unroll=4)
     rest = pltpu.make_async_remote_copy(
         src_ref=packed.at[pl.ds(0, devices - 1)], dst_ref=arrived_ref.at[pl.ds(0, devices - 1)],
         send_sem=part_send, recv_sem=part_recv, device_id=coords((me + 1) % devices), device_id_type=mesh_id,
@@ -164,9 +174,6 @@
             recv_sem=rest_recv.at[source], device_id=(slab, source), device_id_type=mesh_id,
         ).wait_recv()
 
-    tiles = cell_ref.shape[0] // 8
-    place = lax.broadcasted_iota(I32, (8, 128), 0) * 128 + lax.broadcasted_iota(I32, (8, 128), 1)
-
     def keys(j, sums):
         parts = [arrived_ref[4 * j + i] for i in range(4)]
         rows = pl.ds(pl.multiple_of(8 * j, 8), 8)
@@ -174,12 +181,9 @@
             value = jnp.concatenate([part[2 * c : 2 * c + 2] for part in parts], axis=0)
             ref[rows, :] = value
         live = value != 0.0
-        cell = cell_ref[rows, :]
-        block = cell >> 12
-        slot = j * 1024 + place
-        key = ((block - 16) << 27) + (slot << 12) + (cell & 4095)
+        key = key_ref[rows, :]
         key_ref[rows, :] = jnp.where(live, key, LAST)
-        block = jnp.where(live, block, 32)
+        block = jnp.where(live, (key >> 27) + 16, 32)
         return tuple(s + jnp.where(block < b + 1, 1, 0) for b, s in enumerate(sums))
 
     sums = lax.fori_loop(0, tiles, keys, tuple(jnp.zeros((8, 128), I32) for _ in range(32)))
@@ -295,7 +299,7 @@
     lax.fori_loop(0, 32 // group, blocks, 0)
 
 
-def viscous_kernel(bricks_ref, rest_ref, below_ref, above_ref, sum_ref, net_ref, padded):
+def viscous_kernel(bricks_ref, rest_ref, below_ref, above_ref, sum_ref, net_hbm, net_ref, padded, net_sem):
     for c in range(4):
         own = slice(c * 32, (c + 1) * 32)
         for z in range(8):
@@ -322,9 +326,12 @@
                     total[c] = total[c] + weight * (side[c] - centre[c])
             for c in range(3):
                 net_ref[z, c, x8 : x8 + 8, :] = total[c] - sum_ref[z, c, x8 : x8 + 8, :]
+        pltpu.make_async_copy(net_ref.at[z], net_hbm.at[z], net_sem.at[z]).start()
         return carry
 
     lax.fori_loop(0, 8, plane, 0)
+    for z in range(8):
+        pltpu.make_async_copy(net_ref.at[z], net_hbm.at[z], net_sem.at[z]).wait()
 
 
 def per_device(
@@ -340,7 +347,7 @@
     square = jax.ShapeDtypeStruct((256, 128), F32)
     hbm = pl.BlockSpec(memory_space=pl.ANY)
     staged, others, starts, key, p0, p1, p2, drag = pl.pallas_call(
-        functools.partial(exchange_kernel, cap=cap, group=8),
+        functools.partial(exchange_kernel, cap=cap, group=16),
         out_shape=(
             jax.ShapeDtypeStruct((8, 96, 512), F32),
             jax.ShapeDtypeStruct((8, 40, 512), F32),
@@ -391,7 +398,7 @@
     below = lax.ppermute(top, "slab", [(i, i + 1) for i in range(n_slab - 1)])
     above = lax.ppermute(bottom, "slab", [(i + 1, i) for i in range(n_slab - 1)])
     f0, f1, f2, slot, summed = pl.pallas_call(
-        functools.partial(brick_kernel, width=256, group=8),
+        functools.partial(brick_kernel, width=256, group=16),
         out_shape=(
             square, square, square,
             jax.ShapeDtypeStruct((256, 128), I32),
@@ -399,7 +406,7 @@
         ),
         in_specs=[smem] + [vmem] * 7,
         out_specs=(vmem,) * 5,
-        scratch_shapes=[pltpu.VMEM((8, 192, 256), BF16), pltpu.VMEM((8, 144, 256), F32)],
+        scratch_shapes=[pltpu.VMEM((16, 192, 256), BF16), pltpu.VMEM((16, 144, 256), F32)],
         compiler_params=params,
         cost_estimate=pl.CostEstimate(flops=30_000_000_000, bytes_accessed=6_000_000, transcendentals=0),
         name="brick_forces",
@@ -408,8 +415,12 @@
         viscous_kernel,
         out_shape=jax.ShapeDtypeStruct((8, 3, 32, 512), F32),
         in_specs=[vmem] * 5,
-        out_specs=vmem,
-        scratch_shapes=[pltpu.VMEM((10, 4, 48, 512), F32)],
+        out_specs=hbm,
+        scratch_shapes=[
+            pltpu.VMEM((8, 3, 32, 512), F32),
+            pltpu.VMEM((10, 4, 48, 512), F32),
+            pltpu.SemaphoreType.DMA((8,)),
+        ],
         compiler_params=params,
         name="viscous",
     )(bricks, others, below, above, summed)

time: 113 us -> 112 us (level); the launches traced: 112 us -> 112 us
  Pallas kernels: 43.1 us -> 38 us
  waiting for transfers between devices: 0.01 us -> 2.89 us
  starting transfers between devices: 24.3 us -> 26.8 us
    pallas_call x2, Pallas kernels: 39.6 us -> 34.9 us  [the longest x1 30.3 us: per_device(): pl.pallas_call(functools.partial(exchange_kernel, cap=cap, group=16), out...]
    all_to_all x1, waiting for transfers between devices: 0.01 us -> 2.89 us  [per_device(): lax.all_to_all(net, 'brick', split_axis=0, concat_axis=0, tiled=True)]
    all_to_all x1, starting transfers between devices: 13.1 us -> 15.3 us  [per_device(): lax.all_to_all(net, 'brick', split_axis=0, concat_axis=0, tiled=True)]
  transfers between devices with their start and end apart: 4 -> 4, of which waited for: 0 -> 1; matrix products, arithmetic and copies ran while one was open for 36% -> 36% of each run, Pallas kernels for 7% -> 4%
where the time goes in v9:
time: 112 us
  other arithmetic  42.1 us (38%)
  Pallas kernels  38 us (34%)
  starting transfers between devices  26.8 us (24%)
  waiting for transfers between devices  2.89 us (3%)
  local copies, waits for them, and re-layouts  1.56 us (1%)
    pallas_call x1, Pallas kernels, per_device(): pl.pallas_call(functools.partial(exchange_kernel, cap=cap, group=16), out...  30.3 us
    sort x1, other arithmetic, per_device(): lax.sort([part.reshape(-1) for part in (key, drag, p0, p1, p2)], num_keys...  22.5 us
    sort x1, other arithmetic, per_device(): lax.sort([part.reshape(-1) for part in (slot, f0, f1, f2)], num_keys=1, i...  16.6 us
    all_to_all x1, starting transfers between devices, per_device(): lax.all_to_all(net, 'brick', split_axis=0, concat_axis=0, tiled=True)  15.3 us
    all_to_all x1, starting transfers between devices, per_device(): lax.all_to_all(staged, 'brick', split_axis=0, concat_axis=0, tiled=True)  4.83 us
    ppermute x1, starting transfers between devices, per_device(): lax.ppermute(bottom, 'slab', [(i + 1, i) for i in range(n_slab - 1)])  4.76 us
    pallas_call x1, Pallas kernels, per_device(): pl.pallas_call(functools.partial(brick_kernel, width=256, group=16), out_...  4.57 us
    pallas_call x1, Pallas kernels, per_device(): pl.pallas_call(viscous_kernel, out_shape=jax.ShapeDtypeStruct((8, 3, 32,...  3.1 us
  transfers between devices with their start and end apart: 4, of which 1 were waited for; matrix products, arithmetic and copies ran while one was open for 36% of the time, Pallas kernels for 4%

profile of v9, /device:TPU:8, one launch (start us, length us, event | category | flops | bytes accessed | tf_op | source)
XLA Modules:
  0.0 112.2 jit_solution(17283863481742029773)
XLA Ops:
  0.6 30.3 %exchange.1 = (f32[8,96,512]{2,1,0:T(8,128)}, f32[8,40,512]{2,1,0:T(8,128)}, s32[33]{0:T(128)}, s32[256,128]{1,0:T(8,128)}, f32[256,128]{1,0:T(8,128)}, /*index=...) custom-call(s32[128]{0:T(128)} %counts_ref.1, f32[3,16384]{1,0:T(4,128)} %pv_hbm.1, f32[128,128]{1,0:T(8,128)} %bitcast.62, ...), custom_call_target="tpu_custom_call" | custom-call | tf_op jit(solution)/shard_map/exchange/pallas_call | solution.py:349
  30.9 0.0 copy-start.4
  30.9 0.0 copy-start.5
  30.9 0.0 copy-start.6
  31.0 0.0 copy-start.7
  31.0 0.0 copy-start.8
  31.0 0.0 copy-start
  31.0 4.8 %all-to-all-start = ((f32[8,96,512]{2,1,0:T(8,128)}), f32[8,96,512]{2,1,0:T(8,128)S(1)}, u32[]{:S(2)}, u32[]{:S(2)}) async-start(f32[8,96,512]{2,1,0:T(8,128)} %get-tuple-element.39), calls=%async_computation | async-start | bytes 3145728 | tf_op jit(solution)/shard_map/all_to_all | solution.py:393
  35.8 0.0 copy-done.4
  35.8 0.0 copy-done.5
  35.8 0.0 copy-done.6
  35.9 0.0 copy-done.7
  35.9 22.5 %sort.60 = (s32[32768]{0:T(1024)S(1)}, f32[32768]{0:T(1024)S(1)}, f32[32768]{0:T(1024)S(1)}, f32[32768]{0:T(1024)S(1)}, f32[32768]{0:T(1024)S(1)}) sort(s32[32768]{0:T(1024)S(1)} %bitcast.54, f32[32768]{0:T(1024)S(1)} %bitcast.58, f32[32768]{0:T(1024)S(1)} %bitcast.55, f32[32768]{0:T(1024)S(1)} %bitcast.56, f32[32768]{0:T(1024)S(1)} %bitcast.57), dimensions={0}, to_apply=%region_0.0 | sort | flops 491520 | bytes 1310720 | tf_op jit(solution)/shard_map/sort | solution.py:394
  58.4 0.0 all-to-all-done.bricks_ref
  58.5 1.9 %collective-permute-start = (f32[128,512]{1,0:T(8,128)S(1)}, f32[128,512]{1,0:T(8,128)S(1)}, u32[]{:S(2)}, u32[]{:S(2)}) collective-permute-start(f32[128,512]{1,0:T(8,128)S(1)} %pad_maximum_fusion.1), channel_id=1, source_target_pairs={{0,8},{8,16},{16,24},{24,32},{32,40},{40,48},{48,56},{56,64},{64,7... | collective-permute-start | bytes 786440 | tf_op jit(solution)/shard_map/ppermute | solution.py:398
  60.4 4.8 %collective-permute-start.1 = (f32[128,512]{1,0:T(8,128)S(1)}, f32[128,512]{1,0:T(8,128)S(1)}, u32[]{:S(2)}, u32[]{:S(2)}) collective-permute-start(f32[128,512]{1,0:T(8,128)S(1)} %pad_maximum_fusion.2), channel_id=1, source_target_pairs={{8,0},{16,8},{24,16},{32,24},{40,32},{48,40},{56,48},{64,56},{72,6... | collective-permute-start | bytes 786440 | tf_op jit(solution)/shard_map/ppermute | solution.py:399
  65.2 0.0 copy-done.1
  65.2 4.6 %brick_forces.1 = (f32[256,128]{1,0:T(8,128)S(1)}, f32[256,128]{1,0:T(8,128)S(1)}, f32[256,128]{1,0:T(8,128)S(1)}, s32[256,128]{1,0:T(8,128)S(1)}, f32[8,3,32,512]{3,2,1,0:T(8,128)S(1)}) custom-call(s32[33]{0:T(128)S(1)} %copy-done.1, s32[256,128]{1,0:T(8,128)S(1)} %bitcast.43, f32[256,128]{1,0:T(8,128)S(1)} %bitcast.44, f32[256,128]{1,0:T(8,128)S(1)} %bitcast.45, ...), custom_call_target="tpu_custom_call" | custom-call | flops 30000001024 | bytes 6000000 | tf_op jit(solution)/shard_map/brick_forces/pallas_call | solution.py:400
  69.8 0.0 collective-permute-done.below_ref
  69.8 0.0 collective-permute-done.1.above_ref
  69.8 3.1 %viscous.1 = f32[8,3,32,512]{3,2,1,0:T(8,128)} custom-call(f32[8,96,512]{2,1,0:T(8,128)S(1)} %all-to-all-done.bricks_ref, f32[8,40,512]{2,1,0:T(8,128)S(1)} %copy-done, f32[128,512]{1,0:T(8,128)S(1)} %collective-permute-done.below_ref, f32[128,512]{1,0:T(8,128)S(1)} %collective-permute-done.1.above_ref, f32[8,3,32,512]{3,2,1,0:T(8,128)S(1)} %get-tuple-element.45.sum_ref), custom_call_target="tpu_custom_call" | custom-call | tf_op jit(solution)/shard_map/viscous/pallas_call | solution.py:414
  72.9 15.3 %all-to-all-start.1 = ((f32[8,3,32,512]{3,2,1,0:T(8,128)}), f32[8,3,32,512]{3,2,1,0:T(8,128)S(1)}, u32[]{:S(2)}, u32[]{:S(2)}) async-start(f32[8,3,32,512]{3,2,1,0:T(8,128)} %viscous.1), calls=%async_computation.1 | async-start | bytes 3145728 | tf_op jit(solution)/shard_map/all_to_all | solution.py:429
  88.2 16.6 %sort.61 = (s32[32768]{0:T(1024)}, f32[32768]{0:T(1024)S(1)}, f32[32768]{0:T(1024)S(1)}, f32[32768]{0:T(1024)S(1)}) sort(s32[32768]{0:T(1024)S(1)} %bitcast.42, f32[32768]{0:T(1024)S(1)} %bitcast.39, f32[32768]{0:T(1024)S(1)} %bitcast.40, f32[32768]{0:T(1024)S(1)} %bitcast.41), dimensions={0}, to_apply=%region_1.0 | sort | flops 491520 | bytes 1048576 | tf_op jit(solution)/shard_map/sort | solution.py:430
  104.8 1.1 %pad_maximum_fusion = f32[3,32768]{1,0:T(4,128)} fusion(f32[1,32768]{1,0:T(1,128)S(1)} %bitcast.61, f32[1,32768]{1,0:T(1,128)S(1)} %bitcast.60, f32[1,32768]{1,0:T(1,128)S(1)} %bitcast.59), kind=kLoop, calls=%fused_computation.3 | loop fusion | flops 196608 | bytes 786432 | tf_op jit(solution)/shard_map/stack | solution.py:431
  105.9 2.9 %all-to-all-done.1 = f32[8,3,32,512]{3,2,1,0:T(8,128)S(1)} async-done(((f32[8,3,32,512]{3,2,1,0:T(8,128)}), f32[8,3,32,512]{3,2,1,0:T(8,128)S(1)}, u32[]{:S(2)}, u32[]{:S(2)}) %all-to-all-start.1) | async-done | bytes 1572896 | tf_op jit(solution)/shard_map/all_to_all | solution.py:429
  108.8 0.3 multiply_bitcast_fusion
  109.1 0.0 copy-start.2
  109.1 0.0 copy-start.3
  109.1 0.1 copy.9
  109.2 1.3 %copy-done.2 = f32[3,1,256,512]{3,2,1,0:T(8,128)S(1)} copy-done((f32[3,1,256,512]{3,2,1,0:T(8,128)S(1)}, f32[3,1,256,512]{3,2,1,0:T(8,128)}, u32[]{:S(2)}) %copy-start.2) | copy-done | bytes 1572888
  110.5 0.1 copy-done.3
  110.6 1.6 %fusion = f32[3,1,256,512]{3,2,0,1:T(8,128)} fusion(f32[3,8,32,512]{3,2,1,0:T(8,128)S(1)} %copy.9, f32[3,1,256,512]{3,2,1,0:T(8,128)S(1)} %copy-done.2, f32[256,512]{1,0:T(8,128)S(1)} %bitcast.50), kind=kLoop, calls=%fused_computation.1 | loop fusion | flops 786432 | bytes 5242880 | tf_op jit(solution)/shard_map/add | solution.py:433
  (7 shorter events, 0.1 us)
Async XLA Ops:
  30.9 4.9 %copy-start.4 = (s32[256,128]{1,0:T(8,128)S(1)}, s32[256,128]{1,0:T(8,128)}, u32[]{:S(2)}) copy-start(s32[256,128]{1,0:T(8,128)} %get-tuple-element.29) | copy-start | bytes 393220
  30.9 4.9 %copy-start.5 = (f32[256,128]{1,0:T(8,128)S(1)}, f32[256,128]{1,0:T(8,128)}, u32[]{:S(2)}) copy-start(f32[256,128]{1,0:T(8,128)} %get-tuple-element.31) | copy-start | bytes 393220
  30.9 4.9 %copy-start.6 = (f32[256,128]{1,0:T(8,128)S(1)}, f32[256,128]{1,0:T(8,128)}, u32[]{:S(2)}) copy-start(f32[256,128]{1,0:T(8,128)} %get-tuple-element.32) | copy-start | bytes 393220
  31.0 4.9 %copy-start.7 = (f32[256,128]{1,0:T(8,128)S(1)}, f32[256,128]{1,0:T(8,128)}, u32[]{:S(2)}) copy-start(f32[256,128]{1,0:T(8,128)} %get-tuple-element.33) | copy-start | bytes 393220
  31.0 4.9 %copy-start.8 = (f32[256,128]{1,0:T(8,128)S(1)}, f32[256,128]{1,0:T(8,128)}, u32[]{:S(2)}) copy-start(f32[256,128]{1,0:T(8,128)} %get-tuple-element.30) | copy-start | bytes 393220
  31.0 27.4 %copy-start = (f32[8,40,512]{2,1,0:T(8,128)S(1)}, f32[8,40,512]{2,1,0:T(8,128)}, u32[]{:S(2)}) copy-start(f32[8,40,512]{2,1,0:T(8,128)} %get-tuple-element.40.rest_ref) | copy-start | bytes 1966084
  31.0 27.4 %all-to-all-start = ((f32[8,96,512]{2,1,0:T(8,128)}), f32[8,96,512]{2,1,0:T(8,128)S(1)}, u32[]{:S(2)}, u32[]{:S(2)}) async-start(f32[8,96,512]{2,1,0:T(8,128)} %get-tuple-element.39), calls=%async_computation | async-start | bytes 3145728 | tf_op jit(solution)/shard_map/all_to_all | solution.py:393
  35.8 29.4 %copy-start.1 = (s32[33]{0:T(128)S(1)}, s32[33]{0:T(128)}, u32[]{:S(2)}) copy-start(s32[33]{0:T(128)} %get-tuple-element.28.starts_ref) | copy-start | bytes 400
  58.5 11.3 %collective-permute-start = (f32[128,512]{1,0:T(8,128)S(1)}, f32[128,512]{1,0:T(8,128)S(1)}, u32[]{:S(2)}, u32[]{:S(2)}) collective-permute-start(f32[128,512]{1,0:T(8,128)S(1)} %pad_maximum_fusion.1), channel_id=1, source_target_pairs={{0,8},{8,16},{16,24},{24,32},{32,40},{40,48},{48,56},{56,64},{64,7... | collective-permute-start | bytes 786440 | tf_op jit(solution)/shard_map/ppermute | solution.py:398
  60.4 9.4 %collective-permute-start.1 = (f32[128,512]{1,0:T(8,128)S(1)}, f32[128,512]{1,0:T(8,128)S(1)}, u32[]{:S(2)}, u32[]{:S(2)}) collective-permute-start(f32[128,512]{1,0:T(8,128)S(1)} %pad_maximum_fusion.2), channel_id=1, source_target_pairs={{8,0},{16,8},{24,16},{32,24},{40,32},{48,40},{56,48},{64,56},{72,6... | collective-permute-start | bytes 786440 | tf_op jit(solution)/shard_map/ppermute | solution.py:399
  72.9 35.9 %all-to-all-start.1 = ((f32[8,3,32,512]{3,2,1,0:T(8,128)}), f32[8,3,32,512]{3,2,1,0:T(8,128)S(1)}, u32[]{:S(2)}, u32[]{:S(2)}) async-start(f32[8,3,32,512]{3,2,1,0:T(8,128)} %viscous.1), calls=%async_computation.1 | async-start | bytes 3145728 | tf_op jit(solution)/shard_map/all_to_all | solution.py:429
  109.1 1.4 %copy-start.2 = (f32[3,1,256,512]{3,2,1,0:T(8,128)S(1)}, f32[3,1,256,512]{3,2,1,0:T(8,128)}, u32[]{:S(2)}) copy-start(f32[3,1,256,512]{3,2,1,0:T(8,128)} %param.7) | copy-start | bytes 4718596
  109.1 1.5 %copy-start.3 = (f32[1,256,512]{2,1,0:T(8,128)S(1)}, f32[1,256,512]{2,1,0:T(8,128)}, u32[]{:S(2)}) copy-start(f32[1,256,512]{2,1,0:T(8,128)} %param.8) | copy-start | bytes 1572868

commit v10 on v9

--- a/solution.py
+++ b/solution.py
@@ -28,7 +28,7 @@
     *, cap, group,
 ):
     pairs = (
-        (u_hbm, u_ref), (frac_hbm, frac_ref), (pv_hbm, pv_ref), (coef_hbm, coef_ref), (rows_hbm, rows_ref),
+        (pv_hbm, pv_ref), (coef_hbm, coef_ref), (rows_hbm, rows_ref), (u_hbm, u_ref), (frac_hbm, frac_ref),
         (cell_hbm, cell_ref),
     )
     loads = [pltpu.make_async_copy(source, target, load_sem.at[i]) for i, (source, target) in enumerate(pairs)]
@@ -45,27 +45,18 @@
 
     barrier = pltpu.get_barrier_semaphore()
 
-    def greet(j, carry):
+    def greet(j):
         pl.semaphore_signal(barrier, inc=1, device_id=coords((me + j) % devices), device_id_type=mesh_id)
-        return carry
-
-    lax.fori_loop(1, devices, greet, 0)
-
-    loads[0].wait()
-    loads[1].wait()
-    for c in range(4):
-        for b in range(8):
-            field = frac_ref[b * 32 : (b + 1) * 32, :] if c == 3 else u_ref[c, b * 32 : (b + 1) * 32, :]
-            stage[b, c * 32 : (c + 1) * 32, :] = field
-            if b < 7:
-                stage[b + 1, 128 + c : 129 + c, :] = field[31:32]
-            if b > 0:
-                stage[b - 1, 132 + c : 133 + c, :] = field[0:1]
-        stage[0, 128 + c : 129 + c, :] = jnp.zeros((1, 512), F32)
-        stage[7, 132 + c : 133 + c, :] = jnp.zeros((1, 512), F32)
-    saved = pltpu.make_async_copy(stage.at[:, pl.ds(0, 96)], stage_hbm, stage_sem)
-    saved.start()
-    for load in loads[2:]:
+
+    def greet_some(i, carry):
+        for j in range(6):
+            greet(6 * i + j + 1)
+        return carry
+
+    lax.fori_loop(0, 21, greet_some, 0)
+    greet(127)
+
+    for load in loads[:3]:
         load.wait()
     for l in range(128):
         part = pv_ref[:, l * 128 : (l + 1) * 128]
@@ -134,8 +125,22 @@
     def some(i, carry):
         return send(i, fill(i, carry))
 
+    fill(0, 0)
+    for load in loads[3:]:
+        load.wait()
+    for c in range(4):
+        for b in range(8):
+            field = frac_ref[b * 32 : (b + 1) * 32, :] if c == 3 else u_ref[c, b * 32 : (b + 1) * 32, :]
+            stage[b, c * 32 : (c + 1) * 32, :] = field
+            if b < 7:
+                stage[b + 1, 128 + c : 129 + c, :] = field[31:32]
+            if b > 0:
+                stage[b - 1, 132 + c : 133 + c, :] = field[0:1]
+        stage[0, 128 + c : 129 + c, :] = jnp.zeros((1, 512), F32)
+        stage[7, 132 + c : 133 + c, :] = jnp.zeros((1, 512), F32)
+    saved = pltpu.make_async_copy(stage.at[:, pl.ds(0, 96)], stage_hbm, stage_sem)
+    saved.start()
     rest_ref[brick] = stage[brick, 96:136]
-    fill(0, 0)
     pl.semaphore_wait(barrier, devices - 1)
     for j in range(1, 8):
         other(j).start()
@@ -332,6 +337,21 @@
     lax.fori_loop(0, 8, plane, 0)
     for z in range(8):
         pltpu.make_async_copy(net_ref.at[z], net_hbm.at[z], net_sem.at[z]).wait()
+
+
+def step_kernel(u_ref, frac_ref, net_ref, out_hbm, out_ref, save_sem):
+    def save(k):
+        x = pl.ds(k * 64, 64)
+        return pltpu.make_async_copy(out_ref.at[:, x], out_hbm.at[:, x], save_sem.at[k])
+
+    for k in range(4):
+        for b in range(2 * k, 2 * k + 2):
+            x = slice(b * 32, (b + 1) * 32)
+            for c in range(3):
+                out_ref[c, x, :] = u_ref[c, x, :] + time_step * net_ref[b, c] / frac_ref[x, :]
+        save(k).start()
+    for k in range(4):
+        save(k).wait()
 
 
 def per_device(
@@ -429,8 +449,19 @@
     returned = lax.all_to_all(net, "brick", split_axis=0, concat_axis=0, tiled=True)
     back = lax.sort([part.reshape(-1) for part in (slot, f0, f1, f2)], num_keys=1, is_stable=False)
     slot_force = jnp.stack(back[1:])
-    returned = jnp.swapaxes(returned, 0, 1).reshape(fluid_velocity.shape)
-    new_velocity = fluid_velocity + time_step * returned / porosity
+    new_velocity = pl.pallas_call(
+        step_kernel,
+        out_shape=jax.ShapeDtypeStruct((3, 256, 512), F32),
+        in_specs=[vmem] * 3,
+        out_specs=hbm,
+        scratch_shapes=[
+            pltpu.VMEM((3, 256, 512), F32),
+            pltpu.SemaphoreType.DMA((4,)),
+        ],
+        compiler_params=pltpu.CompilerParams(vmem_limit_bytes=12 << 20),
+        name="velocity_step",
+    )(fluid_velocity.reshape(3, 256, 512), porosity.reshape(256, 512), returned)
+    new_velocity = new_velocity.reshape(fluid_velocity.shape)
     return (new_velocity, slot_force)
 
 

time: 112 us -> 111 us (level); the launches traced: 112 us -> 109 us
  starting transfers between devices: 26.8 us -> 21.7 us
  Pallas kernels: 38 us -> 41.4 us
  waiting for transfers between devices: 2.89 us -> 1.67 us
    all_to_all x1, starting transfers between devices: 15.3 us -> 10 us  [per_device(): lax.all_to_all(net, 'brick', split_axis=0, concat_axis=0, tiled=True)]
    pallas_call x1, Pallas kernels: 4.57 us -> 7.27 us  [per_device(): pl.pallas_call(functools.partial(brick_kernel, width=256, group=16), out_...]
    add x1 -> x0, other arithmetic: 1.57 us -> none  [per_device(): new_velocity = fluid_velocity + time_step * returned / porosity]
    all_to_all x1, waiting for transfers between devices: 2.89 us -> 1.66 us  [per_device(): lax.all_to_all(net, 'brick', split_axis=0, concat_axis=0, tiled=True)]
    pallas_call x0 -> x1, Pallas kernels: none -> 1.22 us  [per_device(): pl.pallas_call(step_kernel, out_shape=jax.ShapeDtypeStruct((3, 256, 512),...]
  transfers between devices with their start and end apart: 4 -> 4, of which waited for: 1 -> 1; matrix products, arithmetic and copies ran while one was open for 36% -> 39% of each run, Pallas kernels for 4% -> 7%
where the time goes in v10:
time: 111 us; the launch traced here: 109 us
  other arithmetic  42.3 us (38%)
  Pallas kernels  41.4 us (37%)
  starting transfers between devices  21.7 us (20%)
  waiting for transfers between devices  1.67 us (2%)
  local copies, waits for them, and re-layouts  1.12 us (1%)
    pallas_call x1, Pallas kernels, per_device(): pl.pallas_call(functools.partial(exchange_kernel, cap=cap, group=16), out...  29.8 us
    sort x1, other arithmetic, per_device(): lax.sort([part.reshape(-1) for part in (key, drag, p0, p1, p2)], num_keys...  22.5 us
    sort x1, other arithmetic, per_device(): lax.sort([part.reshape(-1) for part in (slot, f0, f1, f2)], num_keys=1, i...  17.6 us
    all_to_all x1, starting transfers between devices, per_device(): lax.all_to_all(net, 'brick', split_axis=0, concat_axis=0, tiled=True)  10 us
    pallas_call x1, Pallas kernels, per_device(): pl.pallas_call(functools.partial(brick_kernel, width=256, group=16), out_...  7.27 us
    all_to_all x1, starting transfers between devices, per_device(): lax.all_to_all(staged, 'brick', split_axis=0, concat_axis=0, tiled=True)  5.02 us
    ppermute x1, starting transfers between devices, per_device(): lax.ppermute(bottom, 'slab', [(i + 1, i) for i in range(n_slab - 1)])  4.76 us
    pallas_call x1, Pallas kernels, per_device(): pl.pallas_call(viscous_kernel, out_shape=jax.ShapeDtypeStruct((8, 3, 32,...  3.1 us
  transfers between devices with their start and end apart: 4, of which 1 were waited for; matrix products, arithmetic and copies ran while one was open for 39% of the time, Pallas kernels for 7%

profile of v10, /device:TPU:8, one launch (start us, length us, event | category | flops | bytes accessed | tf_op | source)
XLA Modules:
  0.0 109.3 jit_solution(15991472198028594249)
XLA Ops:
  0.6 29.8 %exchange.1 = (f32[8,96,512]{2,1,0:T(8,128)}, f32[8,40,512]{2,1,0:T(8,128)}, s32[33]{0:T(128)}, s32[256,128]{1,0:T(8,128)}, f32[256,128]{1,0:T(8,128)}, /*index=...) custom-call(s32[128]{0:T(128)} %counts_ref.1, f32[3,16384]{1,0:T(4,128)} %pv_hbm.1, f32[128,128]{1,0:T(8,128)} %bitcast.57, ...), custom_call_target="tpu_custom_call" | custom-call | tf_op jit(solution)/shard_map/exchange/pallas_call | solution.py:369
  30.5 0.0 copy-start.5
  30.5 0.0 copy-start.6
  30.5 0.0 copy-start.7
  30.5 0.0 copy-start.8
  30.5 0.0 copy-start.9
  30.5 0.0 copy-start.2
  30.5 5.0 %all-to-all-start = ((f32[8,96,512]{2,1,0:T(8,128)}), f32[8,96,512]{2,1,0:T(8,128)S(1)}, u32[]{:S(2)}, u32[]{:S(2)}) async-start(f32[8,96,512]{2,1,0:T(8,128)} %get-tuple-element.39), calls=%async_computation | async-start | bytes 3145728 | tf_op jit(solution)/shard_map/all_to_all | solution.py:413
  35.5 0.0 copy-done.5
  35.6 0.0 copy-done.6
  35.6 0.0 copy-done.7
  35.6 0.0 copy-done.8
  35.6 0.0 copy-done.9
  35.6 22.5 %sort.60 = (s32[32768]{0:T(1024)S(1)}, f32[32768]{0:T(1024)S(1)}, f32[32768]{0:T(1024)S(1)}, f32[32768]{0:T(1024)S(1)}, f32[32768]{0:T(1024)S(1)}) sort(s32[32768]{0:T(1024)S(1)} %bitcast.49, f32[32768]{0:T(1024)S(1)} %bitcast.53, f32[32768]{0:T(1024)S(1)} %bitcast.50, f32[32768]{0:T(1024)S(1)} %bitcast.51, f32[32768]{0:T(1024)S(1)} %bitcast.52), dimensions={0}, to_apply=%region_0.0 | sort | flops 491520 | bytes 1310720 | tf_op jit(solution)/shard_map/sort | solution.py:414
  58.1 0.0 copy-done.2
  58.1 0.0 all-to-all-done.bricks_ref
  58.2 1.9 %collective-permute-start = (f32[128,512]{1,0:T(8,128)S(1)}, f32[128,512]{1,0:T(8,128)S(1)}, u32[]{:S(2)}, u32[]{:S(2)}) collective-permute-start(f32[128,512]{1,0:T(8,128)S(1)} %pad_maximum_fusion.1), channel_id=1, source_target_pairs={{0,8},{8,16},{16,24},{24,32},{32,40},{40,48},{48,56},{56,64},{64,7... | collective-permute-start | bytes 786440 | tf_op jit(solution)/shard_map/ppermute | solution.py:418
  60.1 4.8 %collective-permute-start.1 = (f32[128,512]{1,0:T(8,128)S(1)}, f32[128,512]{1,0:T(8,128)S(1)}, u32[]{:S(2)}, u32[]{:S(2)}) collective-permute-start(f32[128,512]{1,0:T(8,128)S(1)} %pad_maximum_fusion.2), channel_id=1, source_target_pairs={{8,0},{16,8},{24,16},{32,24},{40,32},{48,40},{56,48},{64,56},{72,6... | collective-permute-start | bytes 786440 | tf_op jit(solution)/shard_map/ppermute | solution.py:419
  64.9 0.0 copy-done.4
  64.9 7.3 %brick_forces.1 = (f32[256,128]{1,0:T(8,128)S(1)}, f32[256,128]{1,0:T(8,128)S(1)}, f32[256,128]{1,0:T(8,128)S(1)}, s32[256,128]{1,0:T(8,128)S(1)}, f32[8,3,32,512]{3,2,1,0:T(8,128)S(1)}) custom-call(s32[33]{0:T(128)S(1)} %copy-done.4, s32[256,128]{1,0:T(8,128)S(1)} %bitcast.41, f32[256,128]{1,0:T(8,128)S(1)} %bitcast.42, f32[256,128]{1,0:T(8,128)S(1)} %bitcast.43, ...), custom_call_target="tpu_custom_call" | custom-call | flops 30000001024 | bytes 6000000 | tf_op jit(solution)/shard_map/brick_forces/pallas_call | solution.py:420
  72.2 0.0 copy-start.3
  72.2 0.0 collective-permute-done.below_ref
  72.2 0.0 collective-permute-done.1.above_ref
  72.2 3.1 %viscous.1 = f32[8,3,32,512]{3,2,1,0:T(8,128)} custom-call(f32[8,96,512]{2,1,0:T(8,128)S(1)} %all-to-all-done.bricks_ref, f32[8,40,512]{2,1,0:T(8,128)S(1)} %copy-done.2, f32[128,512]{1,0:T(8,128)S(1)} %collective-permute-done.below_ref, f32[128,512]{1,0:T(8,128)S(1)} %collective-permute-done.1.above_ref, f32[8,3,32,512]{3,2,1,0:T(8,128)S(1)} %get-tuple-element.45.sum_ref), custom_call_target="tpu_custom_call" | custom-call | tf_op jit(solution)/shard_map/viscous/pallas_call | solution.py:434
  75.3 0.0 copy-done.3
  75.3 0.0 copy-start
  75.4 10.0 %all-to-all-start.1 = ((f32[8,3,32,512]{3,2,1,0:T(8,128)}), f32[8,3,32,512]{3,2,1,0:T(8,128)S(1)}, u32[]{:S(2)}, u32[]{:S(2)}) async-start(f32[8,3,32,512]{3,2,1,0:T(8,128)} %viscous.1), calls=%async_computation.1 | async-start | bytes 3145728 | tf_op jit(solution)/shard_map/all_to_all | solution.py:449
  85.4 17.6 %sort.61 = (s32[32768]{0:T(1024)}, f32[32768]{0:T(1024)}, f32[32768]{0:T(1024)}, f32[32768]{0:T(1024)}) sort(s32[32768]{0:T(1024)} %bitcast.40, f32[32768]{0:T(1024)S(1)} %bitcast.37, f32[32768]{0:T(1024)S(1)} %bitcast.38, f32[32768]{0:T(1024)S(1)} %bitcast.39), dimensions={0}, to_apply=%region_1.0 | sort | flops 491520 | bytes 1048576 | tf_op jit(solution)/shard_map/sort | solution.py:450
  103.0 2.2 %pad_maximum_fusion = f32[3,32768]{1,0:T(4,128)} fusion(f32[1,32768]{1,0:T(1,128)} %bitcast.56, f32[1,32768]{1,0:T(1,128)} %bitcast.55, f32[1,32768]{1,0:T(1,128)} %bitcast.54), kind=kLoop, calls=%fused_computation | loop fusion | flops 196608 | bytes 786432 | tf_op jit(solution)/shard_map/stack | solution.py:451
  105.2 1.7 %all-to-all-done.1.net_ref = f32[8,3,32,512]{3,2,1,0:T(8,128)S(1)} async-done(((f32[8,3,32,512]{3,2,1,0:T(8,128)}), f32[8,3,32,512]{3,2,1,0:T(8,128)S(1)}, u32[]{:S(2)}, u32[]{:S(2)}) %all-to-all-start.1) | async-done | bytes 1572896 | tf_op jit(solution)/shard_map/all_to_all | solution.py:449
  106.9 1.0 copy-done.1
  107.9 1.2 %velocity_step.1 = f32[3,256,512]{2,1,0:T(8,128)} custom-call(f32[3,256,512]{2,1,0:T(8,128)S(1)} %bitcast.34, f32[256,512]{1,0:T(8,128)S(1)} %bitcast.36, f32[8,3,32,512]{3,2,1,0:T(8,128)S(1)} %all-to-all-done.1.net_ref), custom_call_target="tpu_custom_call" | custom-call | tf_op jit(solution)/shard_map/velocity_step/pallas_call | solution.py:452
  (7 shorter events, 0.1 us)
Async XLA Ops:
  30.5 5.1 %copy-start.5 = (s32[256,128]{1,0:T(8,128)S(1)}, s32[256,128]{1,0:T(8,128)}, u32[]{:S(2)}) copy-start(s32[256,128]{1,0:T(8,128)} %get-tuple-element.29) | copy-start | bytes 393220
  30.5 5.1 %copy-start.6 = (f32[256,128]{1,0:T(8,128)S(1)}, f32[256,128]{1,0:T(8,128)}, u32[]{:S(2)}) copy-start(f32[256,128]{1,0:T(8,128)} %get-tuple-element.31) | copy-start | bytes 393220
  30.5 5.1 %copy-start.7 = (f32[256,128]{1,0:T(8,128)S(1)}, f32[256,128]{1,0:T(8,128)}, u32[]{:S(2)}) copy-start(f32[256,128]{1,0:T(8,128)} %get-tuple-element.32) | copy-start | bytes 393220
  30.5 5.1 %copy-start.8 = (f32[256,128]{1,0:T(8,128)S(1)}, f32[256,128]{1,0:T(8,128)}, u32[]{:S(2)}) copy-start(f32[256,128]{1,0:T(8,128)} %get-tuple-element.33) | copy-start | bytes 393220
  30.5 5.1 %copy-start.9 = (f32[256,128]{1,0:T(8,128)S(1)}, f32[256,128]{1,0:T(8,128)}, u32[]{:S(2)}) copy-start(f32[256,128]{1,0:T(8,128)} %get-tuple-element.30) | copy-start | bytes 393220
  30.5 27.6 %copy-start.2 = (f32[8,40,512]{2,1,0:T(8,128)S(1)}, f32[8,40,512]{2,1,0:T(8,128)}, u32[]{:S(2)}) copy-start(f32[8,40,512]{2,1,0:T(8,128)} %get-tuple-element.40.rest_ref) | copy-start | bytes 1966084
  30.5 27.6 %all-to-all-start = ((f32[8,96,512]{2,1,0:T(8,128)}), f32[8,96,512]{2,1,0:T(8,128)S(1)}, u32[]{:S(2)}, u32[]{:S(2)}) async-start(f32[8,96,512]{2,1,0:T(8,128)} %get-tuple-element.39), calls=%async_computation | async-start | bytes 3145728 | tf_op jit(solution)/shard_map/all_to_all | solution.py:413
  35.5 29.4 %copy-start.4 = (s32[33]{0:T(128)S(1)}, s32[33]{0:T(128)}, u32[]{:S(2)}) copy-start(s32[33]{0:T(128)} %get-tuple-element.28.starts_ref) | copy-start | bytes 400
  58.2 14.0 %collective-permute-start = (f32[128,512]{1,0:T(8,128)S(1)}, f32[128,512]{1,0:T(8,128)S(1)}, u32[]{:S(2)}, u32[]{:S(2)}) collective-permute-start(f32[128,512]{1,0:T(8,128)S(1)} %pad_maximum_fusion.1), channel_id=1, source_target_pairs={{0,8},{8,16},{16,24},{24,32},{32,40},{40,48},{48,56},{56,64},{64,7... | collective-permute-start | bytes 786440 | tf_op jit(solution)/shard_map/ppermute | solution.py:418
  60.1 12.1 %collective-permute-start.1 = (f32[128,512]{1,0:T(8,128)S(1)}, f32[128,512]{1,0:T(8,128)S(1)}, u32[]{:S(2)}, u32[]{:S(2)}) collective-permute-start(f32[128,512]{1,0:T(8,128)S(1)} %pad_maximum_fusion.2), channel_id=1, source_target_pairs={{8,0},{16,8},{24,16},{32,24},{40,32},{48,40},{56,48},{64,56},{72,6... | collective-permute-start | bytes 786440 | tf_op jit(solution)/shard_map/ppermute | solution.py:419
  72.2 3.1 %copy-start.3 = (s32[256,128]{1,0:T(8,128)}, s32[256,128]{1,0:T(8,128)S(1)}, u32[]{:S(2)}) copy-start(s32[256,128]{1,0:T(8,128)S(1)} %get-tuple-element.47) | copy-start | bytes 393220
  75.3 31.5 %copy-start = (f32[3,1,256,512]{3,2,1,0:T(8,128)S(1)}, f32[3,1,256,512]{3,2,1,0:T(8,128)}, u32[]{:S(2)}) copy-start(f32[3,1,256,512]{3,2,1,0:T(8,128)} %param.7) | copy-start | bytes 4718596
  75.4 31.5 %all-to-all-start.1 = ((f32[8,3,32,512]{3,2,1,0:T(8,128)}), f32[8,3,32,512]{3,2,1,0:T(8,128)S(1)}, u32[]{:S(2)}, u32[]{:S(2)}) async-start(f32[8,3,32,512]{3,2,1,0:T(8,128)} %viscous.1), calls=%async_computation.1 | async-start | bytes 3145728 | tf_op jit(solution)/shard_map/all_to_all | solution.py:449
  106.9 1.0 copy-start.1

commit v11 on v10

--- a/solution.py
+++ b/solution.py
@@ -337,21 +337,6 @@
     lax.fori_loop(0, 8, plane, 0)
     for z in range(8):
         pltpu.make_async_copy(net_ref.at[z], net_hbm.at[z], net_sem.at[z]).wait()
-
-
-def step_kernel(u_ref, frac_ref, net_ref, out_hbm, out_ref, save_sem):
-    def save(k):
-        x = pl.ds(k * 64, 64)
-        return pltpu.make_async_copy(out_ref.at[:, x], out_hbm.at[:, x], save_sem.at[k])
-
-    for k in range(4):
-        for b in range(2 * k, 2 * k + 2):
-            x = slice(b * 32, (b + 1) * 32)
-            for c in range(3):
-                out_ref[c, x, :] = u_ref[c, x, :] + time_step * net_ref[b, c] / frac_ref[x, :]
-        save(k).start()
-    for k in range(4):
-        save(k).wait()
 
 
 def per_device(
@@ -418,7 +403,7 @@
     below = lax.ppermute(top, "slab", [(i, i + 1) for i in range(n_slab - 1)])
     above = lax.ppermute(bottom, "slab", [(i + 1, i) for i in range(n_slab - 1)])
     f0, f1, f2, slot, summed = pl.pallas_call(
-        functools.partial(brick_kernel, width=256, group=16),
+        functools.partial(brick_kernel, width=256, group=32),
         out_shape=(
             square, square, square,
             jax.ShapeDtypeStruct((256, 128), I32),
@@ -426,7 +411,7 @@
         ),
         in_specs=[smem] + [vmem] * 7,
         out_specs=(vmem,) * 5,
-        scratch_shapes=[pltpu.VMEM((16, 192, 256), BF16), pltpu.VMEM((16, 144, 256), F32)],
+        scratch_shapes=[pltpu.VMEM((32, 192, 256), BF16), pltpu.VMEM((32, 144, 256), F32)],
         compiler_params=params,
         cost_estimate=pl.CostEstimate(flops=30_000_000_000, bytes_accessed=6_000_000, transcendentals=0),
         name="brick_forces",
@@ -449,19 +434,8 @@
     returned = lax.all_to_all(net, "brick", split_axis=0, concat_axis=0, tiled=True)
     back = lax.sort([part.reshape(-1) for part in (slot, f0, f1, f2)], num_keys=1, is_stable=False)
     slot_force = jnp.stack(back[1:])
-    new_velocity = pl.pallas_call(
-        step_kernel,
-        out_shape=jax.ShapeDtypeStruct((3, 256, 512), F32),
-        in_specs=[vmem] * 3,
-        out_specs=hbm,
-        scratch_shapes=[
-            pltpu.VMEM((3, 256, 512), F32),
-            pltpu.SemaphoreType.DMA((4,)),
-        ],
-        compiler_params=pltpu.CompilerParams(vmem_limit_bytes=12 << 20),
-        name="velocity_step",
-    )(fluid_velocity.reshape(3, 256, 512), porosity.reshape(256, 512), returned)
-    new_velocity = new_velocity.reshape(fluid_velocity.shape)
+    returned = jnp.swapaxes(returned, 0, 1).reshape(fluid_velocity.shape)
+    new_velocity = fluid_velocity + time_step * returned / porosity
     return (new_velocity, slot_force)
 
 

time: 111 us -> 111 us (level)
  the two profiles are of different devices: /device:TPU:8 before, /device:TPU:24 now
where the time goes in v11:
time: 111 us
  Pallas kernels  42.6 us (38%)
  other arithmetic  42.1 us (38%)
  starting transfers between devices  20.4 us (18%)
  waiting for transfers between devices  3.24 us (3%)
  local copies, waits for them, and re-layouts  1.56 us (1%)
    pallas_call x1, Pallas kernels, per_device(): pl.pallas_call(functools.partial(exchange_kernel, cap=cap, group=16), out...  29.8 us
    sort x1, other arithmetic, per_device(): lax.sort([part.reshape(-1) for part in (key, drag, p0, p1, p2)], num_keys...  22.5 us
    sort x1, other arithmetic, per_device(): lax.sort([part.reshape(-1) for part in (slot, f0, f1, f2)], num_keys=1, i...  16.6 us
    all_to_all x1, starting transfers between devices, per_device(): lax.all_to_all(net, 'brick', split_axis=0, concat_axis=0, tiled=True)  9.75 us
    pallas_call x1, Pallas kernels, per_device(): pl.pallas_call(functools.partial(brick_kernel, width=256, group=32), out_...  9.72 us
    ppermute x1, starting transfers between devices, per_device(): lax.ppermute(bottom, 'slab', [(i + 1, i) for i in range(n_slab - 1)])  4.54 us
    all_to_all x1, starting transfers between devices, per_device(): lax.all_to_all(staged, 'brick', split_axis=0, concat_axis=0, tiled=True)  4.21 us
    all_to_all x1, waiting for transfers between devices, per_device(): lax.all_to_all(net, 'brick', split_axis=0, concat_axis=0, tiled=True)  3.23 us
  transfers between devices with their start and end apart: 4, of which 1 were waited for; matrix products, arithmetic and copies ran while one was open for 36% of the time, Pallas kernels for 9%

profile of v11, /device:TPU:24, one launch (start us, length us, event | category | flops | bytes accessed | tf_op | source)
XLA Modules:
  0.0 110.8 jit_solution(11869005445727751277)
XLA Ops:
  0.6 29.8 %exchange.1 = (f32[8,96,512]{2,1,0:T(8,128)}, f32[8,40,512]{2,1,0:T(8,128)}, s32[33]{0:T(128)}, s32[256,128]{1,0:T(8,128)}, f32[256,128]{1,0:T(8,128)}, /*index=...) custom-call(s32[128]{0:T(128)} %counts_ref.1, f32[3,16384]{1,0:T(4,128)} %pv_hbm.1, f32[128,128]{1,0:T(8,128)} %bitcast.62, ...), custom_call_target="tpu_custom_call" | custom-call | tf_op jit(solution)/shard_map/exchange/pallas_call | solution.py:354
  30.5 0.0 copy-start.4
  30.5 0.0 copy-start.5
  30.5 0.0 copy-start.6
  30.5 0.0 copy-start.7
  30.5 0.0 copy-start.8
  30.5 0.0 copy-start
  30.5 4.2 %all-to-all-start = ((f32[8,96,512]{2,1,0:T(8,128)}), f32[8,96,512]{2,1,0:T(8,128)S(1)}, u32[]{:S(2)}, u32[]{:S(2)}) async-start(f32[8,96,512]{2,1,0:T(8,128)} %get-tuple-element.39), calls=%async_computation | async-start | bytes 3145728 | tf_op jit(solution)/shard_map/all_to_all | solution.py:398
  34.7 0.0 copy-done.4
  34.7 0.0 copy-done.5
  34.8 0.0 copy-done.6
  34.8 0.0 copy-done.7
  34.8 22.5 %sort.60 = (s32[32768]{0:T(1024)S(1)}, f32[32768]{0:T(1024)S(1)}, f32[32768]{0:T(1024)S(1)}, f32[32768]{0:T(1024)S(1)}, f32[32768]{0:T(1024)S(1)}) sort(s32[32768]{0:T(1024)S(1)} %bitcast.54, f32[32768]{0:T(1024)S(1)} %bitcast.58, f32[32768]{0:T(1024)S(1)} %bitcast.55, f32[32768]{0:T(1024)S(1)} %bitcast.56, f32[32768]{0:T(1024)S(1)} %bitcast.57), dimensions={0}, to_apply=%region_0.0 | sort | flops 491520 | bytes 1310720 | tf_op jit(solution)/shard_map/sort | solution.py:399
  57.3 0.0 copy-done
  57.3 0.0 all-to-all-done.bricks_ref
  57.4 1.9 %collective-permute-start = (f32[128,512]{1,0:T(8,128)S(1)}, f32[128,512]{1,0:T(8,128)S(1)}, u32[]{:S(2)}, u32[]{:S(2)}) collective-permute-start(f32[128,512]{1,0:T(8,128)S(1)} %pad_maximum_fusion.1), channel_id=1, source_target_pairs={{0,8},{8,16},{16,24},{24,32},{32,40},{40,48},{48,56},{56,64},{64,7... | collective-permute-start | bytes 786440 | tf_op jit(solution)/shard_map/ppermute | solution.py:403
  59.3 4.5 %collective-permute-start.1 = (f32[128,512]{1,0:T(8,128)S(1)}, f32[128,512]{1,0:T(8,128)S(1)}, u32[]{:S(2)}, u32[]{:S(2)}) collective-permute-start(f32[128,512]{1,0:T(8,128)S(1)} %pad_maximum_fusion.2), channel_id=1, source_target_pairs={{8,0},{16,8},{24,16},{32,24},{40,32},{48,40},{56,48},{64,56},{72,6... | collective-permute-start | bytes 786440 | tf_op jit(solution)/shard_map/ppermute | solution.py:404
  63.9 9.7 %brick_forces.1 = (f32[256,128]{1,0:T(8,128)S(1)}, f32[256,128]{1,0:T(8,128)S(1)}, f32[256,128]{1,0:T(8,128)S(1)}, s32[256,128]{1,0:T(8,128)S(1)}, f32[8,3,32,512]{3,2,1,0:T(8,128)S(1)}) custom-call(s32[33]{0:T(128)S(1)} %copy-done.1, s32[256,128]{1,0:T(8,128)S(1)} %bitcast.43, f32[256,128]{1,0:T(8,128)S(1)} %bitcast.44, f32[256,128]{1,0:T(8,128)S(1)} %bitcast.45, ...), custom_call_target="tpu_custom_call" | custom-call | flops 30000001024 | bytes 6000000 | tf_op jit(solution)/shard_map/brick_forces/pallas_call | solution.py:405
  73.6 0.0 collective-permute-done.below_ref
  73.6 0.0 collective-permute-done.1.above_ref
  73.6 3.1 %viscous.1 = f32[8,3,32,512]{3,2,1,0:T(8,128)} custom-call(f32[8,96,512]{2,1,0:T(8,128)S(1)} %all-to-all-done.bricks_ref, f32[8,40,512]{2,1,0:T(8,128)S(1)} %copy-done, f32[128,512]{1,0:T(8,128)S(1)} %collective-permute-done.below_ref, f32[128,512]{1,0:T(8,128)S(1)} %collective-permute-done.1.above_ref, f32[8,3,32,512]{3,2,1,0:T(8,128)S(1)} %get-tuple-element.45.sum_ref), custom_call_target="tpu_custom_call" | custom-call | tf_op jit(solution)/shard_map/viscous/pallas_call | solution.py:419
  76.7 9.8 %all-to-all-start.1 = ((f32[8,3,32,512]{3,2,1,0:T(8,128)}), f32[8,3,32,512]{3,2,1,0:T(8,128)S(1)}, u32[]{:S(2)}, u32[]{:S(2)}) async-start(f32[8,3,32,512]{3,2,1,0:T(8,128)} %viscous.1), calls=%async_computation.1 | async-start | bytes 3145728 | tf_op jit(solution)/shard_map/all_to_all | solution.py:434
  86.5 16.6 %sort.61 = (s32[32768]{0:T(1024)}, f32[32768]{0:T(1024)S(1)}, f32[32768]{0:T(1024)S(1)}, f32[32768]{0:T(1024)S(1)}) sort(s32[32768]{0:T(1024)S(1)} %bitcast.42, f32[32768]{0:T(1024)S(1)} %bitcast.39, f32[32768]{0:T(1024)S(1)} %bitcast.40, f32[32768]{0:T(1024)S(1)} %bitcast.41), dimensions={0}, to_apply=%region_1.0 | sort | flops 491520 | bytes 1048576 | tf_op jit(solution)/shard_map/sort | solution.py:435
  103.1 1.1 %pad_maximum_fusion = f32[3,32768]{1,0:T(4,128)} fusion(f32[1,32768]{1,0:T(1,128)S(1)} %bitcast.61, f32[1,32768]{1,0:T(1,128)S(1)} %bitcast.60, f32[1,32768]{1,0:T(1,128)S(1)} %bitcast.59), kind=kLoop, calls=%fused_computation.3 | loop fusion | flops 196608 | bytes 786432 | tf_op jit(solution)/shard_map/stack | solution.py:436
  104.3 3.2 %all-to-all-done.1 = f32[8,3,32,512]{3,2,1,0:T(8,128)S(1)} async-done(((f32[8,3,32,512]{3,2,1,0:T(8,128)}), f32[8,3,32,512]{3,2,1,0:T(8,128)S(1)}, u32[]{:S(2)}, u32[]{:S(2)}) %all-to-all-start.1) | async-done | bytes 1572896 | tf_op jit(solution)/shard_map/all_to_all | solution.py:434
  107.5 0.3 multiply_bitcast_fusion
  107.8 0.0 copy-start.2
  107.8 0.0 copy-start.3
  107.8 0.1 copy.9
  107.9 1.3 %copy-done.2 = f32[3,1,256,512]{3,2,1,0:T(8,128)S(1)} copy-done((f32[3,1,256,512]{3,2,1,0:T(8,128)S(1)}, f32[3,1,256,512]{3,2,1,0:T(8,128)}, u32[]{:S(2)}) %copy-start.2) | copy-done | bytes 1572888
  109.2 0.1 copy-done.3
  109.3 1.6 %fusion = f32[3,1,256,512]{3,2,0,1:T(8,128)} fusion(f32[3,8,32,512]{3,2,1,0:T(8,128)S(1)} %copy.9, f32[3,1,256,512]{3,2,1,0:T(8,128)S(1)} %copy-done.2, f32[256,512]{1,0:T(8,128)S(1)} %bitcast.50), kind=kLoop, calls=%fused_computation.1 | loop fusion | flops 786432 | bytes 5242880 | tf_op jit(solution)/shard_map/add | solution.py:438
  (7 shorter events, 0.1 us)
Async XLA Ops:
  30.5 4.3 %copy-start.4 = (s32[256,128]{1,0:T(8,128)S(1)}, s32[256,128]{1,0:T(8,128)}, u32[]{:S(2)}) copy-start(s32[256,128]{1,0:T(8,128)} %get-tuple-element.29) | copy-start | bytes 393220
  30.5 4.3 %copy-start.5 = (f32[256,128]{1,0:T(8,128)S(1)}, f32[256,128]{1,0:T(8,128)}, u32[]{:S(2)}) copy-start(f32[256,128]{1,0:T(8,128)} %get-tuple-element.31) | copy-start | bytes 393220
  30.5 4.3 %copy-start.6 = (f32[256,128]{1,0:T(8,128)S(1)}, f32[256,128]{1,0:T(8,128)}, u32[]{:S(2)}) copy-start(f32[256,128]{1,0:T(8,128)} %get-tuple-element.32) | copy-start | bytes 393220
  30.5 4.3 %copy-start.7 = (f32[256,128]{1,0:T(8,128)S(1)}, f32[256,128]{1,0:T(8,128)}, u32[]{:S(2)}) copy-start(f32[256,128]{1,0:T(8,128)} %get-tuple-element.33) | copy-start | bytes 393220
  30.5 4.3 %copy-start.8 = (f32[256,128]{1,0:T(8,128)S(1)}, f32[256,128]{1,0:T(8,128)}, u32[]{:S(2)}) copy-start(f32[256,128]{1,0:T(8,128)} %get-tuple-element.30) | copy-start | bytes 393220
  30.5 26.8 %copy-start = (f32[8,40,512]{2,1,0:T(8,128)S(1)}, f32[8,40,512]{2,1,0:T(8,128)}, u32[]{:S(2)}) copy-start(f32[8,40,512]{2,1,0:T(8,128)} %get-tuple-element.40.rest_ref) | copy-start | bytes 1966084
  30.5 26.8 %all-to-all-start = ((f32[8,96,512]{2,1,0:T(8,128)}), f32[8,96,512]{2,1,0:T(8,128)S(1)}, u32[]{:S(2)}, u32[]{:S(2)}) async-start(f32[8,96,512]{2,1,0:T(8,128)} %get-tuple-element.39), calls=%async_computation | async-start | bytes 3145728 | tf_op jit(solution)/shard_map/all_to_all | solution.py:398
  34.7 29.1 %copy-start.1 = (s32[33]{0:T(128)S(1)}, s32[33]{0:T(128)}, u32[]{:S(2)}) copy-start(s32[33]{0:T(128)} %get-tuple-element.28.starts_ref) | copy-start | bytes 400
  57.4 16.2 %collective-permute-start = (f32[128,512]{1,0:T(8,128)S(1)}, f32[128,512]{1,0:T(8,128)S(1)}, u32[]{:S(2)}, u32[]{:S(2)}) collective-permute-start(f32[128,512]{1,0:T(8,128)S(1)} %pad_maximum_fusion.1), channel_id=1, source_target_pairs={{0,8},{8,16},{16,24},{24,32},{32,40},{40,48},{48,56},{56,64},{64,7... | collective-permute-start | bytes 786440 | tf_op jit(solution)/shard_map/ppermute | solution.py:403
  59.3 14.3 %collective-permute-start.1 = (f32[128,512]{1,0:T(8,128)S(1)}, f32[128,512]{1,0:T(8,128)S(1)}, u32[]{:S(2)}, u32[]{:S(2)}) collective-permute-start(f32[128,512]{1,0:T(8,128)S(1)} %pad_maximum_fusion.2), channel_id=1, source_target_pairs={{8,0},{16,8},{24,16},{32,24},{40,32},{48,40},{56,48},{64,56},{72,6... | collective-permute-start | bytes 786440 | tf_op jit(solution)/shard_map/ppermute | solution.py:404
  76.7 30.8 %all-to-all-start.1 = ((f32[8,3,32,512]{3,2,1,0:T(8,128)}), f32[8,3,32,512]{3,2,1,0:T(8,128)S(1)}, u32[]{:S(2)}, u32[]{:S(2)}) async-start(f32[8,3,32,512]{3,2,1,0:T(8,128)} %viscous.1), calls=%async_computation.1 | async-start | bytes 3145728 | tf_op jit(solution)/shard_map/all_to_all | solution.py:434
  107.8 1.4 %copy-start.2 = (f32[3,1,256,512]{3,2,1,0:T(8,128)S(1)}, f32[3,1,256,512]{3,2,1,0:T(8,128)}, u32[]{:S(2)}) copy-start(f32[3,1,256,512]{3,2,1,0:T(8,128)} %param.7) | copy-start | bytes 4718596
  107.8 1.5 %copy-start.3 = (f32[1,256,512]{2,1,0:T(8,128)S(1)}, f32[1,256,512]{2,1,0:T(8,128)}, u32[]{:S(2)}) copy-start(f32[1,256,512]{2,1,0:T(8,128)} %param.8) | copy-start | bytes 1572868

commit v12 on v11

--- a/solution.py
+++ b/solution.py
@@ -352,7 +352,7 @@
     square = jax.ShapeDtypeStruct((256, 128), F32)
     hbm = pl.BlockSpec(memory_space=pl.ANY)
     staged, others, starts, key, p0, p1, p2, drag = pl.pallas_call(
-        functools.partial(exchange_kernel, cap=cap, group=16),
+        functools.partial(exchange_kernel, cap=cap, group=32),
         out_shape=(
             jax.ShapeDtypeStruct((8, 96, 512), F32),
             jax.ShapeDtypeStruct((8, 40, 512), F32),

time: 111 us -> 110 us (level)
  the two profiles are of different devices: /device:TPU:24 before, /device:TPU:8 now
where the time goes in v12:
time: 110 us; the launch traced here: 108 us
  other arithmetic  42.1 us (38%)
  Pallas kernels  39.8 us (36%)
  starting transfers between devices  21 us (19%)
  waiting for transfers between devices  2.52 us (2%)
  local copies, waits for them, and re-layouts  1.56 us (1%)
    pallas_call x1, Pallas kernels, per_device(): pl.pallas_call(functools.partial(exchange_kernel, cap=cap, group=32), out...  29.5 us
    sort x1, other arithmetic, per_device(): lax.sort([part.reshape(-1) for part in (key, drag, p0, p1, p2)], num_keys...  22.5 us
    sort x1, other arithmetic, per_device(): lax.sort([part.reshape(-1) for part in (slot, f0, f1, f2)], num_keys=1, i...  16.6 us
    all_to_all x1, starting transfers between devices, per_device(): lax.all_to_all(net, 'brick', split_axis=0, concat_axis=0, tiled=True)  9.85 us
    pallas_call x1, Pallas kernels, per_device(): pl.pallas_call(functools.partial(brick_kernel, width=256, group=32), out_...  7.2 us
    all_to_all x1, starting transfers between devices, per_device(): lax.all_to_all(staged, 'brick', split_axis=0, concat_axis=0, tiled=True)  4.68 us
    ppermute x1, starting transfers between devices, per_device(): lax.ppermute(bottom, 'slab', [(i + 1, i) for i in range(n_slab - 1)])  4.54 us
    pallas_call x1, Pallas kernels, per_device(): pl.pallas_call(viscous_kernel, out_shape=jax.ShapeDtypeStruct((8, 3, 32,...  3.1 us
  transfers between devices with their start and end apart: 4, of which 1 were waited for; matrix products, arithmetic and copies ran while one was open for 37% of the time, Pallas kernels for 7%

profile of v12, /device:TPU:8, one launch (start us, length us, event | category | flops | bytes accessed | tf_op | source)
XLA Modules:
  0.0 107.8 jit_solution(10688576357179845891)
XLA Ops:
  0.6 29.5 %exchange.1 = (f32[8,96,512]{2,1,0:T(8,128)}, f32[8,40,512]{2,1,0:T(8,128)}, s32[33]{0:T(128)}, s32[256,128]{1,0:T(8,128)}, f32[256,128]{1,0:T(8,128)}, /*index=...) custom-call(s32[128]{0:T(128)} %counts_ref.1, f32[3,16384]{1,0:T(4,128)} %pv_hbm.1, f32[128,128]{1,0:T(8,128)} %bitcast.62, ...), custom_call_target="tpu_custom_call" | custom-call | tf_op jit(solution)/shard_map/exchange/pallas_call | solution.py:354
  30.1 0.0 copy-start.4
  30.1 0.0 copy-start.5
  30.1 0.0 copy-start.6
  30.1 0.0 copy-start.7
  30.2 0.0 copy-start.8
  30.2 0.0 copy-start
  30.2 4.7 %all-to-all-start = ((f32[8,96,512]{2,1,0:T(8,128)}), f32[8,96,512]{2,1,0:T(8,128)S(1)}, u32[]{:S(2)}, u32[]{:S(2)}) async-start(f32[8,96,512]{2,1,0:T(8,128)} %get-tuple-element.39), calls=%async_computation | async-start | bytes 3145728 | tf_op jit(solution)/shard_map/all_to_all | solution.py:398
  34.9 0.0 copy-done.4
  34.9 0.0 copy-done.5
  34.9 0.0 copy-done.6
  34.9 0.0 copy-done.7
  34.9 0.0 copy-done.8
  34.9 22.5 %sort.60 = (s32[32768]{0:T(1024)S(1)}, f32[32768]{0:T(1024)S(1)}, f32[32768]{0:T(1024)S(1)}, f32[32768]{0:T(1024)S(1)}, f32[32768]{0:T(1024)S(1)}) sort(s32[32768]{0:T(1024)S(1)} %bitcast.54, f32[32768]{0:T(1024)S(1)} %bitcast.58, f32[32768]{0:T(1024)S(1)} %bitcast.55, f32[32768]{0:T(1024)S(1)} %bitcast.56, f32[32768]{0:T(1024)S(1)} %bitcast.57), dimensions={0}, to_apply=%region_0.0 | sort | flops 491520 | bytes 1310720 | tf_op jit(solution)/shard_map/sort | solution.py:399
  57.4 0.0 all-to-all-done.bricks_ref
  57.5 1.9 %collective-permute-start = (f32[128,512]{1,0:T(8,128)S(1)}, f32[128,512]{1,0:T(8,128)S(1)}, u32[]{:S(2)}, u32[]{:S(2)}) collective-permute-start(f32[128,512]{1,0:T(8,128)S(1)} %pad_maximum_fusion.1), channel_id=1, source_target_pairs={{0,8},{8,16},{16,24},{24,32},{32,40},{40,48},{48,56},{56,64},{64,7... | collective-permute-start | bytes 786440 | tf_op jit(solution)/shard_map/ppermute | solution.py:403
  59.5 4.5 %collective-permute-start.1 = (f32[128,512]{1,0:T(8,128)S(1)}, f32[128,512]{1,0:T(8,128)S(1)}, u32[]{:S(2)}, u32[]{:S(2)}) collective-permute-start(f32[128,512]{1,0:T(8,128)S(1)} %pad_maximum_fusion.2), channel_id=1, source_target_pairs={{8,0},{16,8},{24,16},{32,24},{40,32},{48,40},{56,48},{64,56},{72,6... | collective-permute-start | bytes 786440 | tf_op jit(solution)/shard_map/ppermute | solution.py:404
  64.0 7.2 %brick_forces.1 = (f32[256,128]{1,0:T(8,128)S(1)}, f32[256,128]{1,0:T(8,128)S(1)}, f32[256,128]{1,0:T(8,128)S(1)}, s32[256,128]{1,0:T(8,128)S(1)}, f32[8,3,32,512]{3,2,1,0:T(8,128)S(1)}) custom-call(s32[33]{0:T(128)S(1)} %copy-done.1, s32[256,128]{1,0:T(8,128)S(1)} %bitcast.43, f32[256,128]{1,0:T(8,128)S(1)} %bitcast.44, f32[256,128]{1,0:T(8,128)S(1)} %bitcast.45, ...), custom_call_target="tpu_custom_call" | custom-call | flops 30000001024 | bytes 6000000 | tf_op jit(solution)/shard_map/brick_forces/pallas_call | solution.py:405
  71.2 0.0 collective-permute-done.below_ref
  71.2 0.0 collective-permute-done.1.above_ref
  71.2 3.1 %viscous.1 = f32[8,3,32,512]{3,2,1,0:T(8,128)} custom-call(f32[8,96,512]{2,1,0:T(8,128)S(1)} %all-to-all-done.bricks_ref, f32[8,40,512]{2,1,0:T(8,128)S(1)} %copy-done, f32[128,512]{1,0:T(8,128)S(1)} %collective-permute-done.below_ref, f32[128,512]{1,0:T(8,128)S(1)} %collective-permute-done.1.above_ref, f32[8,3,32,512]{3,2,1,0:T(8,128)S(1)} %get-tuple-element.45.sum_ref), custom_call_target="tpu_custom_call" | custom-call | tf_op jit(solution)/shard_map/viscous/pallas_call | solution.py:419
  74.3 9.8 %all-to-all-start.1 = ((f32[8,3,32,512]{3,2,1,0:T(8,128)}), f32[8,3,32,512]{3,2,1,0:T(8,128)S(1)}, u32[]{:S(2)}, u32[]{:S(2)}) async-start(f32[8,3,32,512]{3,2,1,0:T(8,128)} %viscous.1), calls=%async_computation.1 | async-start | bytes 3145728 | tf_op jit(solution)/shard_map/all_to_all | solution.py:434
  84.2 16.6 %sort.61 = (s32[32768]{0:T(1024)}, f32[32768]{0:T(1024)S(1)}, f32[32768]{0:T(1024)S(1)}, f32[32768]{0:T(1024)S(1)}) sort(s32[32768]{0:T(1024)S(1)} %bitcast.42, f32[32768]{0:T(1024)S(1)} %bitcast.39, f32[32768]{0:T(1024)S(1)} %bitcast.40, f32[32768]{0:T(1024)S(1)} %bitcast.41), dimensions={0}, to_apply=%region_1.0 | sort | flops 491520 | bytes 1048576 | tf_op jit(solution)/shard_map/sort | solution.py:435
  100.8 1.1 %pad_maximum_fusion = f32[3,32768]{1,0:T(4,128)} fusion(f32[1,32768]{1,0:T(1,128)S(1)} %bitcast.61, f32[1,32768]{1,0:T(1,128)S(1)} %bitcast.60, f32[1,32768]{1,0:T(1,128)S(1)} %bitcast.59), kind=kLoop, calls=%fused_computation.3 | loop fusion | flops 196608 | bytes 786432 | tf_op jit(solution)/shard_map/stack | solution.py:436
  102.0 2.5 %all-to-all-done.1 = f32[8,3,32,512]{3,2,1,0:T(8,128)S(1)} async-done(((f32[8,3,32,512]{3,2,1,0:T(8,128)}), f32[8,3,32,512]{3,2,1,0:T(8,128)S(1)}, u32[]{:S(2)}, u32[]{:S(2)}) %all-to-all-start.1) | async-done | bytes 1572896 | tf_op jit(solution)/shard_map/all_to_all | solution.py:434
  104.5 0.3 multiply_bitcast_fusion
  104.7 0.0 copy-start.2
  104.8 0.0 copy-start.3
  104.8 0.1 copy.9
  104.9 1.3 %copy-done.2 = f32[3,1,256,512]{3,2,1,0:T(8,128)S(1)} copy-done((f32[3,1,256,512]{3,2,1,0:T(8,128)S(1)}, f32[3,1,256,512]{3,2,1,0:T(8,128)}, u32[]{:S(2)}) %copy-start.2) | copy-done | bytes 1572888
  106.2 0.1 copy-done.3
  106.3 1.6 %fusion = f32[3,1,256,512]{3,2,0,1:T(8,128)} fusion(f32[3,8,32,512]{3,2,1,0:T(8,128)S(1)} %copy.9, f32[3,1,256,512]{3,2,1,0:T(8,128)S(1)} %copy-done.2, f32[256,512]{1,0:T(8,128)S(1)} %bitcast.50), kind=kLoop, calls=%fused_computation.1 | loop fusion | flops 786432 | bytes 5242880 | tf_op jit(solution)/shard_map/add | solution.py:438
  (7 shorter events, 0.1 us)
Async XLA Ops:
  30.1 4.7 %copy-start.4 = (s32[256,128]{1,0:T(8,128)S(1)}, s32[256,128]{1,0:T(8,128)}, u32[]{:S(2)}) copy-start(s32[256,128]{1,0:T(8,128)} %get-tuple-element.29) | copy-start | bytes 393220
  30.1 4.7 %copy-start.5 = (f32[256,128]{1,0:T(8,128)S(1)}, f32[256,128]{1,0:T(8,128)}, u32[]{:S(2)}) copy-start(f32[256,128]{1,0:T(8,128)} %get-tuple-element.31) | copy-start | bytes 393220
  30.1 4.7 %copy-start.6 = (f32[256,128]{1,0:T(8,128)S(1)}, f32[256,128]{1,0:T(8,128)}, u32[]{:S(2)}) copy-start(f32[256,128]{1,0:T(8,128)} %get-tuple-element.32) | copy-start | bytes 393220
  30.1 4.7 %copy-start.7 = (f32[256,128]{1,0:T(8,128)S(1)}, f32[256,128]{1,0:T(8,128)}, u32[]{:S(2)}) copy-start(f32[256,128]{1,0:T(8,128)} %get-tuple-element.33) | copy-start | bytes 393220
  30.2 4.7 %copy-start.8 = (f32[256,128]{1,0:T(8,128)S(1)}, f32[256,128]{1,0:T(8,128)}, u32[]{:S(2)}) copy-start(f32[256,128]{1,0:T(8,128)} %get-tuple-element.30) | copy-start | bytes 393220
  30.2 27.2 %copy-start = (f32[8,40,512]{2,1,0:T(8,128)S(1)}, f32[8,40,512]{2,1,0:T(8,128)}, u32[]{:S(2)}) copy-start(f32[8,40,512]{2,1,0:T(8,128)} %get-tuple-element.40.rest_ref) | copy-start | bytes 1966084
  30.2 27.3 %all-to-all-start = ((f32[8,96,512]{2,1,0:T(8,128)}), f32[8,96,512]{2,1,0:T(8,128)S(1)}, u32[]{:S(2)}, u32[]{:S(2)}) async-start(f32[8,96,512]{2,1,0:T(8,128)} %get-tuple-element.39), calls=%async_computation | async-start | bytes 3145728 | tf_op jit(solution)/shard_map/all_to_all | solution.py:398
  34.9 29.1 %copy-start.1 = (s32[33]{0:T(128)S(1)}, s32[33]{0:T(128)}, u32[]{:S(2)}) copy-start(s32[33]{0:T(128)} %get-tuple-element.28.starts_ref) | copy-start | bytes 400
  57.5 13.7 %collective-permute-start = (f32[128,512]{1,0:T(8,128)S(1)}, f32[128,512]{1,0:T(8,128)S(1)}, u32[]{:S(2)}, u32[]{:S(2)}) collective-permute-start(f32[128,512]{1,0:T(8,128)S(1)} %pad_maximum_fusion.1), channel_id=1, source_target_pairs={{0,8},{8,16},{16,24},{24,32},{32,40},{40,48},{48,56},{56,64},{64,7... | collective-permute-start | bytes 786440 | tf_op jit(solution)/shard_map/ppermute | solution.py:403
  59.5 11.8 %collective-permute-start.1 = (f32[128,512]{1,0:T(8,128)S(1)}, f32[128,512]{1,0:T(8,128)S(1)}, u32[]{:S(2)}, u32[]{:S(2)}) collective-permute-start(f32[128,512]{1,0:T(8,128)S(1)} %pad_maximum_fusion.2), channel_id=1, source_target_pairs={{8,0},{16,8},{24,16},{32,24},{40,32},{48,40},{56,48},{64,56},{72,6... | collective-permute-start | bytes 786440 | tf_op jit(solution)/shard_map/ppermute | solution.py:404
  74.3 30.1 %all-to-all-start.1 = ((f32[8,3,32,512]{3,2,1,0:T(8,128)}), f32[8,3,32,512]{3,2,1,0:T(8,128)S(1)}, u32[]{:S(2)}, u32[]{:S(2)}) async-start(f32[8,3,32,512]{3,2,1,0:T(8,128)} %viscous.1), calls=%async_computation.1 | async-start | bytes 3145728 | tf_op jit(solution)/shard_map/all_to_all | solution.py:434
  104.7 1.4 %copy-start.2 = (f32[3,1,256,512]{3,2,1,0:T(8,128)S(1)}, f32[3,1,256,512]{3,2,1,0:T(8,128)}, u32[]{:S(2)}) copy-start(f32[3,1,256,512]{3,2,1,0:T(8,128)} %param.7) | copy-start | bytes 4718596
  104.8 1.5 %copy-start.3 = (f32[1,256,512]{2,1,0:T(8,128)S(1)}, f32[1,256,512]{2,1,0:T(8,128)}, u32[]{:S(2)}) copy-start(f32[1,256,512]{2,1,0:T(8,128)} %param.8) | copy-start | bytes 1572868
